TPU v7x, 32 devices: a whole 2x2x4 slice. The times are simulated.
32 devices in a mesh: row: 8 (over y, x, core), col: 4 (over z).
Axes of the slice: x: 2, y: 2, z: 4, core: 2. Of those that a mesh axis runs over, the one named last changes fastest.
Arguments:
- orbitals: bfloat16 [32768, 512], P(('row', 'col')), may hold values from -6 to 6
- coulomb: bfloat16 [8192, 8192], P('row', 'col'), may hold values from -0.0029296875 to 0.0029296875
- interp: bfloat16 [32768, 1024], P(('row', 'col')), may hold values from -0.1875 to 0.1875
- box_counts: int32 [32], replicated, may hold values from 1 to 768, 8192 in all
- owner_map: int32 [8192], replicated, may hold values from 0 to 8191, as said below
- grid_rows: int32 [32, 1024], P(('row', 'col')), may hold values from 0 to 1023, each once within a row
- listed: int32 [32, 1024], P(('row', 'col')), may hold values from 0 to 255
Outputs:
- exchange_action: float32 [32768, 512], P(('row', 'col'))
Inputs may be any that keep to these rules, and one draw needn't show every extreme that they name: `box_counts`: the counts sum to 8192; the largest is exactly 768. `owner_map`: A permutation of the 8192 positions; a point's owner is position // 256. No box holds more than 24 points of one owner, and the box with 768 points holds exactly 24 of some owner. `grid_rows`: each row is a permutation.
All inputs are finite; a program needn't handle non-finite values.
Results may differ from a plain program's by a relative error of at most 0.012.
Values may be sent and summed in bfloat16 or wider, within the bound.
No kernel may reach another device: no remote copies, remote signals or barrier semaphores. Data moves between devices by JAX's collectives and lax.ppermute only.
A program may use at most 128 MiB of HBM per device.

v0:
```python
import jax
import jax.numpy as jnp
from jax import lax
from jax.sharding import PartitionSpec as P

NORB = 512
LIST = 1024
OWN = 256
SLOTS = 768


def add_block(shard_rows, left_rows, kernel_tile):
    pair_tile = jnp.einsum(
        "ak,bk->ab", left_rows, shard_rows, preferred_element_type=jnp.float32
    ).astype(jnp.bfloat16)
    weighted = (pair_tile.astype(jnp.float32) * kernel_tile.astype(jnp.float32)).astype(
        jnp.bfloat16
    )
    return jnp.dot(weighted, shard_rows, preferred_element_type=jnp.float32)


def shards(orbitals, coulomb, interp, box_counts, owner_map, grid_rows, listed):
    row_count = lax.axis_size("row")
    col_count = lax.axis_size("col")
    box_total = row_count * col_count
    point_total = OWN * box_total
    capacity = (SLOTS + box_total - 1) // box_total
    per_owner = LIST // box_total
    my_box = lax.axis_index("row") * col_count + lax.axis_index("col")
    box_ids = jnp.arange(box_total, dtype=jnp.int32)
    first_point = jnp.sum(jnp.where(box_ids < my_box, box_counts, 0))
    my_count = jnp.sum(jnp.where(box_ids == my_box, box_counts, 0))
    slot_ids = jnp.arange(SLOTS, dtype=jnp.int32)
    is_live = slot_ids < my_count
    listing = jnp.minimum(first_point + slot_ids, point_total - 1)
    owner_ids = owner_map[listing] // OWN
    matches = (
        (owner_ids[:, None] == owner_ids[None, :])
        & is_live[None, :]
        & (slot_ids[None, :] < slot_ids[:, None])
    )
    pair_rank = jnp.sum(matches.astype(jnp.int32), axis=1)
    target = jnp.where(is_live, owner_ids * capacity + pair_rank, box_total * capacity)
    dest_slots = jnp.arange(box_total * capacity, dtype=jnp.int32)
    hits = target[None, :] == dest_slots[:, None]
    source_slot = jnp.sum(jnp.where(hits, slot_ids[None, :], 0), axis=1)
    filled = jnp.any(hits, axis=1)
    picked = orbitals[grid_rows[0, source_slot]]
    outgoing = jnp.where(filled[:, None], picked, jnp.zeros_like(picked))
    received = lax.all_to_all(
        outgoing.reshape(box_total, capacity, NORB),
        ("row", "col"),
        split_axis=0,
        concat_axis=0,
        tiled=True,
    )
    received = received.reshape(box_total * capacity, NORB)
    wanted_pos = my_box * OWN + jnp.arange(OWN, dtype=jnp.int32)
    all_listing = jnp.arange(point_total, dtype=jnp.int32)
    my_points = jnp.sum(
        jnp.where(owner_map[None, :] == wanted_pos[:, None], all_listing[None, :], 0), axis=1
    )
    box_ends = jnp.cumsum(box_counts)
    source = jnp.sum((my_points[:, None] >= box_ends[None, :]).astype(jnp.int32), axis=1)
    earlier = (source[:, None] == source[None, :]) & (my_points[None, :] < my_points[:, None])
    source_rank = jnp.sum(earlier.astype(jnp.int32), axis=1)
    owned_rows = received[source * capacity + source_rank]
    left_rows = lax.all_gather(owned_rows, "col", axis=0, tiled=True)
    partial_sums = add_block(
        lax.all_gather(owned_rows, "row", axis=0, tiled=True), left_rows, coulomb
    )
    owned_result = lax.psum_scatter(partial_sums, "col", scatter_dimension=0, tiled=True).astype(
        jnp.bfloat16
    )
    wanted = listed[0].reshape(box_total, per_owner)
    fetched = lax.all_to_all(
        owned_result[
            lax.all_to_all(wanted, ("row", "col"), split_axis=0, concat_axis=0, tiled=True)
        ],
        ("row", "col"),
        split_axis=0,
        concat_axis=0,
        tiled=True,
    )
    chosen_rows = fetched.reshape(LIST, NORB)
    return -jnp.dot(interp, chosen_rows, preferred_element_type=jnp.float32)


def solution(mesh):
    return jax.shard_map(
        shards,
        mesh=mesh,
        in_specs=(
            P(("row", "col"), None),
            P("row", "col"),
            P(("row", "col"), None),
            P(),
            P(),
            P(("row", "col"), None),
            P(("row", "col"), None),
        ),
        out_specs=P(("row", "col"), None),
        check_vma=False,
    )
```

profile of v0, /device:TPU:1, one launch (start us, length us, event | category | flops | bytes accessed | tf_op | source)
XLA Modules:
  0.0 213.1 jit_solution(4739931188837756951)
XLA Ops:
  6.5 1.5 fusion.13
  8.1 0.7 fusion.8
  8.8 4.5 %gather_fusion = s32[768]{0:T(1024)S(1)} fusion(s32[8192]{0:T(1024)} %param.11, s32[1024]{0:T(1024)S(1)} %pad_clamp_fusion.2), kind=kCustom, calls=%fused_computation | custom fusion | bytes 9216 | tf_op jit(solution)/shard_map/gather | solution.py:36
  13.3 0.7 iota_compare_fusion.2
  14.5 0.7 add_select_fusion.1
  15.9 4.7 %gather_fusion.1 = s32[768]{0:T(1024)S(1)} fusion(s32[1,1024]{1,0:T(1,128)S(1)} %copy-done.1, s32[768]{0:T(1024)S(1)} %fusion.12), kind=kCustom, calls=%fused_computation.1 | custom fusion | bytes 12288 | tf_op jit(solution)/shard_map/gather | solution.py:48
  20.7 3.3 %gather_fusion.2 = bf16[768,512]{1,0:T(8,128)(2,1)} fusion(bf16[1024,512]{1,0:T(8,128)(2,1)S(1)} %copy-done.3, s32[1024]{0:T(1024)S(1)} %pad_clamp_fusion.1), kind=kCustom, calls=%fused_computation.2 | custom fusion | bytes 1575936 | tf_op jit(solution)/shard_map/gather | solution.py:48
  24.0 2.2 %broadcast_select_fusion = bf16[32,24,512]{2,1,0:T(8,128)(2,1)} fusion(bf16[32,24,512]{2,1,0:T(8,128)(2,1)} %bitcast.19, pred[32,24]{1,0:T(8,128)(4,1)S(1)} %broadcast_in_dim.45), kind=kLoop, calls=%fused_computation.17 | loop fusion | flops 393216 | bytes 1573632 | tf_op jit(solution)/shard_map/jit(_where)/select_n | solution.py:49
  26.2 7.1 %all-to-all-start = ((bf16[32,24,512]{2,1,0:T(8,128)(2,1)}), bf16[32,24,512]{2,1,0:T(8,128)(2,1)S(1)}, u32[]{:S(2)}, u32[]{:S(2)}) async-start(bf16[32,24,512]{2,1,0:T(8,128)(2,1)} %broadcast_select_fusion), calls=%async_computation | async-start | bytes 1572864 | tf_op jit(solution)/shard_map/all_to_all | solution.py:50
  33.7 1.2 select_reduce_fusion
  35.2 18.9 %all-to-all-done = bf16[32,24,512]{2,1,0:T(8,128)(2,1)S(1)} async-done(((bf16[32,24,512]{2,1,0:T(8,128)(2,1)}), bf16[32,24,512]{2,1,0:T(8,128)(2,1)S(1)}, u32[]{:S(2)}, u32[]{:S(2)}) %all-to-all-start) | async-done | bytes 786464 | tf_op jit(solution)/shard_map/all_to_all | solution.py:50
  54.2 1.9 gather_fusion.3
  56.1 0.7 all-gather.7.cloned.1.call-update
  56.8 25.3 %all-gather.5.cloned.1.call-done = bf16[1024,512]{1,0:T(8,128)(2,1)} async-done(((bf16[256,512]{1,0:T(8,128)(2,1)}), bf16[1024,512]{1,0:T(8,128)(2,1)}) %all-gather.5.cloned.1.call-update) | async-done | bytes 1048592 | tf_op jit(solution)/shard_map/all_gather | solution.py:68
  82.1 29.9 %all-gather.7.cloned.1.call-done = bf16[2048,512]{1,0:T(8,128)(2,1)} async-done(((bf16[256,512]{1,0:T(8,128)(2,1)}), bf16[2048,512]{1,0:T(8,128)(2,1)}) %all-gather.7.cloned.1.call-update) | async-done | bytes 2097168 | tf_op jit(solution)/shard_map/all_gather | solution.py:70
  112.0 9.7 %fusion = f32[1024,512]{1,0:T(8,128)} fusion(bf16[2048,512]{1,0:T(8,128)(2,1)} %all-gather.7.cloned.1.call-done, bf16[1024,2048]{1,0:T(8,128)(2,1)} %param.8, bf16[1024,512]{1,0:T(8,128)(2,1)} %all-gather.5.cloned.1.call-done), kind=kOutput, calls=%fused_computation.7 | convolution fusion | flops 4305453056 | bytes 9437184 | tf_op jit(solution)/shard_map/dot_general | solution.py:19
  122.3 0.7 reduce.10
  123.1 11.5 %all_to_all.22 = s32[32,1,32]{2,1,0:T(1,128)S(1)} all-to-all(s32[32,1,32]{2,1,0:T(1,128)S(1)} %all_to_all.15), channel_id=1, replica_groups=mesh['row'=8,'col'=4] {'row','col'}, dimensions={0} | all-to-all | bytes 8192 | tf_op jit(solution)/shard_map/all_to_all | solution.py:78
  134.7 30.6 %reduce-scatter.2.cloned.1.call-done = f32[256,512]{1,0:T(8,128)} async-done(((f32[1024,512]{1,0:T(8,128)}), f32[256,512]{1,0:T(8,128)}) %reduce-scatter.2.cloned.1.call-update) | async-done | bytes 524304 | tf_op jit(solution)/shard_map/reduce_scatter | solution.py:72
  165.3 1.1 convert_element_type.31
  166.4 4.0 %gather_fusion.4 = bf16[1024,512]{1,0:T(8,128)(2,1)S(1)} fusion(bf16[256,512]{1,0:T(8,128)(2,1)S(1)} %convert_element_type.31, s32[1024]{0:T(1024)S(1)} %broadcast_clamp_fusion), kind=kCustom, calls=%fused_computation.4 | custom fusion | bytes 2101248 | tf_op jit(solution)/shard_map/gather | solution.py:77
  170.4 30.7 %all_to_all.23 = bf16[32,32,512]{2,1,0:T(8,128)(2,1)S(1)} all-to-all(bf16[32,32,512]{2,1,0:T(8,128)(2,1)S(1)} %bitcast.18), channel_id=1, replica_groups=mesh['row'=8,'col'=4] {'row','col'}, dimensions={0} | all-to-all | bytes 2097152 | tf_op jit(solution)/shard_map/all_to_all | solution.py:76
  201.1 2.7 %negate_bitcast_fusion = f32[1024,512]{0,1:T(8,128)} fusion(bf16[1024,512]{1,0:T(8,128)(2,1)S(1)} %bitcast.20, bf16[1024,1024]{1,0:T(8,128)(2,1)S(1)} %copy-done), kind=kOutput, calls=%fused_computation.15 | convolution fusion | flops 1074266112 | bytes 5242880 | tf_op jit(solution)/shard_map/dot_general | solution.py:86
  203.7 2.9 %copy.15 = f32[1024,512]{1,0:T(8,128)} copy(f32[1024,512]{0,1:T(8,128)} %negate_bitcast_fusion) | data formatting | bytes 4194304 | tf_op jit(solution)/shard_map/neg | solution.py:86
  (40 shorter events, 2.8 us)
Async XLA Ops:
  6.5 194.5 %copy-start = (bf16[1024,1024]{1,0:T(8,128)(2,1)S(1)}, bf16[1024,1024]{1,0:T(8,128)(2,1)}, u32[]{:S(2)}) copy-start(bf16[1024,1024]{1,0:T(8,128)(2,1)} %param.9) | copy-start | bytes 6291460
  6.5 9.3 %copy-start.1 = (s32[1,1024]{1,0:T(1,128)S(1)}, s32[1,1024]{1,0:T(1,128)}, u32[]{:S(2)}) copy-start(s32[1,1024]{1,0:T(1,128)} %param.12) | copy-start | bytes 12292
  13.3 7.4 %copy-start.3 = (bf16[1024,512]{1,0:T(8,128)(2,1)S(1)}, bf16[1024,512]{1,0:T(8,128)(2,1)}, u32[]{:S(2)}) copy-start(bf16[1024,512]{1,0:T(8,128)(2,1)} %param.7) | copy-start | bytes 3145732
  24.0 9.4 %copy-start.5 = (s32[32]{0:T(128)S(1)}, s32[32]{0:T(128)}, u32[]{:S(2)}) copy-start(s32[32]{0:T(128)} %param.10) | copy-start | bytes 388
  24.0 9.6 %copy-start.2 = (s32[8192]{0:T(1024)S(1)}, s32[8192]{0:T(1024)}, u32[]{:S(2)}) copy-start(s32[8192]{0:T(1024)} %param.11) | copy-start | bytes 98308
  26.2 27.9 %all-to-all-start = ((bf16[32,24,512]{2,1,0:T(8,128)(2,1)}), bf16[32,24,512]{2,1,0:T(8,128)(2,1)S(1)}, u32[]{:S(2)}, u32[]{:S(2)}) async-start(bf16[32,24,512]{2,1,0:T(8,128)(2,1)} %broadcast_select_fusion), calls=%async_computation | async-start | bytes 1572864 | tf_op jit(solution)/shard_map/all_to_all | solution.py:50
  33.3 48.8 %all-gather.5.cloned.1.call-start = ((), (), s32[]{:S(2)}) async-start(), calls=%async_computation.5 | async-start | bytes 1310720 | tf_op jit(solution)/shard_map/all_gather | solution.py:68
  56.0 56.0 %all-gather.7.cloned.1.call-start = ((), (), s32[]{:S(2)}) async-start(), calls=%async_computation.6 | async-start | bytes 2359296 | tf_op jit(solution)/shard_map/all_gather | solution.py:70
  56.8 65.5 %copy-start.4 = (s32[1,1024]{1,0:T(1,128)S(1)}, s32[1,1024]{1,0:T(1,128)}, u32[]{:S(2)}) copy-start(s32[1,1024]{1,0:T(1,128)} %param.13) | copy-start | bytes 12292
  56.8 108.5 %reduce-scatter.2.cloned.1.call-start = ((), (), s32[]{:S(2)}) async-start(), calls=%async_computation.4 | async-start | bytes 2621440 | tf_op jit(solution)/shard_map/reduce_scatter | solution.py:72
Sparse Core Ops, SparseCore 0:
  56.1 25.9 all-gather.4
  84.0 27.9 all-gather.6
  121.8 43.4 reduce-scatter.1
where the time goes:
time: 214 us; the launch traced here: 213 us
  waiting for transfers between devices  105 us (49%)
  blocking collectives  42.2 us (20%)
  local copies, waits for them, and re-layouts  22.2 us (10%)
  between operations  13.3 us (6%)
  matrix products  12.3 us (6%)
  other arithmetic  10.5 us (5%)
  starting transfers between devices  7.22 us (3%)
    all_to_all x1, blocking collectives, shards(): lax.all_to_all(owned_result[lax.all_to_all(wanted, ('row', 'col'), split_...  30.7 us
    reduce_scatter x1, waiting for transfers between devices, shards(): lax.psum_scatter(partial_sums, 'col', scatter_dimension=0, tiled=True)  30.6 us
    all_gather x1, waiting for transfers between devices, shards(): lax.all_gather(owned_rows, 'row', axis=0, tiled=True)  29.9 us
    all_gather x1, waiting for transfers between devices, shards(): left_rows = lax.all_gather(owned_rows, 'col', axis=0, tiled=True)  25.3 us
    all_to_all x1, waiting for transfers between devices, shards(): lax.all_to_all(outgoing.reshape(box_total, capacity, NORB), ('row', 'col'...  18.9 us
    all_to_all x1, blocking collectives, shards(): lax.all_to_all(wanted, ('row', 'col'), split_axis=0, concat_axis=0, tiled...  11.5 us
    dot_general x1, matrix products, add_block(): return jnp.dot(weighted, shard_rows, preferred_element_type=jnp.float32)  9.65 us
    gather x2, local copies, waits for them, and re-layouts, shards(): picked = orbitals[grid_rows[0, source_slot]]  8.01 us
  transfers between devices with their start and end apart: 4, of which 4 were waited for; matrix products, arithmetic and copies ran while one was open for 2% of the time, Pallas kernels for 0%

commit v1 on v0

v1 whole, which is shorter than its diff:
```python
import functools

import jax
import jax.numpy as jnp
from jax import lax
from jax.experimental import pallas as pl
from jax.experimental.pallas import tpu as pltpu
from jax.sharding import PartitionSpec as P

NORB = 512
LIST = 1024
OWN = 256
SLOTS = 768
LANES = 128
VMEM_LIMIT = 48 * 1024 * 1024


def vmem():
    return pl.BlockSpec(memory_space=pltpu.VMEM)


def smem():
    return pl.BlockSpec(memory_space=pltpu.SMEM)


def params():
    return pltpu.CompilerParams(vmem_limit_bytes=VMEM_LIMIT)


def pick_kernel(box_total, capacity, scalars, counts, owner_map, grid_rows, orbitals, out):
    targets = box_total * capacity
    my_box = scalars[0]
    start = jnp.int32(0)
    for b in range(box_total):
        start = start + jnp.where(b < my_box, counts[b], 0)
    stop = start + counts[my_box]
    first = start // LANES
    shift = start - first * LANES
    blocks = SLOTS // LANES + 1
    top = owner_map.shape[0] - 1
    lane = lax.broadcasted_iota(jnp.int32, (1, LANES), 1)
    turned = pltpu.roll(grid_rows[...], shift, 1)
    lane8 = lax.broadcasted_iota(jnp.int32, turned.shape, 1)
    lined = jnp.where(lane8 < shift, pltpu.roll(turned, 1, 0), turned)
    before = (
        lax.broadcasted_iota(jnp.int32, (LANES, LANES), 0)
        < lax.broadcasted_iota(jnp.int32, (LANES, LANES), 1)
    ).astype(jnp.bfloat16)
    owner_ids = lax.broadcasted_iota(jnp.int32, (box_total, LANES), 0)
    target_ids = lax.broadcasted_iota(jnp.int32, (targets, LANES), 0)
    base = jnp.zeros((box_total, 1), jnp.float32)
    found = jnp.zeros((targets, LANES), jnp.int32)
    for i in range(blocks):
        k = (first + i) * LANES + lane
        position = owner_map[pl.ds(jnp.minimum(first + i, top), 1), :]
        live = (k >= start) & (k < stop)
        owner = jnp.where(live, position // OWN, -1)
        member = (owner_ids == owner).astype(jnp.float32)
        inner = jnp.dot(member.astype(jnp.bfloat16), before, preferred_element_type=jnp.float32)
        rank = jnp.sum(member * (inner + base), axis=0, keepdims=True).astype(jnp.int32)
        base = base + jnp.sum(member, axis=1, keepdims=True)
        target = jnp.where(live, owner * capacity + rank, -1)
        found = found + jnp.where(target_ids == target, lined[i : i + 1, :] + 1, 0)
    source = jnp.sum(found.astype(jnp.float32), axis=1, keepdims=True).astype(jnp.int32) - 1
    box = orbitals.shape[0]
    step = 256
    for t in range(0, targets, step):
        hot = source[t : t + step] == lax.broadcasted_iota(jnp.int32, (step, box), 1)
        out[t : t + step, :] = jnp.dot(
            hot.astype(jnp.float32).astype(jnp.bfloat16),
            orbitals[...],
            preferred_element_type=jnp.float32,
        ).astype(jnp.bfloat16)


def place_kernel(index, rows, out):
    hot = index[...] == lax.broadcasted_iota(jnp.int32, (index.shape[0], rows.shape[0]), 1)
    out[...] = jnp.dot(
        hot.astype(jnp.float32).astype(jnp.bfloat16), rows[...], preferred_element_type=jnp.float32
    ).astype(jnp.bfloat16)


def block_kernel(row_count, scalars, left, *refs):
    right = refs[: row_count // 2]
    mirrored, coulomb, out, tile, sem = refs[row_count // 2 :]
    block, me = scalars[0], scalars[1]
    copy = pltpu.make_async_copy(coulomb.at[pl.ds(block * OWN, OWN), :], tile, sem)
    copy.start()
    total = None
    for m in range(row_count):
        columns = right[m // 2][...] if m % 2 == 0 else mirrored[m // 2]
        pair = lax.dot_general(
            left[...], columns, (((1,), (1,)), ((), ())), preferred_element_type=jnp.float32
        ).astype(jnp.bfloat16)
        if m == 0:
            copy.wait()
        place = pl.multiple_of(jnp.bitwise_xor(me, m) * OWN, OWN)
        weighted = (
            pair.astype(jnp.float32) * tile[:, pl.ds(place, OWN)].astype(jnp.float32)
        ).astype(jnp.bfloat16)
        term = jnp.dot(weighted, columns, preferred_element_type=jnp.float32)
        total = term if total is None else total + term
    out[...] = total.astype(out.dtype)


def block_sum(row_count, block, me, left, right, mirrored, coulomb, dtype):
    flops = 4 * OWN * OWN * row_count * NORB
    return pl.pallas_call(
        functools.partial(block_kernel, row_count),
        out_shape=jax.ShapeDtypeStruct((OWN, NORB), dtype),
        in_specs=[smem(), vmem()]
        + [vmem()] * (row_count // 2 + 1)
        + [pl.BlockSpec(memory_space=pl.ANY)],
        out_specs=vmem(),
        scratch_shapes=[
            pltpu.VMEM((OWN, row_count * OWN), jnp.bfloat16),
            pltpu.SemaphoreType.DMA,
        ],
        compiler_params=params(),
        cost_estimate=pl.CostEstimate(
            flops=flops, bytes_accessed=OWN * OWN * row_count * 4, transcendentals=0
        ),
    )(jnp.stack([block, me]).astype(jnp.int32), left, *right, mirrored, coulomb)


def select_kernel(others, index, own, *refs):
    out = refs[others]
    total = own[...]
    for ref in refs[:others]:
        total = total + ref[...].astype(jnp.float32)
    projected = total.astype(jnp.bfloat16)
    hot = index[...] == lax.broadcasted_iota(jnp.int32, (index.shape[0], OWN), 1)
    out[...] = jnp.dot(
        hot.astype(jnp.float32).astype(jnp.bfloat16), projected, preferred_element_type=jnp.float32
    ).astype(jnp.bfloat16)


def apply_kernel(interp, chosen, out):
    out[...] = -jnp.dot(interp[...], chosen[...], preferred_element_type=jnp.float32)


def shards(orbitals, coulomb, interp, box_counts, owner_map, grid_rows, listed):
    row_count = lax.axis_size("row")
    col_count = lax.axis_size("col")
    box_total = row_count * col_count
    point_total = OWN * box_total
    capacity = (SLOTS + box_total - 1) // box_total
    per_owner = LIST // box_total
    my_row, my_col = lax.axis_index("row"), lax.axis_index("col")
    my_box = my_row * col_count + my_col
    all_listed = lax.all_gather(listed[0], ("row", "col"), axis=0, tiled=False)
    wanted = lax.dynamic_slice(all_listed, (0, my_box * per_owner), (box_total, per_owner))
    wanted = wanted.reshape(LIST, 1)

    outgoing = pl.pallas_call(
        functools.partial(pick_kernel, box_total, capacity),
        out_shape=jax.ShapeDtypeStruct((box_total * capacity, NORB), jnp.bfloat16),
        in_specs=[smem(), smem(), vmem(), vmem(), vmem()],
        out_specs=vmem(),
        compiler_params=params(),
        cost_estimate=pl.CostEstimate(
            flops=2 * SLOTS * LIST * NORB, bytes_accessed=2 << 20, transcendentals=0
        ),
    )(
        my_box.reshape(1).astype(jnp.int32),
        box_counts,
        owner_map.reshape(point_total // LANES, LANES),
        grid_rows.reshape(grid_rows.shape[1] // LANES, LANES),
        orbitals,
    )
    received = lax.all_to_all(
        outgoing.reshape(box_total, capacity, NORB),
        ("row", "col"),
        split_axis=0,
        concat_axis=0,
        tiled=True,
    ).reshape(box_total * capacity, NORB)

    wanted_pos = my_box * OWN + jnp.arange(OWN, dtype=jnp.int32)
    all_listing = jnp.arange(point_total, dtype=jnp.int32)
    my_points = jnp.sum(
        jnp.where(owner_map[None, :] == wanted_pos[:, None], all_listing[None, :], 0), axis=1
    )
    box_ends = jnp.cumsum(box_counts)
    source = jnp.sum((my_points[:, None] >= box_ends[None, :]).astype(jnp.int32), axis=1)
    earlier = (source[:, None] == source[None, :]) & (my_points[None, :] < my_points[:, None])
    source_rank = jnp.sum(earlier.astype(jnp.int32), axis=1)
    index = (source * capacity + source_rank).reshape(OWN, 1)
    owned_rows = pl.pallas_call(
        place_kernel,
        out_shape=jax.ShapeDtypeStruct((OWN, NORB), jnp.bfloat16),
        in_specs=[vmem(), vmem()],
        out_specs=vmem(),
        compiler_params=params(),
    )(index, received)

    left = [owned_rows]
    for d in range(1, col_count):
        left.append(
            lax.ppermute(owned_rows, "col", [((i + d) % col_count, i) for i in range(col_count)])
        )
    right = [owned_rows]
    for m in range(2, row_count, 2):
        right.append(lax.ppermute(owned_rows, "row", [(i, i ^ m) for i in range(row_count)]))
    mirrored = lax.ppermute(jnp.stack(right), "row", [(i, i ^ 1) for i in range(row_count)])

    sums = []
    for d in range(col_count):
        block = lax.rem(my_col + d, col_count)
        dtype = jnp.float32 if d == 0 else jnp.bfloat16
        sums.append(
            block_sum(row_count, block, my_row, left[d], right, mirrored, coulomb, dtype)
        )
    arrived = [
        lax.ppermute(sums[d], "col", [(i, (i + d) % col_count) for i in range(col_count)])
        for d in range(1, col_count)
    ]
    picked = pl.pallas_call(
        functools.partial(select_kernel, len(arrived)),
        out_shape=jax.ShapeDtypeStruct((LIST, NORB), jnp.bfloat16),
        in_specs=[vmem()] * (2 + len(arrived)),
        out_specs=vmem(),
        compiler_params=params(),
    )(wanted, sums[0], *arrived)
    chosen = lax.all_to_all(
        picked.reshape(box_total, per_owner, NORB),
        ("row", "col"),
        split_axis=0,
        concat_axis=0,
        tiled=True,
    ).reshape(LIST, NORB)
    box = interp.shape[0]
    step = 256
    return pl.pallas_call(
        apply_kernel,
        grid=(box // step,),
        out_shape=jax.ShapeDtypeStruct((box, NORB), jnp.float32),
        in_specs=[
            pl.BlockSpec((step, LIST), lambda i: (i, 0)),
            pl.BlockSpec((LIST, NORB), lambda i: (0, 0)),
        ],
        out_specs=pl.BlockSpec((step, NORB), lambda i: (i, 0)),
        compiler_params=params(),
    )(interp, chosen)


def solution(mesh):
    return jax.shard_map(
        shards,
        mesh=mesh,
        in_specs=(
            P(("row", "col"), None),
            P("row", "col"),
            P(("row", "col"), None),
            P(),
            P(),
            P(("row", "col"), None),
            P(("row", "col"), None),
        ),
        out_specs=P(("row", "col"), None),
        check_vma=False,
    )
```

time: 214 us -> 204 us (0.953)
  waiting for transfers between devices: 105 us -> 43.3 us
  blocking collectives: 42.2 us -> 99.3 us
  Pallas kernels: 0 us -> 24.2 us
  starting transfers between devices: 7.22 us -> 29.1 us
  local copies, waits for them, and re-layouts: 22.2 us -> 4.23 us
  between operations: 13.3 us -> 0.19 us
  matrix products: 12.3 us -> 0 us
  other arithmetic: 10.5 us -> 3.13 us
    all_gather x0 -> x1, blocking collectives: none -> 66.4 us  [shards(): all_listed = lax.all_gather(listed[0], ('row', 'col'), axis=0, tiled=False)]
    all_gather x2 -> x0, waiting for transfers between devices: 55.2 us -> none  [the longest x1 29.9 us: shards(): lax.all_gather(owned_rows, 'row', axis=0, tiled=True)]
    reduce_scatter x1 -> x0, waiting for transfers between devices: 30.6 us -> none  [shards(): lax.psum_scatter(partial_sums, 'col', scatter_dimension=0, tiled=True)]
    ppermute x0 -> x10, waiting for transfers between devices: none -> 24.4 us  [the longest x3 12.4 us: shards(): lax.ppermute(owned_rows, 'col', [((i + d) % col_count, i) for i in range(...]
    pallas_call x0 -> x8, Pallas kernels: none -> 24.2 us  [the longest x4 16 us: block_sum(): pl.pallas_call(functools.partial(block_kernel, row_count), out_shape=jax....]
    ppermute x0 -> x10, starting transfers between devices: none -> 22 us  [the longest x3 15.5 us: shards(): lax.ppermute(sums[d], 'col', [(i, (i + d) % col_count) for i in range(col...]
    gather x5 -> x0, local copies, waits for them, and re-layouts: 18.3 us -> none  [the longest x2 8.01 us: shards(): picked = orbitals[grid_rows[0, source_slot]]]
    dot_general x2 -> x0, matrix products: 12.3 us -> none  [the longest x1 9.65 us: add_block(): return jnp.dot(weighted, shard_rows, preferred_element_type=jnp.float32)]
  transfers between devices with their start and end apart: 4 -> 11, of which waited for: 4 -> 5; matrix products, arithmetic and copies ran while one was open for 2% -> 1% of each run, Pallas kernels for 0% -> 8%
where the time goes in v1:
time: 204 us; the launch traced here: 203 us
  blocking collectives  99.3 us (49%)
  waiting for transfers between devices  43.3 us (21%)
  starting transfers between devices  29.1 us (14%)
  Pallas kernels  24.2 us (12%)
  local copies, waits for them, and re-layouts  4.23 us (2%)
  other arithmetic  3.13 us (2%)
    all_gather x1, blocking collectives, shards(): all_listed = lax.all_gather(listed[0], ('row', 'col'), axis=0, tiled=False)  66.4 us
    all_to_all x1, blocking collectives, shards(): lax.all_to_all(picked.reshape(box_total, per_owner, NORB), ('row', 'col')...  32.9 us
    all_to_all x1, waiting for transfers between devices, shards(): lax.all_to_all(outgoing.reshape(box_total, capacity, NORB), ('row', 'col'...  18.8 us
    pallas_call x4, Pallas kernels, block_sum(): pl.pallas_call(functools.partial(block_kernel, row_count), out_shape=jax....  16 us
    ppermute x3, starting transfers between devices, shards(): lax.ppermute(sums[d], 'col', [(i, (i + d) % col_count) for i in range(col...  15.5 us
    ppermute x3, waiting for transfers between devices, shards(): lax.ppermute(owned_rows, 'col', [((i + d) % col_count, i) for i in range(...  12.4 us
    ppermute x3, waiting for transfers between devices, shards(): lax.ppermute(owned_rows, 'row', [(i, i ^ m) for i in range(row_count)])  12 us
    all_to_all x1, starting transfers between devices, shards(): lax.all_to_all(outgoing.reshape(box_total, capacity, NORB), ('row', 'col'...  7.1 us
  transfers between devices with their start and end apart: 11, of which 5 were waited for; matrix products, arithmetic and copies ran while one was open for 1% of the time, Pallas kernels for 8%

profile of v1, /device:TPU:1, one launch (start us, length us, event | category | flops | bytes accessed | tf_op | source)
XLA Modules:
  0.0 203.4 jit_solution(5787658249936454009)
XLA Ops:
  0.0 0.8 copy-done.1
  1.4 1.2 copy-done.5
  3.3 3.0 %shard_map.73 = bf16[768,512]{1,0:T(8,128)(2,1)} custom-call(s32[1]{0:T(128)} %bitcast.5.scalars, s32[32]{0:T(128)S(1)} %copy-done.3, s32[64,128]{1,0:T(8,128)S(1)} %bitcast.26, s32[8,128]{1,0:T(8,128)S(1)} %bitcast.28, bf16[1024,512]{1,0:T(8,128)(2,1)S(1)} %copy-done.5), custom_call_target="tpu_custom_call" | custom-call | flops 805306368 | bytes 2097152 | tf_op jit(solution)/shard_map/pallas_call | solution.py:155
  6.4 7.1 %all-to-all-start = ((bf16[32,24,512]{2,1,0:T(8,128)(2,1)}), bf16[32,24,512]{2,1,0:T(8,128)(2,1)S(1)}, u32[]{:S(2)}, u32[]{:S(2)}) async-start(bf16[32,24,512]{2,1,0:T(8,128)(2,1)} %bitcast.8), calls=%async_computation | async-start | bytes 1572864 | tf_op jit(solution)/shard_map/all_to_all | solution.py:171
  13.8 1.2 select_reduce_fusion
  15.5 18.8 %all-to-all-done = bf16[32,24,512]{2,1,0:T(8,128)(2,1)S(1)} async-done(((bf16[32,24,512]{2,1,0:T(8,128)(2,1)}), bf16[32,24,512]{2,1,0:T(8,128)(2,1)S(1)}, u32[]{:S(2)}, u32[]{:S(2)}) %all-to-all-start) | async-done | bytes 786464 | tf_op jit(solution)/shard_map/all_to_all | solution.py:171
  34.7 1.3 collective-permute-start
  36.3 1.2 collective-permute-start.2
  37.5 5.6 %collective-permute-done.refs_1_ = bf16[256,512]{1,0:T(8,128)(2,1)S(1)} collective-permute-done((bf16[256,512]{1,0:T(8,128)(2,1)S(1)}, bf16[256,512]{1,0:T(8,128)(2,1)S(1)}, u32[]{:S(2)}, u32[]{:S(2)}) %collective-permute-start) | collective-permute-done | bytes 262176 | tf_op jit(solution)/shard_map/ppermute | solution.py:204
  43.1 6.4 %collective-permute-done.1.refs_2_ = bf16[256,512]{1,0:T(8,128)(2,1)S(1)} collective-permute-done((bf16[256,512]{1,0:T(8,128)(2,1)S(1)}, bf16[256,512]{1,0:T(8,128)(2,1)S(1)}, u32[]{:S(2)}, u32[]{:S(2)}) %collective-permute-start.1) | collective-permute-done | bytes 262176 | tf_op jit(solution)/shard_map/ppermute | solution.py:204
  49.5 1.1 pad_maximum_fusion
  51.2 1.2 collective-permute-start.6
  52.5 2.0 collective-permute-start.4
  54.6 6.1 %collective-permute-done.8.left = bf16[256,512]{1,0:T(8,128)(2,1)S(1)} collective-permute-done((bf16[256,512]{1,0:T(8,128)(2,1)S(1)}, bf16[256,512]{1,0:T(8,128)(2,1)S(1)}, u32[]{:S(2)}, u32[]{:S(2)}) %collective-permute-start.8) | collective-permute-done | bytes 262176 | tf_op jit(solution)/shard_map/ppermute | solution.py:200
  60.7 4.0 %shard_map.78 = bf16[256,512]{1,0:T(8,128)(2,1)S(1)} custom-call(s32[2]{0:T(128)S(1)} %pad_add_fusion.3.scalars, bf16[256,512]{1,0:T(8,128)(2,1)S(1)} %collective-permute-done.8.left, bf16[256,512]{1,0:T(8,128)(2,1)S(1)} %shard_map.74.left.refs_0_, bf16[256,512]{1,0:T(8,128)(2,1)S(1)} %collective-permute-done.refs_1_, ...), custom_call_target="tpu_custom_call" | custom-call | flops 1073741824 | bytes 2097152 | tf_op jit(solution)/shard_map/pallas_call | solution.py:108
  64.8 6.3 %collective-permute-done.6.left = bf16[256,512]{1,0:T(8,128)(2,1)S(1)} collective-permute-done((bf16[256,512]{1,0:T(8,128)(2,1)S(1)}, bf16[256,512]{1,0:T(8,128)(2,1)S(1)}, u32[]{:S(2)}, u32[]{:S(2)}) %collective-permute-start.6) | collective-permute-done | bytes 262176 | tf_op jit(solution)/shard_map/ppermute | solution.py:200
  71.0 4.0 %shard_map.77 = bf16[256,512]{1,0:T(8,128)(2,1)S(1)} custom-call(s32[2]{0:T(128)S(1)} %pad_add_fusion.2.scalars, bf16[256,512]{1,0:T(8,128)(2,1)S(1)} %collective-permute-done.6.left, bf16[256,512]{1,0:T(8,128)(2,1)S(1)} %shard_map.74.left.refs_0_, bf16[256,512]{1,0:T(8,128)(2,1)S(1)} %collective-permute-done.refs_1_, ...), custom_call_target="tpu_custom_call" | custom-call | flops 1073741824 | bytes 2097152 | tf_op jit(solution)/shard_map/pallas_call | solution.py:108
  75.2 4.0 %shard_map.76 = bf16[256,512]{1,0:T(8,128)(2,1)S(1)} custom-call(s32[2]{0:T(128)S(1)} %pad_add_fusion.1.scalars, bf16[256,512]{1,0:T(8,128)(2,1)S(1)} %collective-permute-done.4.left, bf16[256,512]{1,0:T(8,128)(2,1)S(1)} %shard_map.74.left.refs_0_, bf16[256,512]{1,0:T(8,128)(2,1)S(1)} %collective-permute-done.refs_1_, ...), custom_call_target="tpu_custom_call" | custom-call | flops 1073741824 | bytes 2097152 | tf_op jit(solution)/shard_map/pallas_call | solution.py:108
  79.2 15.4 %collective-permute-start.5 = (bf16[256,512]{1,0:T(8,128)(2,1)S(1)}, bf16[256,512]{1,0:T(8,128)(2,1)}, u32[]{:S(2)}, u32[]{:S(2)}) collective-permute-start(bf16[256,512]{1,0:T(8,128)(2,1)S(1)} %shard_map.76), channel_id=1, source_target_pairs={{0,1},{1,2},{2,3},{3,0},{4,5},{5,6},{6,7},{7,4},{8,9},{9,10},{10,1... | collective-permute-start | bytes 786440 | tf_op jit(solution)/shard_map/ppermute | solution.py:215
  94.6 66.4 %all-gather = s32[32,1,1024]{2,1,0:T(1,128)S(1)} all-gather(s32[1,1,1024]{2,1,0:T(1,128)S(1)} %bitcast.30), channel_id=1, replica_groups=mesh['row'=8,'col'=4] {'row','col'}, dimensions={0}, use_global_device_ids=true | all-gather | bytes 135168 | tf_op jit(solution)/shard_map/all_gather | solution.py:151
  161.7 4.0 %shard_map.75.own = f32[256,512]{1,0:T(8,128)S(1)} custom-call(s32[2]{0:T(128)S(1)} %pad_add_fusion.scalars, bf16[256,512]{1,0:T(8,128)(2,1)S(1)} %shard_map.74.left.refs_0_, bf16[256,512]{1,0:T(8,128)(2,1)S(1)} %shard_map.74.left.refs_0_, bf16[256,512]{1,0:T(8,128)(2,1)S(1)} %collective-permute-done.refs_1_, ...), custom_call_target="tpu_custom_call" | custom-call | flops 1073741824 | bytes 2097152 | tf_op jit(solution)/shard_map/pallas_call | solution.py:108
  165.8 1.8 shard_map.79
  167.6 32.9 %all_to_all.10 = bf16[32,32,512]{2,1,0:T(8,128)(2,1)S(1)} all-to-all(bf16[32,32,512]{2,1,0:T(8,128)(2,1)S(1)} %bitcast.24), channel_id=1, replica_groups=mesh['row'=8,'col'=4] {'row','col'}, dimensions={0} | all-to-all | bytes 2097152 | tf_op jit(solution)/shard_map/all_to_all | solution.py:225
  200.4 2.9 %shard_map.80 = f32[1024,512]{1,0:T(8,128)} custom-call(bf16[1024,1024]{1,0:T(8,128)(2,1)S(1)} %copy-done, bf16[1024,512]{1,0:T(8,128)(2,1)S(1)} %bitcast.23), custom_call_target="tpu_custom_call" | custom-call | tf_op jit(solution)/shard_map/pallas_call | solution.py:234
  (40 shorter events, 4.4 us)
Async XLA Ops:
  0.0 13.5 %copy-start.4 = (s32[32]{0:T(128)S(1)}, s32[32]{0:T(128)}, u32[]{:S(2)}) copy-start(s32[32]{0:T(128)} %counts.1) | copy-start | bytes 388
  0.0 0.8 copy-start.1
  0.8 0.7 copy-start.3
  1.4 1.2 copy-start.5
  2.7 0.7 copy-start.6
  3.3 10.4 %copy-start.2 = (s32[8192]{0:T(1024)S(1)}, s32[8192]{0:T(1024)}, u32[]{:S(2)}) copy-start(s32[8192]{0:T(1024)} %param.11) | copy-start | bytes 98308
  6.4 27.9 %all-to-all-start = ((bf16[32,24,512]{2,1,0:T(8,128)(2,1)}), bf16[32,24,512]{2,1,0:T(8,128)(2,1)S(1)}, u32[]{:S(2)}, u32[]{:S(2)}) async-start(bf16[32,24,512]{2,1,0:T(8,128)(2,1)} %bitcast.8), calls=%async_computation | async-start | bytes 1572864 | tf_op jit(solution)/shard_map/all_to_all | solution.py:171
  34.7 8.3 %collective-permute-start = (bf16[256,512]{1,0:T(8,128)(2,1)S(1)}, bf16[256,512]{1,0:T(8,128)(2,1)S(1)}, u32[]{:S(2)}, u32[]{:S(2)}) collective-permute-start(bf16[256,512]{1,0:T(8,128)(2,1)S(1)} %shard_map.74.left.refs_0_), channel_id=1, source_target_pairs={{0,8},{4,12},{8,0},{12,4},{16,24},{20,28},{24,16},{28,20},{1,9},{5... | collective-permute-start | bytes 786440 | tf_op jit(solution)/shard_map/ppermute | solution.py:204
  36.0 13.5 %collective-permute-start.1 = (bf16[256,512]{1,0:T(8,128)(2,1)S(1)}, bf16[256,512]{1,0:T(8,128)(2,1)S(1)}, u32[]{:S(2)}, u32[]{:S(2)}) collective-permute-start(bf16[256,512]{1,0:T(8,128)(2,1)S(1)} %shard_map.74.left.refs_0_), channel_id=1, source_target_pairs={{0,16},{4,20},{8,24},{12,28},{16,0},{20,4},{24,8},{28,12},{1,17},{... | collective-permute-start | bytes 786440 | tf_op jit(solution)/shard_map/ppermute | solution.py:204
  36.3 13.2 %collective-permute-start.2 = (bf16[256,512]{1,0:T(8,128)(2,1)S(1)}, bf16[256,512]{1,0:T(8,128)(2,1)S(1)}, u32[]{:S(2)}, u32[]{:S(2)}) collective-permute-start(bf16[256,512]{1,0:T(8,128)(2,1)S(1)} %shard_map.74.left.refs_0_), channel_id=1, source_target_pairs={{0,24},{4,28},{8,16},{12,20},{16,8},{20,12},{24,0},{28,4},{1,25},{... | collective-permute-start | bytes 786440 | tf_op jit(solution)/shard_map/ppermute | solution.py:204
  50.6 10.1 %collective-permute-start.3 = (bf16[4,256,512]{2,1,0:T(8,128)(2,1)}, bf16[4,256,512]{2,1,0:T(8,128)(2,1)S(1)}, u32[]{:S(2)}, u32[]{:S(2)}) collective-permute-start(bf16[4,256,512]{2,1,0:T(8,128)(2,1)} %pad_maximum_fusion), channel_id=1, source_target_pairs={{0,4},{4,0},{8,12},{12,8},{16,20},{20,16},{24,28},{28,24},{1,5},{5... | collective-permute-start | bytes 3145736 | tf_op jit(solution)/shard_map/ppermute | solution.py:205
  51.0 9.7 %collective-permute-start.8 = (bf16[256,512]{1,0:T(8,128)(2,1)S(1)}, bf16[256,512]{1,0:T(8,128)(2,1)S(1)}, u32[]{:S(2)}, u32[]{:S(2)}) collective-permute-start(bf16[256,512]{1,0:T(8,128)(2,1)S(1)} %shard_map.74.left.refs_0_), channel_id=1, source_target_pairs={{3,0},{0,1},{1,2},{2,3},{7,4},{4,5},{5,6},{6,7},{11,8},{8,9},{9,10... | collective-permute-start | bytes 786440 | tf_op jit(solution)/shard_map/ppermute | solution.py:200
  51.2 19.9 %collective-permute-start.6 = (bf16[256,512]{1,0:T(8,128)(2,1)S(1)}, bf16[256,512]{1,0:T(8,128)(2,1)S(1)}, u32[]{:S(2)}, u32[]{:S(2)}) collective-permute-start(bf16[256,512]{1,0:T(8,128)(2,1)S(1)} %shard_map.74.left.refs_0_), channel_id=1, source_target_pairs={{2,0},{3,1},{0,2},{1,3},{6,4},{7,5},{4,6},{5,7},{10,8},{11,9},{8,1... | collective-permute-start | bytes 786440 | tf_op jit(solution)/shard_map/ppermute | solution.py:200
  52.5 22.7 %collective-permute-start.4 = (bf16[256,512]{1,0:T(8,128)(2,1)S(1)}, bf16[256,512]{1,0:T(8,128)(2,1)S(1)}, u32[]{:S(2)}, u32[]{:S(2)}) collective-permute-start(bf16[256,512]{1,0:T(8,128)(2,1)S(1)} %shard_map.74.left.refs_0_), channel_id=1, source_target_pairs={{1,0},{2,1},{3,2},{0,3},{5,4},{6,5},{7,6},{4,7},{9,8},{10,9},{11,1... | collective-permute-start | bytes 786440 | tf_op jit(solution)/shard_map/ppermute | solution.py:200
  64.7 101.1 %collective-permute-start.9 = (bf16[256,512]{1,0:T(8,128)(2,1)S(1)}, bf16[256,512]{1,0:T(8,128)(2,1)}, u32[]{:S(2)}, u32[]{:S(2)}) collective-permute-start(bf16[256,512]{1,0:T(8,128)(2,1)S(1)} %shard_map.78), channel_id=1, source_target_pairs={{0,3},{1,0},{2,1},{3,2},{4,7},{5,4},{6,5},{7,6},{8,11},{9,8},{10,9... | collective-permute-start | bytes 786440 | tf_op jit(solution)/shard_map/ppermute | solution.py:215
  75.1 19.5 %copy-start.7 = (s32[1,1024]{1,0:T(1,128)S(1)}, s32[1,1024]{1,0:T(1,128)}, u32[]{:S(2)}) copy-start(s32[1,1024]{1,0:T(1,128)} %param.13) | copy-start | bytes 12292
  75.1 90.7 %collective-permute-start.7 = (bf16[256,512]{1,0:T(8,128)(2,1)S(1)}, bf16[256,512]{1,0:T(8,128)(2,1)}, u32[]{:S(2)}, u32[]{:S(2)}) collective-permute-start(bf16[256,512]{1,0:T(8,128)(2,1)S(1)} %shard_map.77), channel_id=1, source_target_pairs={{0,2},{1,3},{2,0},{3,1},{4,6},{5,7},{6,4},{7,5},{8,10},{9,11},{10,... | collective-permute-start | bytes 786440 | tf_op jit(solution)/shard_map/ppermute | solution.py:215
  79.2 86.6 %collective-permute-start.5 = (bf16[256,512]{1,0:T(8,128)(2,1)S(1)}, bf16[256,512]{1,0:T(8,128)(2,1)}, u32[]{:S(2)}, u32[]{:S(2)}) collective-permute-start(bf16[256,512]{1,0:T(8,128)(2,1)S(1)} %shard_map.76), channel_id=1, source_target_pairs={{0,1},{1,2},{2,3},{3,0},{4,5},{5,6},{6,7},{7,4},{8,9},{9,10},{10,1... | collective-permute-start | bytes 786440 | tf_op jit(solution)/shard_map/ppermute | solution.py:215
  165.8 34.7 %copy-start = (bf16[1024,1024]{1,0:T(8,128)(2,1)S(1)}, bf16[1024,1024]{1,0:T(8,128)(2,1)}, u32[]{:S(2)}) copy-start(bf16[1024,1024]{1,0:T(8,128)(2,1)} %interp.1) | copy-start | bytes 6291460

commit v2 on v1

--- a/solution.py
+++ b/solution.py
@@ -13,6 +13,7 @@
 SLOTS = 768
 LANES = 128
 VMEM_LIMIT = 48 * 1024 * 1024
+PICK_LIMIT = 60 * 1024 * 1024
 
 
 def vmem():
@@ -23,11 +24,26 @@
     return pl.BlockSpec(memory_space=pltpu.SMEM)
 
 
-def params():
-    return pltpu.CompilerParams(vmem_limit_bytes=VMEM_LIMIT)
-
-
-def pick_kernel(box_total, capacity, scalars, counts, owner_map, grid_rows, orbitals, out):
+def hbm():
+    return pl.BlockSpec(memory_space=pltpu.HBM)
+
+
+def params(limit=VMEM_LIMIT):
+    return pltpu.CompilerParams(vmem_limit_bytes=limit)
+
+
+def pick_kernel(
+    box_total, capacity, scalars, counts, owner_hbm, grid_hbm, orbitals_hbm, out,
+    owner_map, grid_rows, orbitals, sems,
+):
+    copies = [
+        pltpu.make_async_copy(source, target, sems.at[n])
+        for n, (source, target) in enumerate(
+            [(grid_hbm, grid_rows), (owner_hbm, owner_map), (orbitals_hbm, orbitals)]
+        )
+    ]
+    for copy in copies:
+        copy.start()
     targets = box_total * capacity
     my_box = scalars[0]
     start = jnp.int32(0)
@@ -39,6 +55,8 @@
     blocks = SLOTS // LANES + 1
     top = owner_map.shape[0] - 1
     lane = lax.broadcasted_iota(jnp.int32, (1, LANES), 1)
+    copies[0].wait()
+    copies[1].wait()
     turned = pltpu.roll(grid_rows[...], shift, 1)
     lane8 = lax.broadcasted_iota(jnp.int32, turned.shape, 1)
     lined = jnp.where(lane8 < shift, pltpu.roll(turned, 1, 0), turned)
@@ -64,6 +82,7 @@
     source = jnp.sum(found.astype(jnp.float32), axis=1, keepdims=True).astype(jnp.int32) - 1
     box = orbitals.shape[0]
     step = 256
+    copies[2].wait()
     for t in range(0, targets, step):
         hot = source[t : t + step] == lax.broadcasted_iota(jnp.int32, (step, box), 1)
         out[t : t + step, :] = jnp.dot(
@@ -80,56 +99,85 @@
     ).astype(jnp.bfloat16)
 
 
-def block_kernel(row_count, scalars, left, *refs):
-    right = refs[: row_count // 2]
-    mirrored, coulomb, out, tile, sem = refs[row_count // 2 :]
-    block, me = scalars[0], scalars[1]
-    copy = pltpu.make_async_copy(coulomb.at[pl.ds(block * OWN, OWN), :], tile, sem)
-    copy.start()
-    total = None
-    for m in range(row_count):
-        columns = right[m // 2][...] if m % 2 == 0 else mirrored[m // 2]
-        pair = lax.dot_general(
-            left[...], columns, (((1,), (1,)), ((), ())), preferred_element_type=jnp.float32
+def block_kernel(masks, scalars, left, *refs):
+    columns = refs[: len(masks)]
+    coulomb, *earlier, out, right, tile, weighted, sems = refs[len(masks) :]
+    rows = pl.ds(pl.multiple_of(scalars[0] * OWN, OWN), OWN)
+    copies = []
+    for n, mask in enumerate(masks):
+        place = pl.multiple_of(jnp.bitwise_xor(scalars[1], mask) * OWN, OWN)
+        copies.append(
+            pltpu.make_async_copy(
+                coulomb.at[rows, pl.ds(place, OWN)],
+                tile.at[:, n * OWN : (n + 1) * OWN],
+                sems.at[n],
+            )
+        )
+        copies[-1].start()
+    for n, ref in enumerate(columns):
+        right[n * OWN : (n + 1) * OWN, :] = ref[...]
+    step = 512
+    for t in range(0, right.shape[0], step):
+        weighted[:, t : t + step] = lax.dot_general(
+            left[...],
+            right[t : t + step, :],
+            (((1,), (1,)), ((), ())),
+            preferred_element_type=jnp.float32,
         ).astype(jnp.bfloat16)
-        if m == 0:
-            copy.wait()
-        place = pl.multiple_of(jnp.bitwise_xor(me, m) * OWN, OWN)
-        weighted = (
-            pair.astype(jnp.float32) * tile[:, pl.ds(place, OWN)].astype(jnp.float32)
+    for copy in copies:
+        copy.wait()
+    for t in range(0, right.shape[0], step):
+        pair = weighted[:, t : t + step].astype(jnp.float32)
+        weighted[:, t : t + step] = (
+            pair * tile[:, t : t + step].astype(jnp.float32)
         ).astype(jnp.bfloat16)
-        term = jnp.dot(weighted, columns, preferred_element_type=jnp.float32)
-        total = term if total is None else total + term
+    total = jnp.dot(weighted[...], right[...], preferred_element_type=jnp.float32)
+    for ref in earlier:
+        total = total + ref[...]
     out[...] = total.astype(out.dtype)
 
 
-def block_sum(row_count, block, me, left, right, mirrored, coulomb, dtype):
-    flops = 4 * OWN * OWN * row_count * NORB
+def block_sum(masks, block, me, left, right, coulomb, dtype, earlier=()):
+    columns = len(masks) * OWN
     return pl.pallas_call(
-        functools.partial(block_kernel, row_count),
+        functools.partial(block_kernel, masks),
         out_shape=jax.ShapeDtypeStruct((OWN, NORB), dtype),
         in_specs=[smem(), vmem()]
-        + [vmem()] * (row_count // 2 + 1)
-        + [pl.BlockSpec(memory_space=pl.ANY)],
+        + [vmem()] * len(masks)
+        + [hbm()]
+        + [vmem()] * len(earlier),
         out_specs=vmem(),
         scratch_shapes=[
-            pltpu.VMEM((OWN, row_count * OWN), jnp.bfloat16),
-            pltpu.SemaphoreType.DMA,
+            pltpu.VMEM((columns, NORB), jnp.bfloat16),
+            pltpu.VMEM((OWN, columns), jnp.bfloat16),
+            pltpu.VMEM((OWN, columns), jnp.bfloat16),
+            pltpu.SemaphoreType.DMA((len(masks),)),
         ],
         compiler_params=params(),
-        cost_estimate=pl.CostEstimate(
-            flops=flops, bytes_accessed=OWN * OWN * row_count * 4, transcendentals=0
-        ),
-    )(jnp.stack([block, me]).astype(jnp.int32), left, *right, mirrored, coulomb)
+        cost_estimate=pl.CostEstimate(flops=0, bytes_accessed=0, transcendentals=0),
+    )(
+        jnp.stack([block, me]).astype(jnp.int32),
+        left,
+        *[right[mask] for mask in masks],
+        coulomb,
+        *earlier,
+    )
 
 
 def select_kernel(others, index, own, *refs):
+    boxes, per_owner = index.shape
+    spread = jnp.broadcast_to(index[...][:, None, :], (boxes, per_owner, per_owner))
+    diagonal = lax.broadcasted_iota(jnp.int32, spread.shape, 1) == lax.broadcasted_iota(
+        jnp.int32, spread.shape, 2
+    )
+    picks = jnp.sum(jnp.where(diagonal, spread, 0).astype(jnp.float32), axis=2, keepdims=True)
+    picks = picks.reshape(boxes * per_owner, 1).astype(jnp.int32)
     out = refs[others]
     total = own[...]
     for ref in refs[:others]:
         total = total + ref[...].astype(jnp.float32)
     projected = total.astype(jnp.bfloat16)
-    hot = index[...] == lax.broadcasted_iota(jnp.int32, (index.shape[0], OWN), 1)
+    hot = picks == lax.broadcasted_iota(jnp.int32, (boxes * per_owner, OWN), 1)
     out[...] = jnp.dot(
         hot.astype(jnp.float32).astype(jnp.bfloat16), projected, preferred_element_type=jnp.float32
     ).astype(jnp.bfloat16)
@@ -148,16 +196,18 @@
     per_owner = LIST // box_total
     my_row, my_col = lax.axis_index("row"), lax.axis_index("col")
     my_box = my_row * col_count + my_col
-    all_listed = lax.all_gather(listed[0], ("row", "col"), axis=0, tiled=False)
-    wanted = lax.dynamic_slice(all_listed, (0, my_box * per_owner), (box_total, per_owner))
-    wanted = wanted.reshape(LIST, 1)
-
     outgoing = pl.pallas_call(
         functools.partial(pick_kernel, box_total, capacity),
         out_shape=jax.ShapeDtypeStruct((box_total * capacity, NORB), jnp.bfloat16),
-        in_specs=[smem(), smem(), vmem(), vmem(), vmem()],
+        in_specs=[smem(), smem(), hbm(), hbm(), hbm()],
         out_specs=vmem(),
-        compiler_params=params(),
+        scratch_shapes=[
+            pltpu.VMEM((point_total // LANES, LANES), jnp.int32),
+            pltpu.VMEM((grid_rows.shape[1] // LANES, LANES), jnp.int32),
+            pltpu.VMEM(orbitals.shape, jnp.bfloat16),
+            pltpu.SemaphoreType.DMA((3,)),
+        ],
+        compiler_params=params(PICK_LIMIT),
         cost_estimate=pl.CostEstimate(
             flops=2 * SLOTS * LIST * NORB, bytes_accessed=2 << 20, transcendentals=0
         ),
@@ -199,29 +249,47 @@
         left.append(
             lax.ppermute(owned_rows, "col", [((i + d) % col_count, i) for i in range(col_count)])
         )
-    right = [owned_rows]
-    for m in range(2, row_count, 2):
-        right.append(lax.ppermute(owned_rows, "row", [(i, i ^ m) for i in range(row_count)]))
-    mirrored = lax.ppermute(jnp.stack(right), "row", [(i, i ^ 1) for i in range(row_count)])
-
-    sums = []
-    for d in range(col_count):
-        block = lax.rem(my_col + d, col_count)
-        dtype = jnp.float32 if d == 0 else jnp.bfloat16
-        sums.append(
-            block_sum(row_count, block, my_row, left[d], right, mirrored, coulomb, dtype)
-        )
+    def flip(rows, mask):
+        return lax.ppermute(rows, "row", [(i, i ^ mask) for i in range(row_count)])
+
+    even, odd = list(range(0, row_count, 2)), list(range(1, row_count, 2))
+    right = {0: owned_rows}
+    for mask in even[1:]:
+        right[mask] = flip(owned_rows, mask)
+    for mask in even:
+        right[mask + 1] = flip(right[mask], 1)
+
+    def block_of(d):
+        return lax.rem(my_col + d, col_count)
+
+    def run(masks, d, dtype, earlier=()):
+        return block_sum(masks, block_of(d), my_row, left[d], right, coulomb, dtype, earlier)
+
+    sums = [None] * col_count
+    first = run(even, 1, jnp.float32)
+    sums[1] = run(odd, 1, jnp.bfloat16, (first,))
+    for d in range(2, col_count):
+        sums[d] = run(even + odd, d, jnp.bfloat16)
+    sums[0] = run(even + odd, 0, jnp.float32)
     arrived = [
         lax.ppermute(sums[d], "col", [(i, (i + d) % col_count) for i in range(col_count)])
         for d in range(1, col_count)
     ]
+    own_sum, asked = lax.optimization_barrier((sums[0], listed[0]))
+    wanted = lax.all_to_all(
+        asked.reshape(box_total, per_owner),
+        ("row", "col"),
+        split_axis=0,
+        concat_axis=0,
+        tiled=True,
+    )
     picked = pl.pallas_call(
         functools.partial(select_kernel, len(arrived)),
         out_shape=jax.ShapeDtypeStruct((LIST, NORB), jnp.bfloat16),
         in_specs=[vmem()] * (2 + len(arrived)),
         out_specs=vmem(),
         compiler_params=params(),
-    )(wanted, sums[0], *arrived)
+    )(wanted, own_sum, *arrived)
     chosen = lax.all_to_all(
         picked.reshape(box_total, per_owner, NORB),
         ("row", "col"),

time: 204 us -> 126 us (0.62)
  blocking collectives: 99.3 us -> 39.9 us
  waiting for transfers between devices: 43.3 us -> 33.8 us
  starting transfers between devices: 29.1 us -> 23.2 us
    all_gather x1 -> x0, blocking collectives: 66.4 us -> none  [shards(): all_listed = lax.all_gather(listed[0], ('row', 'col'), axis=0, tiled=False)]
    all_to_all x0 -> x1, blocking collectives: none -> 9.31 us  [shards(): lax.all_to_all(asked.reshape(box_total, per_owner), ('row', 'col'), split...]
    ppermute x3, waiting for transfers between devices: 12.4 us -> 5.35 us  [shards(): lax.ppermute(owned_rows, 'col', [((i + d) % col_count, i) for i in range(...]
    ppermute x3, starting transfers between devices: 15.5 us -> 8.73 us  [shards(): lax.ppermute(sums[d], 'col', [(i, (i + d) % col_count) for i in range(col...]
    ppermute x4 -> x7, waiting for transfers between devices: 12 us -> 9.57 us  [flip(): return lax.ppermute(rows, 'row', [(i, i ^ mask) for i in range(row_count)])]
    all_to_all x1, blocking collectives: 32.9 us -> 30.5 us  [shards(): lax.all_to_all(picked.reshape(box_total, per_owner, NORB), ('row', 'col')...]
    ppermute x4 -> x7, starting transfers between devices: 3.11 us -> 4.65 us  [flip(): return lax.ppermute(rows, 'row', [(i, i ^ mask) for i in range(row_count)])]
    pallas_call x4 -> x5, Pallas kernels: 16 us -> 15.1 us  [block_sum(): pl.pallas_call(functools.partial(block_kernel, masks), out_shape=jax.Shap...]
  transfers between devices with their start and end apart: 11 -> 14, of which waited for: 5 -> 4; matrix products, arithmetic and copies ran while one was open for 1% -> 2% of each run, Pallas kernels for 8% -> 12%
where the time goes in v2:
time: 126 us
  blocking collectives  39.9 us (32%)
  waiting for transfers between devices  33.8 us (27%)
  Pallas kernels  24 us (19%)
  starting transfers between devices  23.2 us (18%)
  local copies, waits for them, and re-layouts  2.52 us (2%)
  other arithmetic  2.03 us (2%)
    all_to_all x1, blocking collectives, shards(): lax.all_to_all(picked.reshape(box_total, per_owner, NORB), ('row', 'col')...  30.5 us
    all_to_all x1, waiting for transfers between devices, shards(): lax.all_to_all(outgoing.reshape(box_total, capacity, NORB), ('row', 'col'...  18.8 us
    pallas_call x5, Pallas kernels, block_sum(): pl.pallas_call(functools.partial(block_kernel, masks), out_shape=jax.Shap...  15.1 us
    ppermute x7, waiting for transfers between devices, flip(): return lax.ppermute(rows, 'row', [(i, i ^ mask) for i in range(row_count)])  9.57 us
    all_to_all x1, blocking collectives, shards(): lax.all_to_all(asked.reshape(box_total, per_owner), ('row', 'col'), split...  9.31 us
    ppermute x3, starting transfers between devices, shards(): lax.ppermute(sums[d], 'col', [(i, (i + d) % col_count) for i in range(col...  8.73 us
    all_to_all x1, starting transfers between devices, shards(): lax.all_to_all(outgoing.reshape(box_total, capacity, NORB), ('row', 'col'...  7.1 us
    ppermute x3, waiting for transfers between devices, shards(): lax.ppermute(owned_rows, 'col', [((i + d) % col_count, i) for i in range(...  5.35 us
  transfers between devices with their start and end apart: 14, of which 4 were waited for; matrix products, arithmetic and copies ran while one was open for 2% of the time, Pallas kernels for 12%

profile of v2, /device:TPU:1, one launch (start us, length us, event | category | flops | bytes accessed | tf_op | source)
XLA Modules:
  0.0 125.5 jit_solution(17802497288283241207)
XLA Ops:
  0.0 4.0 %shard_map.73 = bf16[768,512]{1,0:T(8,128)(2,1)} custom-call(s32[1]{0:T(128)} %bitcast.4.scalars, s32[32]{0:T(128)} %counts.1, s32[64,128]{1,0:T(8,128)} %bitcast.21, s32[8,128]{1,0:T(8,128)} %bitcast.25, bf16[1024,512]{1,0:T(8,128)(2,1)} %orbitals_hbm.1), custom_call_target="tpu_custom_call" | custom-call | flops 805306368 | bytes 2097152 | tf_op jit(solution)/shard_map/pallas_call | solution.py:199
  4.0 7.1 %all-to-all-start = ((bf16[32,24,512]{2,1,0:T(8,128)(2,1)}), bf16[32,24,512]{2,1,0:T(8,128)(2,1)S(1)}, u32[]{:S(2)}, u32[]{:S(2)}) async-start(bf16[32,24,512]{2,1,0:T(8,128)(2,1)} %bitcast.20), calls=%async_computation | async-start | bytes 1572864 | tf_op jit(solution)/shard_map/all_to_all | solution.py:221
  11.4 1.2 select_reduce_fusion
  13.1 18.8 %all-to-all-done = bf16[32,24,512]{2,1,0:T(8,128)(2,1)S(1)} async-done(((bf16[32,24,512]{2,1,0:T(8,128)(2,1)}), bf16[32,24,512]{2,1,0:T(8,128)(2,1)S(1)}, u32[]{:S(2)}, u32[]{:S(2)}) %all-to-all-start) | async-done | bytes 786464 | tf_op jit(solution)/shard_map/all_to_all | solution.py:221
  32.4 1.3 %collective-permute-start = (bf16[256,512]{1,0:T(8,128)(2,1)S(1)}, bf16[256,512]{1,0:T(8,128)(2,1)S(1)}, u32[]{:S(2)}, u32[]{:S(2)}) collective-permute-start(bf16[256,512]{1,0:T(8,128)(2,1)S(1)} %shard_map.74.left.refs_0_), channel_id=1, source_target_pairs={{0,8},{4,12},{8,0},{12,4},{16,24},{20,28},{24,16},{28,20},{1,9},{5... | collective-permute-start | bytes 786440 | tf_op jit(solution)/shard_map/ppermute | solution.py:253
  33.9 1.2 collective-permute-start.2
  35.1 2.7 %collective-permute-start.7 = (bf16[256,512]{1,0:T(8,128)(2,1)S(1)}, bf16[256,512]{1,0:T(8,128)(2,1)S(1)}, u32[]{:S(2)}, u32[]{:S(2)}) collective-permute-start(bf16[256,512]{1,0:T(8,128)(2,1)S(1)} %shard_map.74.left.refs_0_), channel_id=1, source_target_pairs={{1,0},{2,1},{3,2},{0,3},{5,4},{6,5},{7,6},{4,7},{9,8},{10,9},{11,1... | collective-permute-start | bytes 786440 | tf_op jit(solution)/shard_map/ppermute | solution.py:250
  37.8 2.9 %collective-permute-done.refs_1_ = bf16[256,512]{1,0:T(8,128)(2,1)S(1)} collective-permute-done((bf16[256,512]{1,0:T(8,128)(2,1)S(1)}, bf16[256,512]{1,0:T(8,128)(2,1)S(1)}, u32[]{:S(2)}, u32[]{:S(2)}) %collective-permute-start) | collective-permute-done | bytes 262176 | tf_op jit(solution)/shard_map/ppermute | solution.py:253
  40.7 6.7 %collective-permute-done.1.refs_2_ = bf16[256,512]{1,0:T(8,128)(2,1)S(1)} collective-permute-done((bf16[256,512]{1,0:T(8,128)(2,1)S(1)}, bf16[256,512]{1,0:T(8,128)(2,1)S(1)}, u32[]{:S(2)}, u32[]{:S(2)}) %collective-permute-start.1) | collective-permute-done | bytes 262176 | tf_op jit(solution)/shard_map/ppermute | solution.py:253
  47.4 1.4 %collective-permute-start.4 = (bf16[256,512]{1,0:T(8,128)(2,1)S(1)}, bf16[256,512]{1,0:T(8,128)(2,1)S(1)}, u32[]{:S(2)}, u32[]{:S(2)}) collective-permute-start(bf16[256,512]{1,0:T(8,128)(2,1)S(1)} %collective-permute-done.refs_1_), channel_id=1, source_target_pairs={{0,4},{4,0},{8,12},{12,8},{16,20},{20,16},{24,28},{28,24},{1,5},{5... | collective-permute-start | bytes 786440 | tf_op jit(solution)/shard_map/ppermute | solution.py:253
  48.9 0.4 collective-permute-start.6
  49.6 2.2 %copy-done = bf16[1024,2048]{1,0:T(8,128)(2,1)S(1)} copy-done((bf16[1024,2048]{1,0:T(8,128)(2,1)S(1)}, bf16[1024,2048]{1,0:T(8,128)(2,1)}, u32[]{:S(2)}) %copy-start) | copy-done | bytes 4194328
  51.7 1.6 %shard_map.76.refs_5_ = f32[256,512]{1,0:T(8,128)S(1)} custom-call(s32[2]{0:T(128)S(1)} %pad_add_fusion.1.scalars, bf16[256,512]{1,0:T(8,128)(2,1)S(1)} %collective-permute-done.7.left, bf16[256,512]{1,0:T(8,128)(2,1)S(1)} %shard_map.74.left.refs_0_, bf16[256,512]{1,0:T(8,128)(2,1)S(1)} %collective-permute-done.refs_1_, ...), custom_call_target="tpu_custom_call" | custom-call | tf_op jit(solution)/shard_map/pallas_call | solution.py:142
  53.4 3.2 %shard_map.79 = bf16[256,512]{1,0:T(8,128)(2,1)S(1)} custom-call(s32[2]{0:T(128)S(1)} %pad_add_fusion.3.scalars, bf16[256,512]{1,0:T(8,128)(2,1)S(1)} %collective-permute-done.11.left, bf16[256,512]{1,0:T(8,128)(2,1)S(1)} %shard_map.74.left.refs_0_, bf16[256,512]{1,0:T(8,128)(2,1)S(1)} %collective-permute-done.refs_1_, ...), custom_call_target="tpu_custom_call" | custom-call | tf_op jit(solution)/shard_map/pallas_call | solution.py:142
  56.9 5.3 %collective-permute-done.9.left = bf16[256,512]{1,0:T(8,128)(2,1)S(1)} collective-permute-done((bf16[256,512]{1,0:T(8,128)(2,1)S(1)}, bf16[256,512]{1,0:T(8,128)(2,1)S(1)}, u32[]{:S(2)}, u32[]{:S(2)}) %collective-permute-start.9) | collective-permute-done | bytes 262176 | tf_op jit(solution)/shard_map/ppermute | solution.py:250
  62.2 3.9 %shard_map.78 = bf16[256,512]{1,0:T(8,128)(2,1)} custom-call(s32[2]{0:T(128)S(1)} %pad_add_fusion.2.scalars, bf16[256,512]{1,0:T(8,128)(2,1)S(1)} %collective-permute-done.9.left, bf16[256,512]{1,0:T(8,128)(2,1)S(1)} %shard_map.74.left.refs_0_, bf16[256,512]{1,0:T(8,128)(2,1)S(1)} %collective-permute-done.refs_1_, ...), custom_call_target="tpu_custom_call" | custom-call | tf_op jit(solution)/shard_map/pallas_call | solution.py:142
  66.2 4.3 %collective-permute-start.10 = (bf16[256,512]{1,0:T(8,128)(2,1)}, bf16[256,512]{1,0:T(8,128)(2,1)S(1)}, u32[]{:S(2)}, u32[]{:S(2)}) collective-permute-start(bf16[256,512]{1,0:T(8,128)(2,1)} %shard_map.78), channel_id=1, source_target_pairs={{0,2},{1,3},{2,0},{3,1},{4,6},{5,7},{6,4},{7,5},{8,10},{9,11},{10,... | collective-permute-start | bytes 786440 | tf_op jit(solution)/shard_map/ppermute | solution.py:275
  70.4 3.2 %shard_map.77 = bf16[256,512]{1,0:T(8,128)(2,1)} custom-call(s32[2]{0:T(128)S(1)} %pad_add_fusion.1.scalars, bf16[256,512]{1,0:T(8,128)(2,1)S(1)} %collective-permute-done.7.left, bf16[256,512]{1,0:T(8,128)(2,1)S(1)} %collective-permute-done.3.refs_4_.refs_0_, bf16[256,512]{1,0:T(8,128)(2,1)S(1)} %collective-permute-done.4.refs_5_.refs_1_, ...), custom_call_target="tpu_custom_call" | custom-call | tf_op jit(solution)/shard_map/pallas_call | solution.py:142
  73.6 4.2 %collective-permute-start.8 = (bf16[256,512]{1,0:T(8,128)(2,1)}, bf16[256,512]{1,0:T(8,128)(2,1)}, u32[]{:S(2)}, u32[]{:S(2)}) collective-permute-start(bf16[256,512]{1,0:T(8,128)(2,1)} %shard_map.77), channel_id=1, source_target_pairs={{0,1},{1,2},{2,3},{3,0},{4,5},{5,6},{6,7},{7,4},{8,9},{9,10},{10,1... | collective-permute-start | bytes 786440 | tf_op jit(solution)/shard_map/ppermute | solution.py:275
  77.9 3.2 %shard_map.75.own = f32[256,512]{1,0:T(8,128)S(1)} custom-call(s32[2]{0:T(128)S(1)} %pad_add_fusion.scalars, bf16[256,512]{1,0:T(8,128)(2,1)S(1)} %shard_map.74.left.refs_0_, bf16[256,512]{1,0:T(8,128)(2,1)S(1)} %shard_map.74.left.refs_0_, bf16[256,512]{1,0:T(8,128)(2,1)S(1)} %collective-permute-done.refs_1_, ...), custom_call_target="tpu_custom_call" | custom-call | tf_op jit(solution)/shard_map/pallas_call | solution.py:142
  81.2 9.3 %all_to_all.21 = s32[32,1,32]{2,1,0:T(1,128)S(1)} all-to-all(s32[32,1,32]{2,1,0:T(1,128)S(1)} %all_to_all.14), channel_id=1, replica_groups=mesh['row'=8,'col'=4] {'row','col'}, dimensions={0} | all-to-all | bytes 8192 | tf_op jit(solution)/shard_map/all_to_all | solution.py:279
  90.6 1.5 %shard_map.80 = bf16[1024,512]{1,0:T(8,128)(2,1)S(1)} custom-call(s32[32,32]{1,0:T(8,128)S(1)} %bitcast.19, f32[256,512]{1,0:T(8,128)S(1)} %shard_map.75.own, bf16[256,512]{1,0:T(8,128)(2,1)} %collective-permute-done.8.refs_0_, bf16[256,512]{1,0:T(8,128)(2,1)S(1)} %collective-permute-done.10.refs_1_, bf16[256,512]{1,0:T(8,128)(2,1)S(1)} %collective-permute-done.12.refs_2_), custom_call_target="tpu_custom_call" | custom-call | tf_op jit(solution)/shard_map/pallas_call | solution.py:286
  92.1 30.5 %all_to_all.22 = bf16[32,32,512]{2,1,0:T(8,128)(2,1)S(1)} all-to-all(bf16[32,32,512]{2,1,0:T(8,128)(2,1)S(1)} %bitcast.17), channel_id=1, replica_groups=mesh['row'=8,'col'=4] {'row','col'}, dimensions={0} | all-to-all | bytes 2097152 | tf_op jit(solution)/shard_map/all_to_all | solution.py:293
  122.6 2.9 %shard_map.81 = f32[1024,512]{1,0:T(8,128)} custom-call(bf16[1024,1024]{1,0:T(8,128)(2,1)S(1)} %copy-done.1, bf16[1024,512]{1,0:T(8,128)(2,1)S(1)} %bitcast.16), custom_call_target="tpu_custom_call" | custom-call | tf_op jit(solution)/shard_map/pallas_call | solution.py:302
  (39 shorter events, 2.2 us)
Async XLA Ops:
  0.0 11.1 %copy-start.4 = (s32[32]{0:T(128)S(1)}, s32[32]{0:T(128)}, u32[]{:S(2)}) copy-start(s32[32]{0:T(128)} %counts.1) | copy-start | bytes 388
  0.0 11.4 %copy-start.2 = (s32[8192]{0:T(1024)S(1)}, s32[8192]{0:T(1024)}, u32[]{:S(2)}) copy-start(s32[8192]{0:T(1024)} %param.11) | copy-start | bytes 98308
  4.0 27.9 %all-to-all-start = ((bf16[32,24,512]{2,1,0:T(8,128)(2,1)}), bf16[32,24,512]{2,1,0:T(8,128)(2,1)S(1)}, u32[]{:S(2)}, u32[]{:S(2)}) async-start(bf16[32,24,512]{2,1,0:T(8,128)(2,1)} %bitcast.20), calls=%async_computation | async-start | bytes 1572864 | tf_op jit(solution)/shard_map/all_to_all | solution.py:221
  32.4 8.3 %collective-permute-start = (bf16[256,512]{1,0:T(8,128)(2,1)S(1)}, bf16[256,512]{1,0:T(8,128)(2,1)S(1)}, u32[]{:S(2)}, u32[]{:S(2)}) collective-permute-start(bf16[256,512]{1,0:T(8,128)(2,1)S(1)} %shard_map.74.left.refs_0_), channel_id=1, source_target_pairs={{0,8},{4,12},{8,0},{12,4},{16,24},{20,28},{24,16},{28,20},{1,9},{5... | collective-permute-start | bytes 786440 | tf_op jit(solution)/shard_map/ppermute | solution.py:253
  33.6 13.7 %collective-permute-start.1 = (bf16[256,512]{1,0:T(8,128)(2,1)S(1)}, bf16[256,512]{1,0:T(8,128)(2,1)S(1)}, u32[]{:S(2)}, u32[]{:S(2)}) collective-permute-start(bf16[256,512]{1,0:T(8,128)(2,1)S(1)} %shard_map.74.left.refs_0_), channel_id=1, source_target_pairs={{0,16},{4,20},{8,24},{12,28},{16,0},{20,4},{24,8},{28,12},{1,17},{... | collective-permute-start | bytes 786440 | tf_op jit(solution)/shard_map/ppermute | solution.py:253
  33.9 13.5 %collective-permute-start.2 = (bf16[256,512]{1,0:T(8,128)(2,1)S(1)}, bf16[256,512]{1,0:T(8,128)(2,1)S(1)}, u32[]{:S(2)}, u32[]{:S(2)}) collective-permute-start(bf16[256,512]{1,0:T(8,128)(2,1)S(1)} %shard_map.74.left.refs_0_), channel_id=1, source_target_pairs={{0,24},{4,28},{8,16},{12,20},{16,8},{20,12},{24,0},{28,4},{1,25},{... | collective-permute-start | bytes 786440 | tf_op jit(solution)/shard_map/ppermute | solution.py:253
  35.1 13.7 %collective-permute-start.3 = (bf16[256,512]{1,0:T(8,128)(2,1)S(1)}, bf16[256,512]{1,0:T(8,128)(2,1)S(1)}, u32[]{:S(2)}, u32[]{:S(2)}) collective-permute-start(bf16[256,512]{1,0:T(8,128)(2,1)S(1)} %shard_map.74.left.refs_0_), channel_id=1, source_target_pairs={{0,4},{4,0},{8,12},{12,8},{16,20},{20,16},{24,28},{28,24},{1,5},{5... | collective-permute-start | bytes 786440 | tf_op jit(solution)/shard_map/ppermute | solution.py:253
  35.1 13.8 %collective-permute-start.7 = (bf16[256,512]{1,0:T(8,128)(2,1)S(1)}, bf16[256,512]{1,0:T(8,128)(2,1)S(1)}, u32[]{:S(2)}, u32[]{:S(2)}) collective-permute-start(bf16[256,512]{1,0:T(8,128)(2,1)S(1)} %shard_map.74.left.refs_0_), channel_id=1, source_target_pairs={{1,0},{2,1},{3,2},{0,3},{5,4},{6,5},{7,6},{4,7},{9,8},{10,9},{11,1... | collective-permute-start | bytes 786440 | tf_op jit(solution)/shard_map/ppermute | solution.py:250
  40.7 12.6 %collective-permute-start.11 = (bf16[256,512]{1,0:T(8,128)(2,1)S(1)}, bf16[256,512]{1,0:T(8,128)(2,1)S(1)}, u32[]{:S(2)}, u32[]{:S(2)}) collective-permute-start(bf16[256,512]{1,0:T(8,128)(2,1)S(1)} %shard_map.74.left.refs_0_), channel_id=1, source_target_pairs={{3,0},{0,1},{1,2},{2,3},{7,4},{4,5},{5,6},{6,7},{11,8},{8,9},{9,10... | collective-permute-start | bytes 786440 | tf_op jit(solution)/shard_map/ppermute | solution.py:250
  47.4 14.9 %collective-permute-start.9 = (bf16[256,512]{1,0:T(8,128)(2,1)S(1)}, bf16[256,512]{1,0:T(8,128)(2,1)S(1)}, u32[]{:S(2)}, u32[]{:S(2)}) collective-permute-start(bf16[256,512]{1,0:T(8,128)(2,1)S(1)} %shard_map.74.left.refs_0_), channel_id=1, source_target_pairs={{2,0},{3,1},{0,2},{1,3},{6,4},{7,5},{4,6},{5,7},{10,8},{11,9},{8,1... | collective-permute-start | bytes 786440 | tf_op jit(solution)/shard_map/ppermute | solution.py:250
  47.4 6.0 %collective-permute-start.4 = (bf16[256,512]{1,0:T(8,128)(2,1)S(1)}, bf16[256,512]{1,0:T(8,128)(2,1)S(1)}, u32[]{:S(2)}, u32[]{:S(2)}) collective-permute-start(bf16[256,512]{1,0:T(8,128)(2,1)S(1)} %collective-permute-done.refs_1_), channel_id=1, source_target_pairs={{0,4},{4,0},{8,12},{12,8},{16,20},{20,16},{24,28},{28,24},{1,5},{5... | collective-permute-start | bytes 786440 | tf_op jit(solution)/shard_map/ppermute | solution.py:253
  48.8 4.6 %collective-permute-start.5 = (bf16[256,512]{1,0:T(8,128)(2,1)S(1)}, bf16[256,512]{1,0:T(8,128)(2,1)S(1)}, u32[]{:S(2)}, u32[]{:S(2)}) collective-permute-start(bf16[256,512]{1,0:T(8,128)(2,1)S(1)} %collective-permute-done.1.refs_2_), channel_id=1, source_target_pairs={{0,4},{4,0},{8,12},{12,8},{16,20},{20,16},{24,28},{28,24},{1,5},{5... | collective-permute-start | bytes 786440 | tf_op jit(solution)/shard_map/ppermute | solution.py:253
  48.9 4.5 %collective-permute-start.6 = (bf16[256,512]{1,0:T(8,128)(2,1)S(1)}, bf16[256,512]{1,0:T(8,128)(2,1)S(1)}, u32[]{:S(2)}, u32[]{:S(2)}) collective-permute-start(bf16[256,512]{1,0:T(8,128)(2,1)S(1)} %collective-permute-done.2.refs_3_), channel_id=1, source_target_pairs={{0,4},{4,0},{8,12},{12,8},{16,20},{20,16},{24,28},{28,24},{1,5},{5... | collective-permute-start | bytes 786440 | tf_op jit(solution)/shard_map/ppermute | solution.py:253
  49.6 2.2 %copy-start = (bf16[1024,2048]{1,0:T(8,128)(2,1)S(1)}, bf16[1024,2048]{1,0:T(8,128)(2,1)}, u32[]{:S(2)}) copy-start(bf16[1024,2048]{1,0:T(8,128)(2,1)} %refs_8_.5) | copy-start | bytes 12582916
  56.6 33.9 %collective-permute-start.12 = (bf16[256,512]{1,0:T(8,128)(2,1)S(1)}, bf16[256,512]{1,0:T(8,128)(2,1)S(1)}, u32[]{:S(2)}, u32[]{:S(2)}) collective-permute-start(bf16[256,512]{1,0:T(8,128)(2,1)S(1)} %shard_map.79), channel_id=1, source_target_pairs={{0,3},{1,0},{2,1},{3,2},{4,7},{5,4},{6,5},{7,6},{8,11},{9,8},{10,9... | collective-permute-start | bytes 786440 | tf_op jit(solution)/shard_map/ppermute | solution.py:275
  66.2 24.4 %collective-permute-start.10 = (bf16[256,512]{1,0:T(8,128)(2,1)}, bf16[256,512]{1,0:T(8,128)(2,1)S(1)}, u32[]{:S(2)}, u32[]{:S(2)}) collective-permute-start(bf16[256,512]{1,0:T(8,128)(2,1)} %shard_map.78), channel_id=1, source_target_pairs={{0,2},{1,3},{2,0},{3,1},{4,6},{5,7},{6,4},{7,5},{8,10},{9,11},{10,... | collective-permute-start | bytes 786440 | tf_op jit(solution)/shard_map/ppermute | solution.py:275
  73.6 7.6 %copy-start.3 = (s32[1,1024]{1,0:T(1,128)S(1)}, s32[1,1024]{1,0:T(1,128)}, u32[]{:S(2)}) copy-start(s32[1,1024]{1,0:T(1,128)} %param.13) | copy-start | bytes 12292
  73.6 17.0 %collective-permute-start.8 = (bf16[256,512]{1,0:T(8,128)(2,1)}, bf16[256,512]{1,0:T(8,128)(2,1)}, u32[]{:S(2)}, u32[]{:S(2)}) collective-permute-start(bf16[256,512]{1,0:T(8,128)(2,1)} %shard_map.77), channel_id=1, source_target_pairs={{0,1},{1,2},{2,3},{3,0},{4,5},{5,6},{6,7},{7,4},{8,9},{9,10},{10,1... | collective-permute-start | bytes 786440 | tf_op jit(solution)/shard_map/ppermute | solution.py:275
  81.1 41.5 %copy-start.1 = (bf16[1024,1024]{1,0:T(8,128)(2,1)S(1)}, bf16[1024,1024]{1,0:T(8,128)(2,1)}, u32[]{:S(2)}) copy-start(bf16[1024,1024]{1,0:T(8,128)(2,1)} %interp.1) | copy-start | bytes 6291460

commit v3 on v2

v3 whole, which is shorter than its diff:
```python
import functools

import jax
import jax.numpy as jnp
from jax import lax
from jax.experimental import pallas as pl
from jax.experimental.pallas import tpu as pltpu
from jax.sharding import PartitionSpec as P

NORB = 512
LIST = 1024
OWN = 256
SLOTS = 768
LANES = 128
VMEM_LIMIT = 48 * 1024 * 1024
PICK_LIMIT = 60 * 1024 * 1024


def vmem():
    return pl.BlockSpec(memory_space=pltpu.VMEM)


def smem():
    return pl.BlockSpec(memory_space=pltpu.SMEM)


def hbm():
    return pl.BlockSpec(memory_space=pltpu.HBM)


def params(limit=VMEM_LIMIT):
    return pltpu.CompilerParams(vmem_limit_bytes=limit)


def pick_kernel(
    box_total, capacity, scalars, counts, listed, owner_hbm, grid_hbm, orbitals_hbm, out,
    owner_map, grid_rows, orbitals, sems,
):
    copies = [
        pltpu.make_async_copy(source, target, sems.at[n])
        for n, (source, target) in enumerate(
            [(grid_hbm, grid_rows), (owner_hbm, owner_map), (orbitals_hbm, orbitals)]
        )
    ]
    for copy in copies:
        copy.start()
    targets = box_total * capacity
    my_box = scalars[0]
    start = jnp.int32(0)
    for b in range(box_total):
        start = start + jnp.where(b < my_box, counts[b], 0)
    stop = start + counts[my_box]
    first = start // LANES
    shift = start - first * LANES
    blocks = SLOTS // LANES + 1
    top = owner_map.shape[0] - 1
    lane = lax.broadcasted_iota(jnp.int32, (1, LANES), 1)
    copies[0].wait()
    copies[1].wait()
    turned = pltpu.roll(grid_rows[...], shift, 1)
    lane8 = lax.broadcasted_iota(jnp.int32, turned.shape, 1)
    lined = jnp.where(lane8 < shift, pltpu.roll(turned, 1, 0), turned)
    before = (
        lax.broadcasted_iota(jnp.int32, (LANES, LANES), 0)
        < lax.broadcasted_iota(jnp.int32, (LANES, LANES), 1)
    ).astype(jnp.bfloat16)
    owner_ids = lax.broadcasted_iota(jnp.int32, (box_total, LANES), 0)
    target_ids = lax.broadcasted_iota(jnp.int32, (targets, LANES), 0)
    base = jnp.zeros((box_total, 1), jnp.float32)
    found = jnp.zeros((targets, LANES), jnp.int32)
    for i in range(blocks):
        k = (first + i) * LANES + lane
        position = owner_map[pl.ds(jnp.minimum(first + i, top), 1), :]
        live = (k >= start) & (k < stop)
        owner = jnp.where(live, position // OWN, -1)
        member = (owner_ids == owner).astype(jnp.float32)
        inner = jnp.dot(member.astype(jnp.bfloat16), before, preferred_element_type=jnp.float32)
        rank = jnp.sum(member * (inner + base), axis=0, keepdims=True).astype(jnp.int32)
        base = base + jnp.sum(member, axis=1, keepdims=True)
        target = jnp.where(live, owner * capacity + rank, -1)
        found = found + jnp.where(target_ids == target, lined[i : i + 1, :] + 1, 0)
    source = jnp.sum(found.astype(jnp.float32), axis=1, keepdims=True).astype(jnp.int32) - 1
    per_owner = LIST // box_total
    fold = LANES // per_owner
    spread = jnp.broadcast_to(listed[...][:, None, :], (LIST // LANES, fold, LANES))
    spread = spread.reshape(box_total, LANES)
    phase = lax.broadcasted_iota(jnp.int32, spread.shape, 0) % fold
    indices = spread
    for q in range(1, fold):
        indices = jnp.where(phase == q, pltpu.roll(spread, LANES - q * per_owner, 1), indices)
    indices = indices.astype(jnp.float32).astype(jnp.bfloat16)
    tail = out.shape[1] - capacity * (NORB // LANES)
    out[:, capacity * (NORB // LANES) :, :] = jnp.broadcast_to(
        indices[:, None, :], (box_total, tail, LANES)
    )
    box = orbitals.shape[0]
    step = targets // 4
    copies[2].wait()
    for t in range(0, targets, step):
        hot = source[t : t + step] == lax.broadcasted_iota(jnp.int32, (step, box), 1)
        rows = jnp.dot(
            hot.astype(jnp.float32).astype(jnp.bfloat16),
            orbitals[...],
            preferred_element_type=jnp.float32,
        ).astype(jnp.bfloat16)
        first_owner = t // capacity
        for c in range(NORB // LANES):
            out[
                first_owner : first_owner + step // capacity, c * capacity : (c + 1) * capacity, :
            ] = rows[:, c * LANES : (c + 1) * LANES].reshape(step // capacity, capacity, LANES)


def place_kernel(capacity, index, received, out, wanted):
    boxes = received.shape[0]
    rows = jnp.concatenate(
        [
            received[:, c * capacity : (c + 1) * capacity, :].reshape(boxes * capacity, LANES)
            for c in range(NORB // LANES)
        ],
        axis=1,
    )
    hot = index[...] == lax.broadcasted_iota(jnp.int32, (index.shape[0], rows.shape[0]), 1)
    out[...] = jnp.dot(
        hot.astype(jnp.float32).astype(jnp.bfloat16), rows, preferred_element_type=jnp.float32
    ).astype(jnp.bfloat16)
    tail = received[:, capacity * (NORB // LANES) :, :].astype(jnp.float32)
    wanted[...] = tail[:, 0, :].astype(jnp.int32)


def join_kernel(*refs):
    out, at = refs[-1], 0
    for ref in refs[:-1]:
        out[at : at + ref.shape[0], :] = ref[...]
        at += ref.shape[0]


def hold_kernel(*refs):
    count = len(refs) // 2
    for source, target in zip(refs[:count], refs[count:]):
        target[...] = source[...]


def pair_block(left, right):
    return lax.dot_general(
        left, right, (((1,), (1,)), ((), ())), preferred_element_type=jnp.float32
    ).astype(jnp.bfloat16)


def order_kernel(scalars, even, odd, out):
    for parity, ref in enumerate((even, odd)):
        for n in range(ref.shape[0] // OWN):
            place = jnp.bitwise_xor(scalars[0], 2 * n + parity) * OWN
            out[pl.ds(pl.multiple_of(place, OWN), OWN), :] = ref[n * OWN : (n + 1) * OWN, :]


def block_kernel(scalars, left, right, coulomb, out, tile, weighted, sem):
    source = pl.ds(pl.multiple_of(scalars[1] * OWN, OWN), OWN)
    copy = pltpu.make_async_copy(coulomb.at[source, :], tile, sem)
    copy.start()
    step = 512
    for t in range(0, right.shape[0], step):
        weighted[:, t : t + step] = pair_block(left[...], right[t : t + step, :])
    copy.wait()
    for t in range(0, right.shape[0], step):
        pair = weighted[:, t : t + step].astype(jnp.float32)
        weighted[:, t : t + step] = (
            pair * tile[:, t : t + step].astype(jnp.float32)
        ).astype(jnp.bfloat16)
    out[...] = jnp.dot(
        weighted[...], right[...], preferred_element_type=jnp.float32
    ).astype(out.dtype)


def block_sum(numbers, left, right, coulomb, dtype):
    columns = right.shape[0]
    return local(
        block_kernel,
        jax.ShapeDtypeStruct((OWN, NORB), dtype),
        numbers,
        left,
        right,
        coulomb,
        flops=4 * OWN * columns * NORB,
        far=3,
        scratch=[
            pltpu.VMEM((OWN, columns), jnp.bfloat16),
            pltpu.VMEM((OWN, columns), jnp.bfloat16),
            pltpu.SemaphoreType.DMA,
        ],
    )


def local(kernel, out, *args, flops=0, far=None, scratch=()):
    def spec(n, a):
        if n == far:
            return hbm()
        return smem() if a.ndim == 1 else vmem()

    return pl.pallas_call(
        kernel,
        out_shape=out,
        in_specs=[spec(n, a) for n, a in enumerate(args)],
        out_specs=jax.tree.map(lambda _: vmem(), out),
        scratch_shapes=scratch,
        compiler_params=params(),
        cost_estimate=pl.CostEstimate(flops=flops, bytes_accessed=0, transcendentals=0),
    )(*args)


def select_kernel(others, per_owner, index, own, *refs):
    boxes = index.shape[0]
    spread = jnp.broadcast_to(index[...][:, None, :], (boxes, per_owner, LANES))
    diagonal = lax.broadcasted_iota(jnp.int32, spread.shape, 1) == lax.broadcasted_iota(
        jnp.int32, spread.shape, 2
    )
    picks = jnp.sum(jnp.where(diagonal, spread, 0).astype(jnp.float32), axis=2, keepdims=True)
    picks = picks.reshape(boxes * per_owner, 1).astype(jnp.int32)
    out = refs[-1]
    totals, rows = [], refs[0].shape[0]
    for n in range(OWN // rows):
        total = own[n * rows : (n + 1) * rows, :]
        for ref in refs[n * others : (n + 1) * others]:
            total = total + ref[...].astype(jnp.float32)
        totals.append(total.astype(jnp.bfloat16))
    projected = jnp.concatenate(totals)
    hot = picks == lax.broadcasted_iota(jnp.int32, (boxes * per_owner, OWN), 1)
    out[...] = jnp.dot(
        hot.astype(jnp.float32).astype(jnp.bfloat16), projected, preferred_element_type=jnp.float32
    ).astype(jnp.bfloat16)


def apply_kernel(interp, chosen, out):
    out[...] = -jnp.dot(interp[...], chosen[...], preferred_element_type=jnp.float32)


def shards(orbitals, coulomb, interp, box_counts, owner_map, grid_rows, listed):
    row_count = lax.axis_size("row")
    col_count = lax.axis_size("col")
    box_total = row_count * col_count
    point_total = OWN * box_total
    capacity = (SLOTS + box_total - 1) // box_total
    per_owner = LIST // box_total
    my_row, my_col = lax.axis_index("row"), lax.axis_index("col")
    my_box = my_row * col_count + my_col
    packed = capacity * (NORB // LANES)
    packed = (packed // 8 + 1) * 8
    outgoing = pl.pallas_call(
        functools.partial(pick_kernel, box_total, capacity),
        out_shape=jax.ShapeDtypeStruct((box_total, packed, LANES), jnp.bfloat16),
        in_specs=[smem(), smem(), vmem(), hbm(), hbm(), hbm()],
        out_specs=vmem(),
        scratch_shapes=[
            pltpu.VMEM((point_total // LANES, LANES), jnp.int32),
            pltpu.VMEM((grid_rows.shape[1] // LANES, LANES), jnp.int32),
            pltpu.VMEM(orbitals.shape, jnp.bfloat16),
            pltpu.SemaphoreType.DMA((3,)),
        ],
        compiler_params=params(PICK_LIMIT),
        cost_estimate=pl.CostEstimate(
            flops=2 * SLOTS * LIST * NORB, bytes_accessed=2 << 20, transcendentals=0
        ),
    )(
        my_box.reshape(1).astype(jnp.int32),
        box_counts,
        listed.reshape(LIST // LANES, LANES),
        owner_map.reshape(point_total // LANES, LANES),
        grid_rows.reshape(grid_rows.shape[1] // LANES, LANES),
        orbitals,
    )
    received = lax.all_to_all(
        outgoing, ("row", "col"), split_axis=0, concat_axis=0, tiled=True
    )

    wanted_pos = my_box * OWN + jnp.arange(OWN, dtype=jnp.int32)
    all_listing = jnp.arange(point_total, dtype=jnp.int32)
    my_points = jnp.sum(
        jnp.where(owner_map[None, :] == wanted_pos[:, None], all_listing[None, :], 0), axis=1
    )
    box_ends = jnp.cumsum(box_counts)
    source = jnp.sum((my_points[:, None] >= box_ends[None, :]).astype(jnp.int32), axis=1)
    earlier = (source[:, None] == source[None, :]) & (my_points[None, :] < my_points[:, None])
    source_rank = jnp.sum(earlier.astype(jnp.int32), axis=1)
    index = (source * capacity + source_rank).reshape(OWN, 1)
    owned_rows, wanted = pl.pallas_call(
        functools.partial(place_kernel, capacity),
        out_shape=(
            jax.ShapeDtypeStruct((OWN, NORB), jnp.bfloat16),
            jax.ShapeDtypeStruct((box_total, LANES), jnp.int32),
        ),
        in_specs=[vmem(), vmem()],
        out_specs=(vmem(), vmem()),
        compiler_params=params(),
    )(index, received)

    def swap(rows, mask):
        return lax.ppermute(rows, "col", [(i, i ^ mask) for i in range(col_count)])

    def flip(rows, mask):
        return lax.ppermute(rows, "row", [(i, i ^ mask) for i in range(row_count)])

    left = {0: owned_rows}
    for mask in range(1, col_count):
        if mask & (mask - 1) == 0:
            left[mask] = swap(owned_rows, mask)

    blocks = {0: [owned_rows]}
    whole = {0: owned_rows}
    half = OWN // 2
    for mask in range(2, row_count, 2):
        bits = [1 << b for b in range(1, mask.bit_length()) if mask >> b & 1]
        if len(bits) == 1:
            blocks[mask] = [flip(owned_rows, mask)]
        else:
            low, high = bits[0], bits[-1]
            blocks[mask] = [
                flip(whole[mask ^ high][:half], high),
                flip(whole[mask ^ low][half:], low),
            ]
        whole[mask] = jnp.concatenate(blocks[mask])
    pieces = [piece for mask in range(0, row_count, 2) for piece in blocks[mask]]
    shape = jax.ShapeDtypeStruct
    even = local(join_kernel, shape((row_count // 2 * OWN, NORB), jnp.bfloat16), *pieces)
    odd = flip(even, 1)
    direct = [mask for mask in left if mask]
    held = local(
        hold_kernel,
        tuple(shape(owned_rows.shape, owned_rows.dtype) for _ in direct),
        *[left[mask] for mask in direct],
        flops=20 * 10**9,
    )
    *held, odd = lax.optimization_barrier((*held, odd))
    left.update(zip(direct, held))
    for mask in range(1, col_count):
        if mask not in left:
            low = mask & -mask
            left[mask] = swap(left[mask ^ low], low)

    def numbers(mask):
        return jnp.stack([my_row, jnp.bitwise_xor(my_col, mask)]).astype(jnp.int32)

    right = local(
        order_kernel, shape((row_count * OWN, NORB), jnp.bfloat16), numbers(0), even, odd
    )

    def partial_sum(mask, dtype):
        return block_sum(numbers(mask), left[mask], right, coulomb, dtype)

    arrived = []
    for mask in sorted(range(1, col_count), key=lambda m: (m & 1, m)):
        arrived.append(swap(partial_sum(mask, jnp.bfloat16), mask))
    own_sum = partial_sum(0, jnp.float32)
    picked = pl.pallas_call(
        functools.partial(select_kernel, col_count - 1, per_owner),
        out_shape=jax.ShapeDtypeStruct((LIST, NORB), jnp.bfloat16),
        in_specs=[vmem()] * (2 + len(arrived)),
        out_specs=vmem(),
        compiler_params=params(),
    )(wanted, own_sum, *arrived)
    chosen = lax.all_to_all(
        picked.reshape(box_total, per_owner, NORB),
        ("row", "col"),
        split_axis=0,
        concat_axis=0,
        tiled=True,
    ).reshape(LIST, NORB)
    box = interp.shape[0]
    step = 256
    return pl.pallas_call(
        apply_kernel,
        grid=(box // step,),
        out_shape=jax.ShapeDtypeStruct((box, NORB), jnp.float32),
        in_specs=[
            pl.BlockSpec((step, LIST), lambda i: (i, 0)),
            pl.BlockSpec((LIST, NORB), lambda i: (0, 0)),
        ],
        out_specs=pl.BlockSpec((step, NORB), lambda i: (i, 0)),
        compiler_params=params(),
    )(interp, chosen)


def solution(mesh):
    return jax.shard_map(
        shards,
        mesh=mesh,
        in_specs=(
            P(("row", "col"), None),
            P("row", "col"),
            P(("row", "col"), None),
            P(),
            P(),
            P(("row", "col"), None),
            P(("row", "col"), None),
        ),
        out_specs=P(("row", "col"), None),
        check_vma=False,
    )
```

time: 126 us -> 114 us (0.905)
  waiting for transfers between devices: 33.8 us -> 43.3 us
  starting transfers between devices: 23.2 us -> 14.7 us
  blocking collectives: 39.9 us -> 34 us
  Pallas kernels: 24 us -> 18.8 us
  local copies, waits for them, and re-layouts: 2.52 us -> 0.26 us
    all_to_all x1 -> x0, blocking collectives: 9.31 us -> none  [shards(): lax.all_to_all(asked.reshape(box_total, per_owner), ('row', 'col'), split...]
    ppermute x6, starting transfers between devices: 11.4 us -> 3.48 us  [swap(): return lax.ppermute(rows, 'col', [(i, i ^ mask) for i in range(col_count)])]
    ppermute x6, waiting for transfers between devices: 5.36 us -> 10.7 us  [swap(): return lax.ppermute(rows, 'col', [(i, i ^ mask) for i in range(col_count)])]
    pallas_call x7 -> x9, Pallas kernels: 17 us -> 11.9 us  [the longest x7 10.9 us: local(): pl.pallas_call(kernel, out_shape=out, in_specs=[spec(n, a) for n, a in en...]
    all_to_all x1, blocking collectives: 30.5 us -> 34 us  [shards(): lax.all_to_all(picked.reshape(box_total, per_owner, NORB), ('row', 'col')...]
    ppermute x7 -> x5, waiting for transfers between devices: 9.57 us -> 12.3 us  [flip(): return lax.ppermute(rows, 'row', [(i, i ^ mask) for i in range(row_count)])]
    unnamed x10 -> x6, local copies, waits for them, and re-layouts: 2.21 us -> 0.01 us
    all_to_all x1, waiting for transfers between devices: 18.8 us -> 20.2 us  [shards(): lax.all_to_all(outgoing, ('row', 'col'), split_axis=0, concat_axis=0, til...]
  transfers between devices with their start and end apart: 14 -> 12, of which waited for: 4 -> 9; matrix products, arithmetic and copies ran while one was open for 2% -> 2% of each run, Pallas kernels for 12% -> 10%
where the time goes in v3:
time: 114 us; the launch traced here: 113 us
  waiting for transfers between devices  43.3 us (38%)
  blocking collectives  34 us (30%)
  Pallas kernels  18.8 us (16%)
  starting transfers between devices  14.7 us (13%)
  other arithmetic  2.03 us (2%)
    all_to_all x1, blocking collectives, shards(): lax.all_to_all(picked.reshape(box_total, per_owner, NORB), ('row', 'col')...  34 us
    all_to_all x1, waiting for transfers between devices, shards(): lax.all_to_all(outgoing, ('row', 'col'), split_axis=0, concat_axis=0, til...  20.2 us
    ppermute x5, waiting for transfers between devices, flip(): return lax.ppermute(rows, 'row', [(i, i ^ mask) for i in range(row_count)])  12.3 us
    pallas_call x7, Pallas kernels, local(): pl.pallas_call(kernel, out_shape=out, in_specs=[spec(n, a) for n, a in en...  10.9 us
    ppermute x6, waiting for transfers between devices, swap(): return lax.ppermute(rows, 'col', [(i, i ^ mask) for i in range(col_count)])  10.7 us
    all_to_all x1, starting transfers between devices, shards(): lax.all_to_all(outgoing, ('row', 'col'), split_axis=0, concat_axis=0, til...  7.1 us
    ppermute x5, starting transfers between devices, flip(): return lax.ppermute(rows, 'row', [(i, i ^ mask) for i in range(row_count)])  4.17 us
    pallas_call x1, Pallas kernels, shards(): pl.pallas_call(functools.partial(pick_kernel, box_total, capacity), out_s...  4.07 us
  transfers between devices with their start and end apart: 12, of which 9 were waited for; matrix products, arithmetic and copies ran while one was open for 2% of the time, Pallas kernels for 10%

profile of v3, /device:TPU:1, one launch (start us, length us, event | category | flops | bytes accessed | tf_op | source)
XLA Modules:
  0.0 113.3 jit_solution(5219604238798544106)
XLA Ops:
  0.0 4.1 %shard_map.73 = bf16[32,104,128]{2,1,0:T(8,128)(2,1)} custom-call(s32[1]{0:T(128)} %bitcast.2.scalars, s32[32]{0:T(128)} %counts.1, s32[8,128]{1,0:T(8,128)} %bitcast.18, s32[64,128]{1,0:T(8,128)} %bitcast.15, s32[8,128]{1,0:T(8,128)} %bitcast.19, bf16[1024,512]{1,0:T(8,128)(2,1)} %orbitals_hbm.1), custom_call_target="tpu_custom_call" | custom-call | flops 805306368 | bytes 2097152 | tf_op jit(solution)/shard_map/pallas_call | solution.py:247
  4.1 7.1 %all-to-all-start = ((bf16[32,104,128]{2,1,0:T(8,128)(2,1)}), bf16[32,104,128]{2,1,0:T(8,128)(2,1)S(1)}, u32[]{:S(2)}, u32[]{:S(2)}) async-start(bf16[32,104,128]{2,1,0:T(8,128)(2,1)} %shard_map.73), calls=%async_computation | async-start | bytes 1703936 | tf_op jit(solution)/shard_map/all_to_all | solution.py:270
  11.5 1.2 %select_reduce_fusion = s32[256]{0:T(256)S(1)} fusion(s32[8192]{0:T(1024)S(1)} %copy-done.1, s32[256]{0:T(256)S(1)} %iota_add_fusion), kind=kLoop, calls=%fused_computation | loop fusion | flops 6291200 | bytes 34816 | tf_op jit(solution)/shard_map/reduce_sum | solution.py:276
  13.2 20.2 %all-to-all-done.received = bf16[32,104,128]{2,1,0:T(8,128)(2,1)S(1)} async-done(((bf16[32,104,128]{2,1,0:T(8,128)(2,1)}), bf16[32,104,128]{2,1,0:T(8,128)(2,1)S(1)}, u32[]{:S(2)}, u32[]{:S(2)}) %all-to-all-start) | async-done | bytes 852000 | tf_op jit(solution)/shard_map/all_to_all | solution.py:270
  33.8 1.3 %collective-permute-start = (bf16[256,512]{1,0:T(8,128)(2,1)S(1)}, bf16[256,512]{1,0:T(8,128)(2,1)S(1)}, u32[]{:S(2)}, u32[]{:S(2)}) collective-permute-start(bf16[256,512]{1,0:T(8,128)(2,1)S(1)} %get-tuple-element.13.refs_0_.left), channel_id=1, source_target_pairs={{0,8},{4,12},{8,0},{12,4},{16,24},{20,28},{24,16},{28,20},{1,9},{5... | collective-permute-start | bytes 786440 | tf_op jit(solution)/shard_map/ppermute | solution.py:299
  36.3 5.4 %collective-permute-done.refs_1_ = bf16[256,512]{1,0:T(8,128)(2,1)S(1)} collective-permute-done((bf16[256,512]{1,0:T(8,128)(2,1)S(1)}, bf16[256,512]{1,0:T(8,128)(2,1)S(1)}, u32[]{:S(2)}, u32[]{:S(2)}) %collective-permute-start) | collective-permute-done | bytes 262176 | tf_op jit(solution)/shard_map/ppermute | solution.py:299
  41.7 1.3 %collective-permute-start.2 = (bf16[128,512]{1,0:T(8,128)(2,1)S(1)}, bf16[128,512]{1,0:T(8,128)(2,1)S(1)}, u32[]{:S(2)}, u32[]{:S(2)}) collective-permute-start(bf16[128,512]{1,0:T(8,128)(2,1)S(1)} %slice.8), channel_id=1, source_target_pairs={{0,16},{4,20},{8,24},{12,28},{16,0},{20,4},{24,8},{28,12},{1,17},{... | collective-permute-start | bytes 393224 | tf_op jit(solution)/shard_map/ppermute | solution.py:299
  43.7 3.3 %collective-permute-done.2.refs_3_ = bf16[128,512]{1,0:T(8,128)(2,1)S(1)} collective-permute-done((bf16[128,512]{1,0:T(8,128)(2,1)S(1)}, bf16[128,512]{1,0:T(8,128)(2,1)S(1)}, u32[]{:S(2)}, u32[]{:S(2)}) %collective-permute-start.2) | collective-permute-done | bytes 131104 | tf_op jit(solution)/shard_map/ppermute | solution.py:299
  47.0 1.2 %collective-permute-done.3.refs_4_ = bf16[128,512]{1,0:T(8,128)(2,1)S(1)} collective-permute-done((bf16[128,512]{1,0:T(8,128)(2,1)S(1)}, bf16[128,512]{1,0:T(8,128)(2,1)S(1)}, u32[]{:S(2)}, u32[]{:S(2)}) %collective-permute-start.3) | collective-permute-done | bytes 131104 | tf_op jit(solution)/shard_map/ppermute | solution.py:299
  48.3 1.0 collective-permute-start.6
  49.4 2.2 %collective-permute-done.6.odd = bf16[1024,512]{1,0:T(8,128)(2,1)S(1)} collective-permute-done((bf16[1024,512]{1,0:T(8,128)(2,1)S(1)}, bf16[1024,512]{1,0:T(8,128)(2,1)S(1)}, u32[]{:S(2)}, u32[]{:S(2)}) %collective-permute-start.6) | collective-permute-done | bytes 1048608 | tf_op jit(solution)/shard_map/ppermute | solution.py:299
  51.7 0.7 shard_map.77.right
  52.4 2.5 %shard_map.79 = bf16[256,512]{1,0:T(8,128)(2,1)S(1)} custom-call(s32[2]{0:T(128)S(1)} %pad_add_fusion.1.scalars, bf16[256,512]{1,0:T(8,128)(2,1)S(1)} %get-tuple-element.17.left, bf16[2048,512]{1,0:T(8,128)(2,1)S(1)} %shard_map.77.right, bf16[1024,2048]{1,0:T(8,128)(2,1)} %coulomb.7), custom_call_target="tpu_custom_call" | custom-call | flops 1073741824 | tf_op jit(solution)/shard_map/pallas_call | solution.py:199
  54.9 1.0 collective-permute-start.7
  55.9 2.5 %shard_map.80 = bf16[256,512]{1,0:T(8,128)(2,1)S(1)} custom-call(s32[2]{0:T(128)S(1)} %pad_add_fusion.2.scalars, bf16[256,512]{1,0:T(8,128)(2,1)S(1)} %get-tuple-element.18.left, bf16[2048,512]{1,0:T(8,128)(2,1)S(1)} %shard_map.77.right, bf16[1024,2048]{1,0:T(8,128)(2,1)} %coulomb.7), custom_call_target="tpu_custom_call" | custom-call | flops 1073741824 | tf_op jit(solution)/shard_map/pallas_call | solution.py:199
  58.4 0.9 collective-permute-start.8
  59.3 1.2 %collective-permute-done.9.left = bf16[256,512]{1,0:T(8,128)(2,1)S(1)} collective-permute-done((bf16[256,512]{1,0:T(8,128)(2,1)S(1)}, bf16[256,512]{1,0:T(8,128)(2,1)S(1)}, u32[]{:S(2)}, u32[]{:S(2)}) %collective-permute-start.9) | collective-permute-done | bytes 262176 | tf_op jit(solution)/shard_map/ppermute | solution.py:296
  60.5 2.5 %shard_map.81 = bf16[256,512]{1,0:T(8,128)(2,1)S(1)} custom-call(s32[2]{0:T(128)S(1)} %pad_add_fusion.3.scalars, bf16[256,512]{1,0:T(8,128)(2,1)S(1)} %collective-permute-done.9.left, bf16[2048,512]{1,0:T(8,128)(2,1)S(1)} %shard_map.77.right, bf16[1024,2048]{1,0:T(8,128)(2,1)} %coulomb.7), custom_call_target="tpu_custom_call" | custom-call | flops 1073741824 | tf_op jit(solution)/shard_map/pallas_call | solution.py:199
  63.0 0.7 collective-permute-start.10
  63.8 2.6 %shard_map.78.own = f32[256,512]{1,0:T(8,128)S(1)} custom-call(s32[2]{0:T(128)S(1)} %pad_add_fusion.scalars, bf16[256,512]{1,0:T(8,128)(2,1)S(1)} %get-tuple-element.13.refs_0_.left, bf16[2048,512]{1,0:T(8,128)(2,1)S(1)} %shard_map.77.right, bf16[1024,2048]{1,0:T(8,128)(2,1)} %coulomb.7), custom_call_target="tpu_custom_call" | custom-call | flops 1073741824 | tf_op jit(solution)/shard_map/pallas_call | solution.py:199
  66.3 2.5 %collective-permute-done.7.refs_0_ = bf16[256,512]{1,0:T(8,128)(2,1)S(1)} collective-permute-done((bf16[256,512]{1,0:T(8,128)(2,1)S(1)}, bf16[256,512]{1,0:T(8,128)(2,1)S(1)}, u32[]{:S(2)}, u32[]{:S(2)}) %collective-permute-start.7) | collective-permute-done | bytes 262176 | tf_op jit(solution)/shard_map/ppermute | solution.py:296
  68.8 7.0 %collective-permute-done.10.refs_2_ = bf16[256,512]{1,0:T(8,128)(2,1)S(1)} collective-permute-done((bf16[256,512]{1,0:T(8,128)(2,1)S(1)}, bf16[256,512]{1,0:T(8,128)(2,1)S(1)}, u32[]{:S(2)}, u32[]{:S(2)}) %collective-permute-start.10) | collective-permute-done | bytes 262176 | tf_op jit(solution)/shard_map/ppermute | solution.py:296
  76.4 34.0 %all_to_all.10 = bf16[32,32,512]{2,1,0:T(8,128)(2,1)S(1)} all-to-all(bf16[32,32,512]{2,1,0:T(8,128)(2,1)S(1)} %bitcast.14), channel_id=1, replica_groups=mesh['row'=8,'col'=4] {'row','col'}, dimensions={0} | all-to-all | bytes 2097152 | tf_op jit(solution)/shard_map/all_to_all | solution.py:359
  110.4 2.9 %shard_map.83 = f32[1024,512]{1,0:T(8,128)} custom-call(bf16[1024,1024]{1,0:T(8,128)(2,1)S(1)} %copy-done, bf16[1024,512]{1,0:T(8,128)(2,1)S(1)} %bitcast.13), custom_call_target="tpu_custom_call" | custom-call | tf_op jit(solution)/shard_map/pallas_call | solution.py:368
  (33 shorter events, 3.8 us)
Async XLA Ops:
  0.0 11.2 %copy-start.2 = (s32[32]{0:T(128)S(1)}, s32[32]{0:T(128)}, u32[]{:S(2)}) copy-start(s32[32]{0:T(128)} %counts.1) | copy-start | bytes 388
  0.0 11.5 %copy-start.1 = (s32[8192]{0:T(1024)S(1)}, s32[8192]{0:T(1024)}, u32[]{:S(2)}) copy-start(s32[8192]{0:T(1024)} %param.11) | copy-start | bytes 98308
  4.1 29.3 %all-to-all-start = ((bf16[32,104,128]{2,1,0:T(8,128)(2,1)}), bf16[32,104,128]{2,1,0:T(8,128)(2,1)S(1)}, u32[]{:S(2)}, u32[]{:S(2)}) async-start(bf16[32,104,128]{2,1,0:T(8,128)(2,1)} %shard_map.73), calls=%async_computation | async-start | bytes 1703936 | tf_op jit(solution)/shard_map/all_to_all | solution.py:270
  33.8 7.9 %collective-permute-start = (bf16[256,512]{1,0:T(8,128)(2,1)S(1)}, bf16[256,512]{1,0:T(8,128)(2,1)S(1)}, u32[]{:S(2)}, u32[]{:S(2)}) collective-permute-start(bf16[256,512]{1,0:T(8,128)(2,1)S(1)} %get-tuple-element.13.refs_0_.left), channel_id=1, source_target_pairs={{0,8},{4,12},{8,0},{12,4},{16,24},{20,28},{24,16},{28,20},{1,9},{5... | collective-permute-start | bytes 786440 | tf_op jit(solution)/shard_map/ppermute | solution.py:299
  35.1 8.1 %collective-permute-start.1 = (bf16[256,512]{1,0:T(8,128)(2,1)S(1)}, bf16[256,512]{1,0:T(8,128)(2,1)S(1)}, u32[]{:S(2)}, u32[]{:S(2)}) collective-permute-start(bf16[256,512]{1,0:T(8,128)(2,1)S(1)} %get-tuple-element.13.refs_0_.left), channel_id=1, source_target_pairs={{0,16},{4,20},{8,24},{12,28},{16,0},{20,4},{24,8},{28,12},{1,17},{... | collective-permute-start | bytes 786440 | tf_op jit(solution)/shard_map/ppermute | solution.py:299
  35.4 13.9 %collective-permute-start.4 = (bf16[256,512]{1,0:T(8,128)(2,1)S(1)}, bf16[256,512]{1,0:T(8,128)(2,1)S(1)}, u32[]{:S(2)}, u32[]{:S(2)}) collective-permute-start(bf16[256,512]{1,0:T(8,128)(2,1)S(1)} %get-tuple-element.13.refs_0_.left), channel_id=1, source_target_pairs={{0,1},{1,0},{2,3},{3,2},{4,5},{5,4},{6,7},{7,6},{8,9},{9,8},{10,11... | collective-permute-start | bytes 786440 | tf_op jit(solution)/shard_map/ppermute | solution.py:296
  36.0 13.3 %collective-permute-start.5 = (bf16[256,512]{1,0:T(8,128)(2,1)S(1)}, bf16[256,512]{1,0:T(8,128)(2,1)S(1)}, u32[]{:S(2)}, u32[]{:S(2)}) collective-permute-start(bf16[256,512]{1,0:T(8,128)(2,1)S(1)} %get-tuple-element.13.refs_0_.left), channel_id=1, source_target_pairs={{0,2},{1,3},{2,0},{3,1},{4,6},{5,7},{6,4},{7,5},{8,10},{9,11},{10,... | collective-permute-start | bytes 786440 | tf_op jit(solution)/shard_map/ppermute | solution.py:296
  41.7 5.3 %collective-permute-start.2 = (bf16[128,512]{1,0:T(8,128)(2,1)S(1)}, bf16[128,512]{1,0:T(8,128)(2,1)S(1)}, u32[]{:S(2)}, u32[]{:S(2)}) collective-permute-start(bf16[128,512]{1,0:T(8,128)(2,1)S(1)} %slice.8), channel_id=1, source_target_pairs={{0,16},{4,20},{8,24},{12,28},{16,0},{20,4},{24,8},{28,12},{1,17},{... | collective-permute-start | bytes 393224 | tf_op jit(solution)/shard_map/ppermute | solution.py:299
  43.2 5.0 %collective-permute-start.3 = (bf16[128,512]{1,0:T(8,128)(2,1)S(1)}, bf16[128,512]{1,0:T(8,128)(2,1)S(1)}, u32[]{:S(2)}, u32[]{:S(2)}) collective-permute-start(bf16[128,512]{1,0:T(8,128)(2,1)S(1)} %slice.9), channel_id=1, source_target_pairs={{0,8},{4,12},{8,0},{12,4},{16,24},{20,28},{24,16},{28,20},{1,9},{5... | collective-permute-start | bytes 393224 | tf_op jit(solution)/shard_map/ppermute | solution.py:299
  48.3 3.3 %collective-permute-start.6 = (bf16[1024,512]{1,0:T(8,128)(2,1)S(1)}, bf16[1024,512]{1,0:T(8,128)(2,1)S(1)}, u32[]{:S(2)}, u32[]{:S(2)}) collective-permute-start(bf16[1024,512]{1,0:T(8,128)(2,1)S(1)} %shard_map.75.even), channel_id=1, source_target_pairs={{0,4},{4,0},{8,12},{12,8},{16,20},{20,16},{24,28},{28,24},{1,5},{5... | collective-permute-start | bytes 3145736 | tf_op jit(solution)/shard_map/ppermute | solution.py:299
  51.6 8.9 %collective-permute-start.9 = (bf16[256,512]{1,0:T(8,128)(2,1)S(1)}, bf16[256,512]{1,0:T(8,128)(2,1)S(1)}, u32[]{:S(2)}, u32[]{:S(2)}) collective-permute-start(bf16[256,512]{1,0:T(8,128)(2,1)S(1)} %get-tuple-element.17.left), channel_id=1, source_target_pairs={{0,1},{1,0},{2,3},{3,2},{4,5},{5,4},{6,7},{7,6},{8,9},{9,8},{10,11... | collective-permute-start | bytes 786440 | tf_op jit(solution)/shard_map/ppermute | solution.py:296
  54.9 13.9 %collective-permute-start.7 = (bf16[256,512]{1,0:T(8,128)(2,1)S(1)}, bf16[256,512]{1,0:T(8,128)(2,1)S(1)}, u32[]{:S(2)}, u32[]{:S(2)}) collective-permute-start(bf16[256,512]{1,0:T(8,128)(2,1)S(1)} %shard_map.79), channel_id=1, source_target_pairs={{0,2},{1,3},{2,0},{3,1},{4,6},{5,7},{6,4},{7,5},{8,10},{9,11},{10,... | collective-permute-start | bytes 786440 | tf_op jit(solution)/shard_map/ppermute | solution.py:296
  58.4 10.4 %collective-permute-start.8 = (bf16[256,512]{1,0:T(8,128)(2,1)S(1)}, bf16[256,512]{1,0:T(8,128)(2,1)S(1)}, u32[]{:S(2)}, u32[]{:S(2)}) collective-permute-start(bf16[256,512]{1,0:T(8,128)(2,1)S(1)} %shard_map.80), channel_id=1, source_target_pairs={{0,1},{1,0},{2,3},{3,2},{4,5},{5,4},{6,7},{7,6},{8,9},{9,8},{10,11... | collective-permute-start | bytes 786440 | tf_op jit(solution)/shard_map/ppermute | solution.py:296
  63.0 47.3 %copy-start = (bf16[1024,1024]{1,0:T(8,128)(2,1)S(1)}, bf16[1024,1024]{1,0:T(8,128)(2,1)}, u32[]{:S(2)}) copy-start(bf16[1024,1024]{1,0:T(8,128)(2,1)} %interp.1) | copy-start | bytes 6291460
  63.0 12.8 %collective-permute-start.10 = (bf16[256,512]{1,0:T(8,128)(2,1)S(1)}, bf16[256,512]{1,0:T(8,128)(2,1)S(1)}, u32[]{:S(2)}, u32[]{:S(2)}) collective-permute-start(bf16[256,512]{1,0:T(8,128)(2,1)S(1)} %shard_map.81), channel_id=1, source_target_pairs={{0,3},{1,2},{2,1},{3,0},{4,7},{5,6},{6,5},{7,4},{8,11},{9,10},{10,... | collective-permute-start | bytes 786440 | tf_op jit(solution)/shard_map/ppermute | solution.py:296

commit v4 on v3

--- a/solution.py
+++ b/solution.py
@@ -33,19 +33,26 @@
 
 
 def pick_kernel(
-    box_total, capacity, scalars, counts, listed, owner_hbm, grid_hbm, orbitals_hbm, out,
-    owner_map, grid_rows, orbitals, sems,
+    box_total, capacity, counts_hbm, grid_hbm, owner_hbm, listed_hbm, orbitals_hbm, out,
+    counts, grid_rows, owner_map, listed, orbitals, sems,
 ):
     copies = [
         pltpu.make_async_copy(source, target, sems.at[n])
         for n, (source, target) in enumerate(
-            [(grid_hbm, grid_rows), (owner_hbm, owner_map), (orbitals_hbm, orbitals)]
+            [
+                (counts_hbm, counts),
+                (grid_hbm, grid_rows),
+                (owner_hbm, owner_map),
+                (listed_hbm, listed),
+                (orbitals_hbm, orbitals),
+            ]
         )
     ]
     for copy in copies:
         copy.start()
     targets = box_total * capacity
-    my_box = scalars[0]
+    my_box = lax.axis_index("row") * lax.axis_size("col") + lax.axis_index("col")
+    copies[0].wait()
     start = jnp.int32(0)
     for b in range(box_total):
         start = start + jnp.where(b < my_box, counts[b], 0)
@@ -55,8 +62,8 @@
     blocks = SLOTS // LANES + 1
     top = owner_map.shape[0] - 1
     lane = lax.broadcasted_iota(jnp.int32, (1, LANES), 1)
-    copies[0].wait()
     copies[1].wait()
+    copies[2].wait()
     turned = pltpu.roll(grid_rows[...], shift, 1)
     lane8 = lax.broadcasted_iota(jnp.int32, turned.shape, 1)
     lined = jnp.where(lane8 < shift, pltpu.roll(turned, 1, 0), turned)
@@ -80,6 +87,7 @@
         target = jnp.where(live, owner * capacity + rank, -1)
         found = found + jnp.where(target_ids == target, lined[i : i + 1, :] + 1, 0)
     source = jnp.sum(found.astype(jnp.float32), axis=1, keepdims=True).astype(jnp.int32) - 1
+    copies[3].wait()
     per_owner = LIST // box_total
     fold = LANES // per_owner
     spread = jnp.broadcast_to(listed[...][:, None, :], (LIST // LANES, fold, LANES))
@@ -95,7 +103,7 @@
     )
     box = orbitals.shape[0]
     step = targets // 4
-    copies[2].wait()
+    copies[4].wait()
     for t in range(0, targets, step):
         hot = source[t : t + step] == lax.broadcasted_iota(jnp.int32, (step, box), 1)
         rows = jnp.dot(
@@ -146,23 +154,30 @@
     ).astype(jnp.bfloat16)
 
 
-def order_kernel(scalars, even, odd, out):
-    for parity, ref in enumerate((even, odd)):
+def order_kernel(masks, scalars, *refs):
+    pieces, out = refs[:-1], refs[-1]
+    places = [mask ^ parity for parity in (0, 1) for mask in masks]
+    for ref in pieces:
         for n in range(ref.shape[0] // OWN):
-            place = jnp.bitwise_xor(scalars[0], 2 * n + parity) * OWN
+            place = jnp.bitwise_xor(scalars[0], places.pop(0)) * OWN
             out[pl.ds(pl.multiple_of(place, OWN), OWN), :] = ref[n * OWN : (n + 1) * OWN, :]
 
 
-def block_kernel(scalars, left, right, coulomb, out, tile, weighted, sem):
-    source = pl.ds(pl.multiple_of(scalars[1] * OWN, OWN), OWN)
-    copy = pltpu.make_async_copy(coulomb.at[source, :], tile, sem)
-    copy.start()
+def fetch_kernel(scalars, coulomb, *refs):
+    outs, sems = refs[:-1], refs[-1]
+    copies = []
+    for n, out in enumerate(outs):
+        source = pl.ds(pl.multiple_of(scalars[n] * OWN, OWN), OWN)
+        copies.append(pltpu.make_async_copy(coulomb.at[source, :], out, sems.at[n]))
+        copies[-1].start()
+    for copy in copies:
+        copy.wait()
+
+
+def block_kernel(left, right, tile, out, weighted):
     step = 512
     for t in range(0, right.shape[0], step):
-        weighted[:, t : t + step] = pair_block(left[...], right[t : t + step, :])
-    copy.wait()
-    for t in range(0, right.shape[0], step):
-        pair = weighted[:, t : t + step].astype(jnp.float32)
+        pair = pair_block(left[...], right[t : t + step, :]).astype(jnp.float32)
         weighted[:, t : t + step] = (
             pair * tile[:, t : t + step].astype(jnp.float32)
         ).astype(jnp.bfloat16)
@@ -171,22 +186,16 @@
     ).astype(out.dtype)
 
 
-def block_sum(numbers, left, right, coulomb, dtype):
+def block_sum(left, right, tile, dtype):
     columns = right.shape[0]
     return local(
         block_kernel,
         jax.ShapeDtypeStruct((OWN, NORB), dtype),
-        numbers,
         left,
         right,
-        coulomb,
+        tile,
         flops=4 * OWN * columns * NORB,
-        far=3,
-        scratch=[
-            pltpu.VMEM((OWN, columns), jnp.bfloat16),
-            pltpu.VMEM((OWN, columns), jnp.bfloat16),
-            pltpu.SemaphoreType.DMA,
-        ],
+        scratch=[pltpu.VMEM((OWN, columns), jnp.bfloat16)],
     )
 
 
@@ -229,8 +238,18 @@
     ).astype(jnp.bfloat16)
 
 
-def apply_kernel(interp, chosen, out):
-    out[...] = -jnp.dot(interp[...], chosen[...], preferred_element_type=jnp.float32)
+def apply_kernel(interp, chosen, out, parts, sems):
+    rows = parts.shape[1]
+    copies = []
+    for n in range(parts.shape[0]):
+        parts[n] = -jnp.dot(
+            interp[n * rows : (n + 1) * rows, :], chosen[...], preferred_element_type=jnp.float32
+        )
+        target = out.at[n * rows : (n + 1) * rows, :]
+        copies.append(pltpu.make_async_copy(parts.at[n], target, sems.at[n]))
+        copies[-1].start()
+    for copy in copies:
+        copy.wait()
 
 
 def shards(orbitals, coulomb, interp, box_counts, owner_map, grid_rows, listed):
@@ -247,24 +266,25 @@
     outgoing = pl.pallas_call(
         functools.partial(pick_kernel, box_total, capacity),
         out_shape=jax.ShapeDtypeStruct((box_total, packed, LANES), jnp.bfloat16),
-        in_specs=[smem(), smem(), vmem(), hbm(), hbm(), hbm()],
+        in_specs=[hbm()] * 5,
         out_specs=vmem(),
         scratch_shapes=[
+            pltpu.SMEM((box_total,), jnp.int32),
+            pltpu.VMEM((grid_rows.shape[1] // LANES, LANES), jnp.int32),
             pltpu.VMEM((point_total // LANES, LANES), jnp.int32),
-            pltpu.VMEM((grid_rows.shape[1] // LANES, LANES), jnp.int32),
+            pltpu.VMEM((LIST // LANES, LANES), jnp.int32),
             pltpu.VMEM(orbitals.shape, jnp.bfloat16),
-            pltpu.SemaphoreType.DMA((3,)),
+            pltpu.SemaphoreType.DMA((5,)),
         ],
         compiler_params=params(PICK_LIMIT),
         cost_estimate=pl.CostEstimate(
             flops=2 * SLOTS * LIST * NORB, bytes_accessed=2 << 20, transcendentals=0
         ),
     )(
-        my_box.reshape(1).astype(jnp.int32),
         box_counts,
+        grid_rows.reshape(grid_rows.shape[1] // LANES, LANES),
+        owner_map.reshape(point_total // LANES, LANES),
         listed.reshape(LIST // LANES, LANES),
-        owner_map.reshape(point_total // LANES, LANES),
-        grid_rows.reshape(grid_rows.shape[1] // LANES, LANES),
         orbitals,
     )
     received = lax.all_to_all(
@@ -295,6 +315,10 @@
     def swap(rows, mask):
         return lax.ppermute(rows, "col", [(i, i ^ mask) for i in range(col_count)])
 
+    def join(*rows):
+        total = sum(r.shape[0] for r in rows)
+        return local(join_kernel, jax.ShapeDtypeStruct((total, NORB), rows[0].dtype), *rows)
+
     def flip(rows, mask):
         return lax.ppermute(rows, "row", [(i, i ^ mask) for i in range(row_count)])
 
@@ -303,24 +327,33 @@
         if mask & (mask - 1) == 0:
             left[mask] = swap(owned_rows, mask)
 
-    blocks = {0: [owned_rows]}
     whole = {0: owned_rows}
     half = OWN // 2
-    for mask in range(2, row_count, 2):
-        bits = [1 << b for b in range(1, mask.bit_length()) if mask >> b & 1]
-        if len(bits) == 1:
-            blocks[mask] = [flip(owned_rows, mask)]
-        else:
-            low, high = bits[0], bits[-1]
-            blocks[mask] = [
-                flip(whole[mask ^ high][:half], high),
-                flip(whole[mask ^ low][half:], low),
-            ]
-        whole[mask] = jnp.concatenate(blocks[mask])
-    pieces = [piece for mask in range(0, row_count, 2) for piece in blocks[mask]]
+    single = [1 << b for b in range(1, row_count.bit_length() - 1)]
+    double = [mask for mask in range(2, row_count, 2) if mask not in single]
+    for mask in single:
+        whole[mask] = flip(owned_rows, mask)
+    passed_on = [owned_rows, join(*[whole[mask] for mask in single])]
+    for mask in double:
+        low, high = mask & -mask, 1 << (mask.bit_length() - 1)
+        whole[mask] = join(
+            flip(whole[mask ^ high][:half], high), flip(whole[mask ^ low][half:], low)
+        )
+    if double:
+        passed_on.append(join(*[whole[mask] for mask in double]))
+    masks = [0] + single + double
     shape = jax.ShapeDtypeStruct
-    even = local(join_kernel, shape((row_count // 2 * OWN, NORB), jnp.bfloat16), *pieces)
-    odd = flip(even, 1)
+    tiles = local(
+        fetch_kernel,
+        tuple(shape((OWN, row_count * OWN), jnp.bfloat16) for _ in range(col_count)),
+        jnp.bitwise_xor(my_col, jnp.arange(col_count)).astype(jnp.int32),
+        coulomb,
+        far=1,
+        scratch=[pltpu.SemaphoreType.DMA((col_count,))],
+    )
+
+    passed_on[-1], *tiles = lax.optimization_barrier((passed_on[-1], *tiles))
+    mirrored = [flip(rows, 1) for rows in passed_on]
     direct = [mask for mask in left if mask]
     held = local(
         hold_kernel,
@@ -328,22 +361,22 @@
         *[left[mask] for mask in direct],
         flops=20 * 10**9,
     )
-    *held, odd = lax.optimization_barrier((*held, odd))
+    *held, mirrored[-1] = lax.optimization_barrier((*held, mirrored[-1]))
     left.update(zip(direct, held))
     for mask in range(1, col_count):
         if mask not in left:
             low = mask & -mask
             left[mask] = swap(left[mask ^ low], low)
 
-    def numbers(mask):
-        return jnp.stack([my_row, jnp.bitwise_xor(my_col, mask)]).astype(jnp.int32)
-
     right = local(
-        order_kernel, shape((row_count * OWN, NORB), jnp.bfloat16), numbers(0), even, odd
-    )
-
+        functools.partial(order_kernel, masks),
+        shape((row_count * OWN, NORB), jnp.bfloat16),
+        my_row.reshape(1).astype(jnp.int32),
+        *passed_on,
+        *mirrored,
+    )
     def partial_sum(mask, dtype):
-        return block_sum(numbers(mask), left[mask], right, coulomb, dtype)
+        return block_sum(left[mask], right, tiles[mask], dtype)
 
     arrived = []
     for mask in sorted(range(1, col_count), key=lambda m: (m & 1, m)):
@@ -363,17 +396,16 @@
         concat_axis=0,
         tiled=True,
     ).reshape(LIST, NORB)
-    box = interp.shape[0]
-    step = 256
+    box, count = interp.shape[0], 4
     return pl.pallas_call(
         apply_kernel,
-        grid=(box // step,),
         out_shape=jax.ShapeDtypeStruct((box, NORB), jnp.float32),
-        in_specs=[
-            pl.BlockSpec((step, LIST), lambda i: (i, 0)),
-            pl.BlockSpec((LIST, NORB), lambda i: (0, 0)),
+        in_specs=[vmem(), vmem()],
+        out_specs=hbm(),
+        scratch_shapes=[
+            pltpu.VMEM((count, box // count, NORB), jnp.float32),
+            pltpu.SemaphoreType.DMA((count,)),
         ],
-        out_specs=pl.BlockSpec((step, NORB), lambda i: (i, 0)),
         compiler_params=params(),
     )(interp, chosen)
 

time: 114 us -> 109 us (0.956)
  Pallas kernels: 18.8 us -> 14.6 us
  blocking collectives: 34 us -> 31.3 us
  starting transfers between devices: 14.7 us -> 16.4 us
    ppermute x6, waiting for transfers between devices: 10.7 us -> 17.1 us  [swap(): return lax.ppermute(rows, 'col', [(i, i ^ mask) for i in range(col_count)])]
    ppermute x5 -> x7, waiting for transfers between devices: 12.3 us -> 6.76 us  [flip(): return lax.ppermute(rows, 'row', [(i, i ^ mask) for i in range(row_count)])]
    pallas_call x7 -> x10, Pallas kernels: 10.9 us -> 8.11 us  [local(): pl.pallas_call(kernel, out_shape=out, in_specs=[spec(n, a) for n, a in en...]
    all_to_all x1, blocking collectives: 34 us -> 31.3 us  [shards(): lax.all_to_all(picked.reshape(box_total, per_owner, NORB), ('row', 'col')...]
    ppermute x5 -> x7, starting transfers between devices: 4.17 us -> 5.56 us  [flip(): return lax.ppermute(rows, 'row', [(i, i ^ mask) for i in range(row_count)])]
  transfers between devices with their start and end apart: 12 -> 14, of which waited for: 9 -> 10; matrix products, arithmetic and copies ran while one was open for 2% -> 2% of each run, Pallas kernels for 10% -> 7%
where the time goes in v4:
time: 109 us
  waiting for transfers between devices  44.1 us (40%)
  blocking collectives  31.3 us (29%)
  starting transfers between devices  16.4 us (15%)
  Pallas kernels  14.6 us (13%)
  other arithmetic  1.73 us (2%)
    all_to_all x1, blocking collectives, shards(): lax.all_to_all(picked.reshape(box_total, per_owner, NORB), ('row', 'col')...  31.3 us
    all_to_all x1, waiting for transfers between devices, shards(): lax.all_to_all(outgoing, ('row', 'col'), split_axis=0, concat_axis=0, til...  20.2 us
    ppermute x6, waiting for transfers between devices, swap(): return lax.ppermute(rows, 'col', [(i, i ^ mask) for i in range(col_count)])  17.1 us
    pallas_call x10, Pallas kernels, local(): pl.pallas_call(kernel, out_shape=out, in_specs=[spec(n, a) for n, a in en...  8.11 us
    all_to_all x1, starting transfers between devices, shards(): lax.all_to_all(outgoing, ('row', 'col'), split_axis=0, concat_axis=0, til...  7.1 us
    ppermute x7, waiting for transfers between devices, flip(): return lax.ppermute(rows, 'row', [(i, i ^ mask) for i in range(row_count)])  6.76 us
    ppermute x7, starting transfers between devices, flip(): return lax.ppermute(rows, 'row', [(i, i ^ mask) for i in range(row_count)])  5.56 us
    ppermute x6, starting transfers between devices, swap(): return lax.ppermute(rows, 'col', [(i, i ^ mask) for i in range(col_count)])  3.7 us
  transfers between devices with their start and end apart: 14, of which 10 were waited for; matrix products, arithmetic and copies ran while one was open for 2% of the time, Pallas kernels for 7%

profile of v4, /device:TPU:1, one launch (start us, length us, event | category | flops | bytes accessed | tf_op | source)
XLA Modules:
  0.0 108.5 jit_solution(13376863126504735244)
XLA Ops:
  0.0 3.4 %shard_map.73 = bf16[32,104,128]{2,1,0:T(8,128)(2,1)} custom-call(s32[32]{0:T(128)} %counts_hbm.1, s32[8,128]{1,0:T(8,128)} %bitcast.13, s32[64,128]{1,0:T(8,128)} %bitcast.10, s32[8,128]{1,0:T(8,128)} %bitcast.14, bf16[1024,512]{1,0:T(8,128)(2,1)} %orbitals_hbm.1), custom_call_target="tpu_custom_call" | custom-call | flops 805306368 | bytes 2097152 | tf_op jit(solution)/shard_map/pallas_call | solution.py:266
  3.5 7.1 %all-to-all-start = ((bf16[32,104,128]{2,1,0:T(8,128)(2,1)}), bf16[32,104,128]{2,1,0:T(8,128)(2,1)S(1)}, u32[]{:S(2)}, u32[]{:S(2)}) async-start(bf16[32,104,128]{2,1,0:T(8,128)(2,1)} %shard_map.73), calls=%async_computation | async-start | bytes 1703936 | tf_op jit(solution)/shard_map/all_to_all | solution.py:290
  10.9 1.2 %select_reduce_fusion = s32[256]{0:T(256)S(1)} fusion(s32[8192]{0:T(1024)S(1)} %copy-done.1, s32[256]{0:T(256)S(1)} %iota_add_fusion), kind=kLoop, calls=%fused_computation | loop fusion | flops 6291200 | bytes 34816 | tf_op jit(solution)/shard_map/reduce_sum | solution.py:296
  12.6 20.2 %all-to-all-done.received = bf16[32,104,128]{2,1,0:T(8,128)(2,1)S(1)} async-done(((bf16[32,104,128]{2,1,0:T(8,128)(2,1)}), bf16[32,104,128]{2,1,0:T(8,128)(2,1)S(1)}, u32[]{:S(2)}, u32[]{:S(2)}) %all-to-all-start) | async-done | bytes 852000 | tf_op jit(solution)/shard_map/all_to_all | solution.py:290
  33.2 1.3 %collective-permute-start.1 = (bf16[256,512]{1,0:T(8,128)(2,1)S(1)}, bf16[256,512]{1,0:T(8,128)(2,1)S(1)}, u32[]{:S(2)}, u32[]{:S(2)}) collective-permute-start(bf16[256,512]{1,0:T(8,128)(2,1)S(1)} %get-tuple-element.22.refs_0_.left), channel_id=1, source_target_pairs={{0,16},{4,20},{8,24},{12,28},{16,0},{20,4},{24,8},{28,12},{1,17},{... | collective-permute-start | bytes 786440 | tf_op jit(solution)/shard_map/ppermute | solution.py:323
  35.6 5.5 %collective-permute-done.1.refs_1_ = bf16[256,512]{1,0:T(8,128)(2,1)S(1)} collective-permute-done((bf16[256,512]{1,0:T(8,128)(2,1)S(1)}, bf16[256,512]{1,0:T(8,128)(2,1)S(1)}, u32[]{:S(2)}, u32[]{:S(2)}) %collective-permute-start.1) | collective-permute-done | bytes 262176 | tf_op jit(solution)/shard_map/ppermute | solution.py:323
  41.1 1.2 %collective-permute-start.3 = (bf16[128,512]{1,0:T(8,128)(2,1)S(1)}, bf16[128,512]{1,0:T(8,128)(2,1)S(1)}, u32[]{:S(2)}, u32[]{:S(2)}) collective-permute-start(bf16[128,512]{1,0:T(8,128)(2,1)S(1)} %slice.9), channel_id=1, source_target_pairs={{0,8},{4,12},{8,0},{12,4},{16,24},{20,28},{24,16},{28,20},{1,9},{5... | collective-permute-start | bytes 393224 | tf_op jit(solution)/shard_map/ppermute | solution.py:323
  42.9 2.8 %shard_map.78 = (bf16[256,2048]{1,0:T(8,128)(2,1)S(1)}, bf16[256,2048]{1,0:T(8,128)(2,1)S(1)}, bf16[256,2048]{1,0:T(8,128)(2,1)S(1)}, bf16[256,2048]{1,0:T(8,128)(2,1)S(1)}) custom-call(s32[4]{0:T(128)S(1)} %iota_xor_fusion.scalars, bf16[1024,2048]{1,0:T(8,128)(2,1)} %coulomb.1), custom_call_target="tpu_custom_call" | custom-call | tf_op jit(solution)/shard_map/pallas_call | solution.py:208
  45.7 1.3 %collective-permute-start.4 = (bf16[256,512]{1,0:T(8,128)(2,1)S(1)}, bf16[256,512]{1,0:T(8,128)(2,1)S(1)}, u32[]{:S(2)}, u32[]{:S(2)}) collective-permute-start(bf16[256,512]{1,0:T(8,128)(2,1)S(1)} %get-tuple-element.22.refs_0_.left), channel_id=1, source_target_pairs={{0,4},{4,0},{8,12},{12,8},{16,20},{20,16},{24,28},{28,24},{1,5},{5... | collective-permute-start | bytes 786440 | tf_op jit(solution)/shard_map/ppermute | solution.py:323
  47.6 1.0 collective-permute-start.8
  49.2 0.6 collective-permute-done.8.refs_5_
  50.2 1.3 %shard_map.82 = bf16[256,512]{1,0:T(8,128)(2,1)S(1)} custom-call(bf16[256,512]{1,0:T(8,128)(2,1)S(1)} %get-tuple-element.32.left, bf16[2048,512]{1,0:T(8,128)(2,1)S(1)} %shard_map.80.right, bf16[256,2048]{1,0:T(8,128)(2,1)S(1)} %get-tuple-element.33.tile), custom_call_target="tpu_custom_call" | custom-call | flops 1073741824 | tf_op jit(solution)/shard_map/pallas_call | solution.py:208
  51.5 0.8 collective-permute-start.9
  52.2 1.3 %shard_map.83 = bf16[256,512]{1,0:T(8,128)(2,1)S(1)} custom-call(bf16[256,512]{1,0:T(8,128)(2,1)S(1)} %get-tuple-element.34.left, bf16[2048,512]{1,0:T(8,128)(2,1)S(1)} %shard_map.80.right, bf16[256,2048]{1,0:T(8,128)(2,1)S(1)} %get-tuple-element.35.tile), custom_call_target="tpu_custom_call" | custom-call | flops 1073741824 | tf_op jit(solution)/shard_map/pallas_call | solution.py:208
  53.5 1.2 %collective-permute-start.10 = (bf16[256,512]{1,0:T(8,128)(2,1)S(1)}, bf16[256,512]{1,0:T(8,128)(2,1)S(1)}, u32[]{:S(2)}, u32[]{:S(2)}) collective-permute-start(bf16[256,512]{1,0:T(8,128)(2,1)S(1)} %shard_map.83), channel_id=1, source_target_pairs={{0,1},{1,0},{2,3},{3,2},{4,5},{5,4},{6,7},{7,6},{8,9},{9,8},{10,11... | collective-permute-start | bytes 786440 | tf_op jit(solution)/shard_map/ppermute | solution.py:316
  54.8 6.0 %collective-permute-done.11.left = bf16[256,512]{1,0:T(8,128)(2,1)S(1)} collective-permute-done((bf16[256,512]{1,0:T(8,128)(2,1)S(1)}, bf16[256,512]{1,0:T(8,128)(2,1)S(1)}, u32[]{:S(2)}, u32[]{:S(2)}) %collective-permute-start.11) | collective-permute-done | bytes 262176 | tf_op jit(solution)/shard_map/ppermute | solution.py:316
  60.8 1.3 %shard_map.84 = bf16[256,512]{1,0:T(8,128)(2,1)S(1)} custom-call(bf16[256,512]{1,0:T(8,128)(2,1)S(1)} %collective-permute-done.11.left, bf16[2048,512]{1,0:T(8,128)(2,1)S(1)} %shard_map.80.right, bf16[256,2048]{1,0:T(8,128)(2,1)S(1)} %get-tuple-element.36.tile), custom_call_target="tpu_custom_call" | custom-call | flops 1073741824 | tf_op jit(solution)/shard_map/pallas_call | solution.py:208
  62.1 0.6 collective-permute-start.12
  62.7 1.3 %shard_map.81.own = f32[256,512]{1,0:T(8,128)S(1)} custom-call(bf16[256,512]{1,0:T(8,128)(2,1)S(1)} %get-tuple-element.22.refs_0_.left, bf16[2048,512]{1,0:T(8,128)(2,1)S(1)} %shard_map.80.right, bf16[256,2048]{1,0:T(8,128)(2,1)S(1)} %get-tuple-element.31.tile), custom_call_target="tpu_custom_call" | custom-call | flops 1073741824 | tf_op jit(solution)/shard_map/pallas_call | solution.py:208
  64.0 1.5 %collective-permute-done.9.refs_0_ = bf16[256,512]{1,0:T(8,128)(2,1)S(1)} collective-permute-done((bf16[256,512]{1,0:T(8,128)(2,1)S(1)}, bf16[256,512]{1,0:T(8,128)(2,1)S(1)}, u32[]{:S(2)}, u32[]{:S(2)}) %collective-permute-start.9) | collective-permute-done | bytes 262176 | tf_op jit(solution)/shard_map/ppermute | solution.py:316
  65.4 3.1 %collective-permute-done.10.refs_1_ = bf16[256,512]{1,0:T(8,128)(2,1)S(1)} collective-permute-done((bf16[256,512]{1,0:T(8,128)(2,1)S(1)}, bf16[256,512]{1,0:T(8,128)(2,1)S(1)}, u32[]{:S(2)}, u32[]{:S(2)}) %collective-permute-start.10) | collective-permute-done | bytes 262176 | tf_op jit(solution)/shard_map/ppermute | solution.py:316
  68.6 6.0 %collective-permute-done.12.refs_2_ = bf16[256,512]{1,0:T(8,128)(2,1)S(1)} collective-permute-done((bf16[256,512]{1,0:T(8,128)(2,1)S(1)}, bf16[256,512]{1,0:T(8,128)(2,1)S(1)}, u32[]{:S(2)}, u32[]{:S(2)}) %collective-permute-start.12) | collective-permute-done | bytes 262176 | tf_op jit(solution)/shard_map/ppermute | solution.py:316
  75.2 31.3 %all_to_all.10 = bf16[32,32,512]{2,1,0:T(8,128)(2,1)S(1)} all-to-all(bf16[32,32,512]{2,1,0:T(8,128)(2,1)S(1)} %bitcast.9), channel_id=1, replica_groups=mesh['row'=8,'col'=4] {'row','col'}, dimensions={0} | all-to-all | bytes 2097152 | tf_op jit(solution)/shard_map/all_to_all | solution.py:392
  106.5 2.1 %shard_map.86 = f32[1024,512]{1,0:T(8,128)} custom-call(bf16[1024,1024]{1,0:T(8,128)(2,1)S(1)} %copy-done, bf16[1024,512]{1,0:T(8,128)(2,1)S(1)} %bitcast.8), custom_call_target="tpu_custom_call" | custom-call | tf_op jit(solution)/shard_map/pallas_call | solution.py:400
  (37 shorter events, 4.9 us)
Async XLA Ops:
  0.0 10.6 %copy-start.2 = (s32[32]{0:T(128)S(1)}, s32[32]{0:T(128)}, u32[]{:S(2)}) copy-start(s32[32]{0:T(128)} %counts_hbm.1) | copy-start | bytes 388
  0.0 10.9 %copy-start.1 = (s32[8192]{0:T(1024)S(1)}, s32[8192]{0:T(1024)}, u32[]{:S(2)}) copy-start(s32[8192]{0:T(1024)} %param.11) | copy-start | bytes 98308
  3.5 29.3 %all-to-all-start = ((bf16[32,104,128]{2,1,0:T(8,128)(2,1)}), bf16[32,104,128]{2,1,0:T(8,128)(2,1)S(1)}, u32[]{:S(2)}, u32[]{:S(2)}) async-start(bf16[32,104,128]{2,1,0:T(8,128)(2,1)} %shard_map.73), calls=%async_computation | async-start | bytes 1703936 | tf_op jit(solution)/shard_map/all_to_all | solution.py:290
  33.2 7.9 %collective-permute-start.1 = (bf16[256,512]{1,0:T(8,128)(2,1)S(1)}, bf16[256,512]{1,0:T(8,128)(2,1)S(1)}, u32[]{:S(2)}, u32[]{:S(2)}) collective-permute-start(bf16[256,512]{1,0:T(8,128)(2,1)S(1)} %get-tuple-element.22.refs_0_.left), channel_id=1, source_target_pairs={{0,16},{4,20},{8,24},{12,28},{16,0},{20,4},{24,8},{28,12},{1,17},{... | collective-permute-start | bytes 786440 | tf_op jit(solution)/shard_map/ppermute | solution.py:323
  34.5 8.1 %collective-permute-start = (bf16[256,512]{1,0:T(8,128)(2,1)S(1)}, bf16[256,512]{1,0:T(8,128)(2,1)S(1)}, u32[]{:S(2)}, u32[]{:S(2)}) collective-permute-start(bf16[256,512]{1,0:T(8,128)(2,1)S(1)} %get-tuple-element.22.refs_0_.left), channel_id=1, source_target_pairs={{0,8},{4,12},{8,0},{12,4},{16,24},{20,28},{24,16},{28,20},{1,9},{5... | collective-permute-start | bytes 786440 | tf_op jit(solution)/shard_map/ppermute | solution.py:323
  34.7 14.4 %collective-permute-start.7 = (bf16[256,512]{1,0:T(8,128)(2,1)S(1)}, bf16[256,512]{1,0:T(8,128)(2,1)S(1)}, u32[]{:S(2)}, u32[]{:S(2)}) collective-permute-start(bf16[256,512]{1,0:T(8,128)(2,1)S(1)} %get-tuple-element.22.refs_0_.left), channel_id=1, source_target_pairs={{0,2},{1,3},{2,0},{3,1},{4,6},{5,7},{6,4},{7,5},{8,10},{9,11},{10,... | collective-permute-start | bytes 786440 | tf_op jit(solution)/shard_map/ppermute | solution.py:316
  35.3 13.9 %collective-permute-start.6 = (bf16[256,512]{1,0:T(8,128)(2,1)S(1)}, bf16[256,512]{1,0:T(8,128)(2,1)S(1)}, u32[]{:S(2)}, u32[]{:S(2)}) collective-permute-start(bf16[256,512]{1,0:T(8,128)(2,1)S(1)} %get-tuple-element.22.refs_0_.left), channel_id=1, source_target_pairs={{0,1},{1,0},{2,3},{3,2},{4,5},{5,4},{6,7},{7,6},{8,9},{9,8},{10,11... | collective-permute-start | bytes 786440 | tf_op jit(solution)/shard_map/ppermute | solution.py:316
  41.1 5.9 %collective-permute-start.3 = (bf16[128,512]{1,0:T(8,128)(2,1)S(1)}, bf16[128,512]{1,0:T(8,128)(2,1)S(1)}, u32[]{:S(2)}, u32[]{:S(2)}) collective-permute-start(bf16[128,512]{1,0:T(8,128)(2,1)S(1)} %slice.9), channel_id=1, source_target_pairs={{0,8},{4,12},{8,0},{12,4},{16,24},{20,28},{24,16},{28,20},{1,9},{5... | collective-permute-start | bytes 393224 | tf_op jit(solution)/shard_map/ppermute | solution.py:323
  42.6 5.0 %collective-permute-start.2 = (bf16[128,512]{1,0:T(8,128)(2,1)S(1)}, bf16[128,512]{1,0:T(8,128)(2,1)S(1)}, u32[]{:S(2)}, u32[]{:S(2)}) collective-permute-start(bf16[128,512]{1,0:T(8,128)(2,1)S(1)} %slice.8), channel_id=1, source_target_pairs={{0,16},{4,20},{8,24},{12,28},{16,0},{20,4},{24,8},{28,12},{1,17},{... | collective-permute-start | bytes 393224 | tf_op jit(solution)/shard_map/ppermute | solution.py:323
  45.7 4.3 %collective-permute-start.4 = (bf16[256,512]{1,0:T(8,128)(2,1)S(1)}, bf16[256,512]{1,0:T(8,128)(2,1)S(1)}, u32[]{:S(2)}, u32[]{:S(2)}) collective-permute-start(bf16[256,512]{1,0:T(8,128)(2,1)S(1)} %get-tuple-element.22.refs_0_.left), channel_id=1, source_target_pairs={{0,4},{4,0},{8,12},{12,8},{16,20},{20,16},{24,28},{28,24},{1,5},{5... | collective-permute-start | bytes 786440 | tf_op jit(solution)/shard_map/ppermute | solution.py:323
  47.1 3.0 %collective-permute-start.5 = (bf16[512,512]{1,0:T(8,128)(2,1)S(1)}, bf16[512,512]{1,0:T(8,128)(2,1)S(1)}, u32[]{:S(2)}, u32[]{:S(2)}) collective-permute-start(bf16[512,512]{1,0:T(8,128)(2,1)S(1)} %shard_map.75.refs_1_), channel_id=1, source_target_pairs={{0,4},{4,0},{8,12},{12,8},{16,20},{20,16},{24,28},{28,24},{1,5},{5... | collective-permute-start | bytes 1572872 | tf_op jit(solution)/shard_map/ppermute | solution.py:323
  47.6 2.2 %collective-permute-start.8 = (bf16[256,512]{1,0:T(8,128)(2,1)S(1)}, bf16[256,512]{1,0:T(8,128)(2,1)S(1)}, u32[]{:S(2)}, u32[]{:S(2)}) collective-permute-start(bf16[256,512]{1,0:T(8,128)(2,1)S(1)} %shard_map.77.refs_2_), channel_id=1, source_target_pairs={{0,4},{4,0},{8,12},{12,8},{16,20},{20,16},{24,28},{28,24},{1,5},{5... | collective-permute-start | bytes 786440 | tf_op jit(solution)/shard_map/ppermute | solution.py:323
  49.8 10.9 %collective-permute-start.11 = (bf16[256,512]{1,0:T(8,128)(2,1)S(1)}, bf16[256,512]{1,0:T(8,128)(2,1)S(1)}, u32[]{:S(2)}, u32[]{:S(2)}) collective-permute-start(bf16[256,512]{1,0:T(8,128)(2,1)S(1)} %get-tuple-element.32.left), channel_id=1, source_target_pairs={{0,1},{1,0},{2,3},{3,2},{4,5},{5,4},{6,7},{7,6},{8,9},{9,8},{10,11... | collective-permute-start | bytes 786440 | tf_op jit(solution)/shard_map/ppermute | solution.py:316
  51.5 14.0 %collective-permute-start.9 = (bf16[256,512]{1,0:T(8,128)(2,1)S(1)}, bf16[256,512]{1,0:T(8,128)(2,1)S(1)}, u32[]{:S(2)}, u32[]{:S(2)}) collective-permute-start(bf16[256,512]{1,0:T(8,128)(2,1)S(1)} %shard_map.82), channel_id=1, source_target_pairs={{0,2},{1,3},{2,0},{3,1},{4,6},{5,7},{6,4},{7,5},{8,10},{9,11},{10,... | collective-permute-start | bytes 786440 | tf_op jit(solution)/shard_map/ppermute | solution.py:316
  53.5 15.1 %collective-permute-start.10 = (bf16[256,512]{1,0:T(8,128)(2,1)S(1)}, bf16[256,512]{1,0:T(8,128)(2,1)S(1)}, u32[]{:S(2)}, u32[]{:S(2)}) collective-permute-start(bf16[256,512]{1,0:T(8,128)(2,1)S(1)} %shard_map.83), channel_id=1, source_target_pairs={{0,1},{1,0},{2,3},{3,2},{4,5},{5,4},{6,7},{7,6},{8,9},{9,8},{10,11... | collective-permute-start | bytes 786440 | tf_op jit(solution)/shard_map/ppermute | solution.py:316
  62.1 44.4 %copy-start = (bf16[1024,1024]{1,0:T(8,128)(2,1)S(1)}, bf16[1024,1024]{1,0:T(8,128)(2,1)}, u32[]{:S(2)}) copy-start(bf16[1024,1024]{1,0:T(8,128)(2,1)} %interp.1) | copy-start | bytes 6291460
  62.1 12.5 %collective-permute-start.12 = (bf16[256,512]{1,0:T(8,128)(2,1)S(1)}, bf16[256,512]{1,0:T(8,128)(2,1)S(1)}, u32[]{:S(2)}, u32[]{:S(2)}) collective-permute-start(bf16[256,512]{1,0:T(8,128)(2,1)S(1)} %shard_map.84), channel_id=1, source_target_pairs={{0,3},{1,2},{2,1},{3,0},{4,7},{5,6},{6,5},{7,4},{8,11},{9,10},{10,... | collective-permute-start | bytes 786440 | tf_op jit(solution)/shard_map/ppermute | solution.py:316

commit v5 on v4

--- a/solution.py
+++ b/solution.py
@@ -12,6 +12,7 @@
 OWN = 256
 SLOTS = 768
 LANES = 128
+UPPER = 160
 VMEM_LIMIT = 48 * 1024 * 1024
 PICK_LIMIT = 60 * 1024 * 1024
 
@@ -174,28 +175,39 @@
         copy.wait()
 
 
-def block_kernel(left, right, tile, out, weighted):
+def block_kernel(count, left, right, tile, *refs):
+    earlier, outs, weighted = refs[: -1 - count], refs[-1 - count : -1], refs[-1]
     step = 512
     for t in range(0, right.shape[0], step):
         pair = pair_block(left[...], right[t : t + step, :]).astype(jnp.float32)
         weighted[:, t : t + step] = (
             pair * tile[:, t : t + step].astype(jnp.float32)
         ).astype(jnp.bfloat16)
-    out[...] = jnp.dot(
-        weighted[...], right[...], preferred_element_type=jnp.float32
-    ).astype(out.dtype)
-
-
-def block_sum(left, right, tile, dtype):
-    columns = right.shape[0]
+    total = jnp.dot(weighted[...], right[...], preferred_element_type=jnp.float32)
+    at = 0
+    for out in outs:
+        rows = out.shape[0]
+        out[...] = total[at : at + rows, :].astype(out.dtype)
+        at += rows
+    for ref in earlier:
+        rows = ref.shape[0]
+        outs[0][:rows, :] = total[:rows, :] + ref[...].astype(jnp.float32)
+
+
+def add_kernel(one, other, out):
+    out[...] = (one[...] + other[...].astype(jnp.float32)).astype(out.dtype)
+
+
+def block_sum(left, right, tile, *parts, earlier=(), flops=0):
     return local(
-        block_kernel,
-        jax.ShapeDtypeStruct((OWN, NORB), dtype),
+        functools.partial(block_kernel, len(parts)),
+        tuple(jax.ShapeDtypeStruct((rows, NORB), dtype) for rows, dtype in parts),
         left,
         right,
         tile,
-        flops=4 * OWN * columns * NORB,
-        scratch=[pltpu.VMEM((OWN, columns), jnp.bfloat16)],
+        *earlier,
+        flops=flops,
+        scratch=[pltpu.VMEM((OWN, right.shape[0]), jnp.bfloat16)],
     )
 
 
@@ -216,7 +228,7 @@
     )(*args)
 
 
-def select_kernel(others, per_owner, index, own, *refs):
+def select_kernel(per_owner, index, own, *refs):
     boxes = index.shape[0]
     spread = jnp.broadcast_to(index[...][:, None, :], (boxes, per_owner, LANES))
     diagonal = lax.broadcasted_iota(jnp.int32, spread.shape, 1) == lax.broadcasted_iota(
@@ -225,11 +237,14 @@
     picks = jnp.sum(jnp.where(diagonal, spread, 0).astype(jnp.float32), axis=2, keepdims=True)
     picks = picks.reshape(boxes * per_owner, 1).astype(jnp.int32)
     out = refs[-1]
-    totals, rows = [], refs[0].shape[0]
-    for n in range(OWN // rows):
-        total = own[n * rows : (n + 1) * rows, :]
-        for ref in refs[n * others : (n + 1) * others]:
-            total = total + ref[...].astype(jnp.float32)
+    totals = []
+    for rows in (slice(0, UPPER), slice(UPPER, OWN)):
+        total = own[rows, :]
+        for ref in refs[:-1]:
+            if ref.shape[0] == OWN:
+                total = total + ref[rows, :].astype(jnp.float32)
+            elif ref.shape[0] == rows.stop - rows.start:
+                total = total + ref[...].astype(jnp.float32)
         totals.append(total.astype(jnp.bfloat16))
     projected = jnp.concatenate(totals)
     hot = picks == lax.broadcasted_iota(jnp.int32, (boxes * per_owner, OWN), 1)
@@ -361,7 +376,7 @@
         *[left[mask] for mask in direct],
         flops=20 * 10**9,
     )
-    *held, mirrored[-1] = lax.optimization_barrier((*held, mirrored[-1]))
+    *held, mirrored[0] = lax.optimization_barrier((*held, mirrored[0]))
     left.update(zip(direct, held))
     for mask in range(1, col_count):
         if mask not in left:
@@ -375,15 +390,24 @@
         *passed_on,
         *mirrored,
     )
-    def partial_sum(mask, dtype):
-        return block_sum(left[mask], right, tiles[mask], dtype)
-
-    arrived = []
-    for mask in sorted(range(1, col_count), key=lambda m: (m & 1, m)):
-        arrived.append(swap(partial_sum(mask, jnp.bfloat16), mask))
-    own_sum = partial_sum(0, jnp.float32)
+    def partial_sum(mask, *parts, **options):
+        return block_sum(left[mask], right, tiles[mask], *parts, **options)
+
+    short, wide = jnp.bfloat16, jnp.float32
+    upper_two, lower_two = partial_sum(2, (UPPER, short), (OWN - UPPER, wide))
+    left[3], _ = lax.optimization_barrier((left[3], upper_two))
+    upper_three, lower_three = partial_sum(3, (UPPER, short), (OWN - UPPER, short))
+    first = swap(upper_two, 2)
+    handed = swap(lower_three, 1)
+    arrived = [swap(upper_three, 3)]
+    lower = local(add_kernel, shape(lower_two.shape, short), lower_two, handed)
+    arrived.append(swap(lower, 2))
+    left[1], _ = lax.optimization_barrier((left[1], upper_three))
+    for mask in [1, *range(4, col_count)]:
+        arrived.append(swap(partial_sum(mask, (OWN, short))[0], mask))
+    (own_sum,) = partial_sum(0, (OWN, wide), earlier=[first], flops=10**10)
     picked = pl.pallas_call(
-        functools.partial(select_kernel, col_count - 1, per_owner),
+        functools.partial(select_kernel, per_owner),
         out_shape=jax.ShapeDtypeStruct((LIST, NORB), jnp.bfloat16),
         in_specs=[vmem()] * (2 + len(arrived)),
         out_specs=vmem(),

time: 109 us -> 107 us (0.982)
  waiting for transfers between devices: 44.1 us -> 40.2 us
  blocking collectives: 31.3 us -> 33.7 us
    ppermute x6 -> x8, waiting for transfers between devices: 17.1 us -> 12.9 us  [swap(): return lax.ppermute(rows, 'col', [(i, i ^ mask) for i in range(col_count)])]
    all_to_all x1, blocking collectives: 31.3 us -> 33.7 us  [shards(): lax.all_to_all(picked.reshape(box_total, per_owner, NORB), ('row', 'col')...]
    ppermute x6 -> x8, starting transfers between devices: 3.7 us -> 3.57 us  [swap(): return lax.ppermute(rows, 'col', [(i, i ^ mask) for i in range(col_count)])]
    pallas_call x10 -> x11, Pallas kernels: 8.11 us -> 8.13 us  [local(): pl.pallas_call(kernel, out_shape=out, in_specs=[spec(n, a) for n, a in en...]
  transfers between devices with their start and end apart: 14 -> 16, of which waited for: 10 -> 10; matrix products, arithmetic and copies ran while one was open for 2% -> 2% of each run, Pallas kernels for 7% -> 8%
where the time goes in v5:
time: 107 us
  waiting for transfers between devices  40.2 us (38%)
  blocking collectives  33.7 us (31%)
  starting transfers between devices  16.3 us (15%)
  Pallas kernels  14.6 us (14%)
  other arithmetic  1.73 us (2%)
    all_to_all x1, blocking collectives, shards(): lax.all_to_all(picked.reshape(box_total, per_owner, NORB), ('row', 'col')...  33.7 us
    all_to_all x1, waiting for transfers between devices, shards(): lax.all_to_all(outgoing, ('row', 'col'), split_axis=0, concat_axis=0, til...  20.2 us
    ppermute x8, waiting for transfers between devices, swap(): return lax.ppermute(rows, 'col', [(i, i ^ mask) for i in range(col_count)])  12.9 us
    pallas_call x11, Pallas kernels, local(): pl.pallas_call(kernel, out_shape=out, in_specs=[spec(n, a) for n, a in en...  8.13 us
    ppermute x7, waiting for transfers between devices, flip(): return lax.ppermute(rows, 'row', [(i, i ^ mask) for i in range(row_count)])  7.12 us
    all_to_all x1, starting transfers between devices, shards(): lax.all_to_all(outgoing, ('row', 'col'), split_axis=0, concat_axis=0, til...  7.1 us
    ppermute x7, starting transfers between devices, flip(): return lax.ppermute(rows, 'row', [(i, i ^ mask) for i in range(row_count)])  5.59 us
    ppermute x8, starting transfers between devices, swap(): return lax.ppermute(rows, 'col', [(i, i ^ mask) for i in range(col_count)])  3.57 us
  transfers between devices with their start and end apart: 16, of which 10 were waited for; matrix products, arithmetic and copies ran while one was open for 2% of the time, Pallas kernels for 8%

profile of v5, /device:TPU:1, one launch (start us, length us, event | category | flops | bytes accessed | tf_op | source)
XLA Modules:
  0.0 106.9 jit_solution(6163749133037686427)
XLA Ops:
  0.0 3.4 %shard_map.73 = bf16[32,104,128]{2,1,0:T(8,128)(2,1)} custom-call(s32[32]{0:T(128)} %counts_hbm.1, s32[8,128]{1,0:T(8,128)} %bitcast.13, s32[64,128]{1,0:T(8,128)} %bitcast.10, s32[8,128]{1,0:T(8,128)} %bitcast.14, bf16[1024,512]{1,0:T(8,128)(2,1)} %orbitals_hbm.1), custom_call_target="tpu_custom_call" | custom-call | flops 805306368 | bytes 2097152 | tf_op jit(solution)/shard_map/pallas_call | solution.py:281
  3.5 7.1 %all-to-all-start = ((bf16[32,104,128]{2,1,0:T(8,128)(2,1)}), bf16[32,104,128]{2,1,0:T(8,128)(2,1)S(1)}, u32[]{:S(2)}, u32[]{:S(2)}) async-start(bf16[32,104,128]{2,1,0:T(8,128)(2,1)} %shard_map.73), calls=%async_computation | async-start | bytes 1703936 | tf_op jit(solution)/shard_map/all_to_all | solution.py:305
  10.9 1.2 %select_reduce_fusion = s32[256]{0:T(256)S(1)} fusion(s32[8192]{0:T(1024)S(1)} %copy-done.1, s32[256]{0:T(256)S(1)} %iota_add_fusion), kind=kLoop, calls=%fused_computation | loop fusion | flops 6291200 | bytes 34816 | tf_op jit(solution)/shard_map/reduce_sum | solution.py:311
  12.6 20.2 %all-to-all-done.received = bf16[32,104,128]{2,1,0:T(8,128)(2,1)S(1)} async-done(((bf16[32,104,128]{2,1,0:T(8,128)(2,1)}), bf16[32,104,128]{2,1,0:T(8,128)(2,1)S(1)}, u32[]{:S(2)}, u32[]{:S(2)}) %all-to-all-start) | async-done | bytes 852000 | tf_op jit(solution)/shard_map/all_to_all | solution.py:305
  33.2 1.3 %collective-permute-start = (bf16[256,512]{1,0:T(8,128)(2,1)S(1)}, bf16[256,512]{1,0:T(8,128)(2,1)S(1)}, u32[]{:S(2)}, u32[]{:S(2)}) collective-permute-start(bf16[256,512]{1,0:T(8,128)(2,1)S(1)} %get-tuple-element.28.refs_0_.left), channel_id=1, source_target_pairs={{0,8},{4,12},{8,0},{12,4},{16,24},{20,28},{24,16},{28,20},{1,9},{5... | collective-permute-start | bytes 786440 | tf_op jit(solution)/shard_map/ppermute | solution.py:338
  34.7 0.6 collective-permute-start.4
  35.6 5.5 %collective-permute-done.refs_0_ = bf16[256,512]{1,0:T(8,128)(2,1)S(1)} collective-permute-done((bf16[256,512]{1,0:T(8,128)(2,1)S(1)}, bf16[256,512]{1,0:T(8,128)(2,1)S(1)}, u32[]{:S(2)}, u32[]{:S(2)}) %collective-permute-start) | collective-permute-done | bytes 262176 | tf_op jit(solution)/shard_map/ppermute | solution.py:338
  41.1 1.3 %collective-permute-start.2 = (bf16[128,512]{1,0:T(8,128)(2,1)S(1)}, bf16[128,512]{1,0:T(8,128)(2,1)S(1)}, u32[]{:S(2)}, u32[]{:S(2)}) collective-permute-start(bf16[128,512]{1,0:T(8,128)(2,1)S(1)} %slice.8), channel_id=1, source_target_pairs={{0,16},{4,20},{8,24},{12,28},{16,0},{20,4},{24,8},{28,12},{1,17},{... | collective-permute-start | bytes 393224 | tf_op jit(solution)/shard_map/ppermute | solution.py:338
  42.9 2.8 %shard_map.78 = (bf16[256,2048]{1,0:T(8,128)(2,1)S(1)}, bf16[256,2048]{1,0:T(8,128)(2,1)S(1)}, bf16[256,2048]{1,0:T(8,128)(2,1)S(1)}, bf16[256,2048]{1,0:T(8,128)(2,1)S(1)}) custom-call(s32[4]{0:T(128)S(1)} %iota_xor_fusion.scalars, bf16[1024,2048]{1,0:T(8,128)(2,1)} %coulomb.1), custom_call_target="tpu_custom_call" | custom-call | tf_op jit(solution)/shard_map/pallas_call | solution.py:220
  45.7 1.3 %collective-permute-start.6 = (bf16[256,512]{1,0:T(8,128)(2,1)S(1)}, bf16[256,512]{1,0:T(8,128)(2,1)S(1)}, u32[]{:S(2)}, u32[]{:S(2)}) collective-permute-start(bf16[256,512]{1,0:T(8,128)(2,1)S(1)} %get-tuple-element.28.refs_0_.left), channel_id=1, source_target_pairs={{0,4},{4,0},{8,12},{12,8},{16,20},{20,16},{24,28},{28,24},{1,5},{5... | collective-permute-start | bytes 786440 | tf_op jit(solution)/shard_map/ppermute | solution.py:338
  47.6 1.0 collective-permute-start.8
  48.8 1.0 collective-permute-done.8.refs_5_
  50.0 1.3 %shard_map.81 = (bf16[160,512]{1,0:T(8,128)(2,1)S(1)}, f32[96,512]{1,0:T(8,128)S(1)}) custom-call(bf16[256,512]{1,0:T(8,128)(2,1)S(1)} %get-tuple-element.38.left, bf16[2048,512]{1,0:T(8,128)(2,1)S(1)} %shard_map.80.right, bf16[256,2048]{1,0:T(8,128)(2,1)S(1)} %get-tuple-element.39.tile), custom_call_target="tpu_custom_call" | custom-call | tf_op jit(solution)/shard_map/pallas_call | solution.py:220
  51.6 3.1 %collective-permute-done.10.left = bf16[256,512]{1,0:T(8,128)(2,1)S(1)} collective-permute-done((bf16[256,512]{1,0:T(8,128)(2,1)S(1)}, bf16[256,512]{1,0:T(8,128)(2,1)S(1)}, u32[]{:S(2)}, u32[]{:S(2)}) %collective-permute-start.10) | collective-permute-done | bytes 262176 | tf_op jit(solution)/shard_map/ppermute | solution.py:331
  54.6 1.3 %shard_map.83 = (bf16[160,512]{1,0:T(8,128)(2,1)S(1)}, bf16[96,512]{1,0:T(8,128)(2,1)S(1)}) custom-call(bf16[256,512]{1,0:T(8,128)(2,1)S(1)} %collective-permute-done.10.left, bf16[2048,512]{1,0:T(8,128)(2,1)S(1)} %shard_map.80.right, bf16[256,2048]{1,0:T(8,128)(2,1)S(1)} %get-tuple-element.42.tile), custom_call_target="tpu_custom_call" | custom-call | tf_op jit(solution)/shard_map/pallas_call | solution.py:220
  56.3 1.5 %collective-permute-start.11 = (bf16[160,512]{1,0:T(8,128)(2,1)S(1)}, bf16[160,512]{1,0:T(8,128)(2,1)S(1)}, u32[]{:S(2)}, u32[]{:S(2)}) collective-permute-start(bf16[160,512]{1,0:T(8,128)(2,1)S(1)} %get-tuple-element.43), channel_id=1, source_target_pairs={{0,3},{1,2},{2,1},{3,0},{4,7},{5,6},{6,5},{7,4},{8,11},{9,10},{10,... | collective-permute-start | bytes 491528 | tf_op jit(solution)/shard_map/ppermute | solution.py:331
  57.7 1.3 %shard_map.85 = bf16[256,512]{1,0:T(8,128)(2,1)S(1)} custom-call(bf16[256,512]{1,0:T(8,128)(2,1)S(1)} %get-tuple-element.47.left, bf16[2048,512]{1,0:T(8,128)(2,1)S(1)} %shard_map.80.right, bf16[256,2048]{1,0:T(8,128)(2,1)S(1)} %get-tuple-element.48.tile), custom_call_target="tpu_custom_call" | custom-call | tf_op jit(solution)/shard_map/pallas_call | solution.py:220
  59.1 2.0 %collective-permute-done.12.other = bf16[96,512]{1,0:T(8,128)(2,1)S(1)} collective-permute-done((bf16[96,512]{1,0:T(8,128)(2,1)S(1)}, bf16[96,512]{1,0:T(8,128)(2,1)S(1)}, u32[]{:S(2)}, u32[]{:S(2)}) %collective-permute-start.12) | collective-permute-done | bytes 98336 | tf_op jit(solution)/shard_map/ppermute | solution.py:331
  61.5 1.3 %shard_map.82.own = f32[256,512]{1,0:T(8,128)S(1)} custom-call(bf16[256,512]{1,0:T(8,128)(2,1)S(1)} %get-tuple-element.28.refs_0_.left, bf16[2048,512]{1,0:T(8,128)(2,1)S(1)} %shard_map.80.right, bf16[256,2048]{1,0:T(8,128)(2,1)S(1)} %get-tuple-element.37.tile, bf16[160,512]{1,0:T(8,128)(2,1)S(1)} %collective-permute-done.9.refs_0_), custom_call_target="tpu_custom_call" | custom-call | flops 10000000000 | tf_op jit(solution)/shard_map/pallas_call | solution.py:220
  63.2 3.9 %collective-permute-done.13.refs_1_ = bf16[96,512]{1,0:T(8,128)(2,1)S(1)} collective-permute-done((bf16[96,512]{1,0:T(8,128)(2,1)S(1)}, bf16[96,512]{1,0:T(8,128)(2,1)S(1)}, u32[]{:S(2)}, u32[]{:S(2)}) %collective-permute-start.13) | collective-permute-done | bytes 98336 | tf_op jit(solution)/shard_map/ppermute | solution.py:331
  67.1 3.5 %collective-permute-done.14.refs_2_ = bf16[256,512]{1,0:T(8,128)(2,1)S(1)} collective-permute-done((bf16[256,512]{1,0:T(8,128)(2,1)S(1)}, bf16[256,512]{1,0:T(8,128)(2,1)S(1)}, u32[]{:S(2)}, u32[]{:S(2)}) %collective-permute-start.14) | collective-permute-done | bytes 262176 | tf_op jit(solution)/shard_map/ppermute | solution.py:331
  70.6 0.5 shard_map.86
  71.1 33.7 %all_to_all.10 = bf16[32,32,512]{2,1,0:T(8,128)(2,1)S(1)} all-to-all(bf16[32,32,512]{2,1,0:T(8,128)(2,1)S(1)} %bitcast.9), channel_id=1, replica_groups=mesh['row'=8,'col'=4] {'row','col'}, dimensions={0} | all-to-all | bytes 2097152 | tf_op jit(solution)/shard_map/all_to_all | solution.py:416
  104.8 2.1 %shard_map.87 = f32[1024,512]{1,0:T(8,128)} custom-call(bf16[1024,1024]{1,0:T(8,128)(2,1)S(1)} %copy-done, bf16[1024,512]{1,0:T(8,128)(2,1)S(1)} %bitcast.8), custom_call_target="tpu_custom_call" | custom-call | tf_op jit(solution)/shard_map/pallas_call | solution.py:424
  (42 shorter events, 4.7 us)
Async XLA Ops:
  0.0 10.6 %copy-start.2 = (s32[32]{0:T(128)S(1)}, s32[32]{0:T(128)}, u32[]{:S(2)}) copy-start(s32[32]{0:T(128)} %counts_hbm.1) | copy-start | bytes 388
  0.0 10.9 %copy-start.1 = (s32[8192]{0:T(1024)S(1)}, s32[8192]{0:T(1024)}, u32[]{:S(2)}) copy-start(s32[8192]{0:T(1024)} %param.11) | copy-start | bytes 98308
  3.5 29.3 %all-to-all-start = ((bf16[32,104,128]{2,1,0:T(8,128)(2,1)}), bf16[32,104,128]{2,1,0:T(8,128)(2,1)S(1)}, u32[]{:S(2)}, u32[]{:S(2)}) async-start(bf16[32,104,128]{2,1,0:T(8,128)(2,1)} %shard_map.73), calls=%async_computation | async-start | bytes 1703936 | tf_op jit(solution)/shard_map/all_to_all | solution.py:305
  33.2 7.9 %collective-permute-start = (bf16[256,512]{1,0:T(8,128)(2,1)S(1)}, bf16[256,512]{1,0:T(8,128)(2,1)S(1)}, u32[]{:S(2)}, u32[]{:S(2)}) collective-permute-start(bf16[256,512]{1,0:T(8,128)(2,1)S(1)} %get-tuple-element.28.refs_0_.left), channel_id=1, source_target_pairs={{0,8},{4,12},{8,0},{12,4},{16,24},{20,28},{24,16},{28,20},{1,9},{5... | collective-permute-start | bytes 786440 | tf_op jit(solution)/shard_map/ppermute | solution.py:338
  34.5 8.1 %collective-permute-start.1 = (bf16[256,512]{1,0:T(8,128)(2,1)S(1)}, bf16[256,512]{1,0:T(8,128)(2,1)S(1)}, u32[]{:S(2)}, u32[]{:S(2)}) collective-permute-start(bf16[256,512]{1,0:T(8,128)(2,1)S(1)} %get-tuple-element.28.refs_0_.left), channel_id=1, source_target_pairs={{0,16},{4,20},{8,24},{12,28},{16,0},{20,4},{24,8},{28,12},{1,17},{... | collective-permute-start | bytes 786440 | tf_op jit(solution)/shard_map/ppermute | solution.py:338
  34.7 13.9 %collective-permute-start.4 = (bf16[256,512]{1,0:T(8,128)(2,1)S(1)}, bf16[256,512]{1,0:T(8,128)(2,1)S(1)}, u32[]{:S(2)}, u32[]{:S(2)}) collective-permute-start(bf16[256,512]{1,0:T(8,128)(2,1)S(1)} %get-tuple-element.28.refs_0_.left), channel_id=1, source_target_pairs={{0,1},{1,0},{2,3},{3,2},{4,5},{5,4},{6,7},{7,6},{8,9},{9,8},{10,11... | collective-permute-start | bytes 786440 | tf_op jit(solution)/shard_map/ppermute | solution.py:331
  35.3 13.3 %collective-permute-start.5 = (bf16[256,512]{1,0:T(8,128)(2,1)S(1)}, bf16[256,512]{1,0:T(8,128)(2,1)S(1)}, u32[]{:S(2)}, u32[]{:S(2)}) collective-permute-start(bf16[256,512]{1,0:T(8,128)(2,1)S(1)} %get-tuple-element.28.refs_0_.left), channel_id=1, source_target_pairs={{0,2},{1,3},{2,0},{3,1},{4,6},{5,7},{6,4},{7,5},{8,10},{9,11},{10,... | collective-permute-start | bytes 786440 | tf_op jit(solution)/shard_map/ppermute | solution.py:331
  41.1 5.9 %collective-permute-start.2 = (bf16[128,512]{1,0:T(8,128)(2,1)S(1)}, bf16[128,512]{1,0:T(8,128)(2,1)S(1)}, u32[]{:S(2)}, u32[]{:S(2)}) collective-permute-start(bf16[128,512]{1,0:T(8,128)(2,1)S(1)} %slice.8), channel_id=1, source_target_pairs={{0,16},{4,20},{8,24},{12,28},{16,0},{20,4},{24,8},{28,12},{1,17},{... | collective-permute-start | bytes 393224 | tf_op jit(solution)/shard_map/ppermute | solution.py:338
  42.6 5.0 %collective-permute-start.3 = (bf16[128,512]{1,0:T(8,128)(2,1)S(1)}, bf16[128,512]{1,0:T(8,128)(2,1)S(1)}, u32[]{:S(2)}, u32[]{:S(2)}) collective-permute-start(bf16[128,512]{1,0:T(8,128)(2,1)S(1)} %slice.9), channel_id=1, source_target_pairs={{0,8},{4,12},{8,0},{12,4},{16,24},{20,28},{24,16},{28,20},{1,9},{5... | collective-permute-start | bytes 393224 | tf_op jit(solution)/shard_map/ppermute | solution.py:338
  45.7 3.0 %collective-permute-start.6 = (bf16[256,512]{1,0:T(8,128)(2,1)S(1)}, bf16[256,512]{1,0:T(8,128)(2,1)S(1)}, u32[]{:S(2)}, u32[]{:S(2)}) collective-permute-start(bf16[256,512]{1,0:T(8,128)(2,1)S(1)} %get-tuple-element.28.refs_0_.left), channel_id=1, source_target_pairs={{0,4},{4,0},{8,12},{12,8},{16,20},{20,16},{24,28},{28,24},{1,5},{5... | collective-permute-start | bytes 786440 | tf_op jit(solution)/shard_map/ppermute | solution.py:338
  47.1 2.8 %collective-permute-start.7 = (bf16[512,512]{1,0:T(8,128)(2,1)S(1)}, bf16[512,512]{1,0:T(8,128)(2,1)S(1)}, u32[]{:S(2)}, u32[]{:S(2)}) collective-permute-start(bf16[512,512]{1,0:T(8,128)(2,1)S(1)} %shard_map.75.refs_1_), channel_id=1, source_target_pairs={{0,4},{4,0},{8,12},{12,8},{16,20},{20,16},{24,28},{28,24},{1,5},{5... | collective-permute-start | bytes 1572872 | tf_op jit(solution)/shard_map/ppermute | solution.py:338
  47.6 2.2 %collective-permute-start.8 = (bf16[256,512]{1,0:T(8,128)(2,1)S(1)}, bf16[256,512]{1,0:T(8,128)(2,1)S(1)}, u32[]{:S(2)}, u32[]{:S(2)}) collective-permute-start(bf16[256,512]{1,0:T(8,128)(2,1)S(1)} %shard_map.77.refs_2_), channel_id=1, source_target_pairs={{0,4},{4,0},{8,12},{12,8},{16,20},{20,16},{24,28},{28,24},{1,5},{5... | collective-permute-start | bytes 786440 | tf_op jit(solution)/shard_map/ppermute | solution.py:338
  48.7 5.9 %collective-permute-start.10 = (bf16[256,512]{1,0:T(8,128)(2,1)S(1)}, bf16[256,512]{1,0:T(8,128)(2,1)S(1)}, u32[]{:S(2)}, u32[]{:S(2)}) collective-permute-start(bf16[256,512]{1,0:T(8,128)(2,1)S(1)} %get-tuple-element.38.left), channel_id=1, source_target_pairs={{0,1},{1,0},{2,3},{3,2},{4,5},{5,4},{6,7},{7,6},{8,9},{9,8},{10,11... | collective-permute-start | bytes 786440 | tf_op jit(solution)/shard_map/ppermute | solution.py:331
  51.3 10.3 %collective-permute-start.9 = (bf16[160,512]{1,0:T(8,128)(2,1)S(1)}, bf16[160,512]{1,0:T(8,128)(2,1)S(1)}, u32[]{:S(2)}, u32[]{:S(2)}) collective-permute-start(bf16[160,512]{1,0:T(8,128)(2,1)S(1)} %get-tuple-element.40), channel_id=1, source_target_pairs={{0,2},{1,3},{2,0},{3,1},{4,6},{5,7},{6,4},{7,5},{8,10},{9,11},{10,... | collective-permute-start | bytes 491528 | tf_op jit(solution)/shard_map/ppermute | solution.py:331
  55.9 5.2 %collective-permute-start.12 = (bf16[96,512]{1,0:T(8,128)(2,1)S(1)}, bf16[96,512]{1,0:T(8,128)(2,1)S(1)}, u32[]{:S(2)}, u32[]{:S(2)}) collective-permute-start(bf16[96,512]{1,0:T(8,128)(2,1)S(1)} %get-tuple-element.45), channel_id=1, source_target_pairs={{0,1},{1,0},{2,3},{3,2},{4,5},{5,4},{6,7},{7,6},{8,9},{9,8},{10,11... | collective-permute-start | bytes 294920 | tf_op jit(solution)/shard_map/ppermute | solution.py:331
  56.3 6.9 %collective-permute-start.11 = (bf16[160,512]{1,0:T(8,128)(2,1)S(1)}, bf16[160,512]{1,0:T(8,128)(2,1)S(1)}, u32[]{:S(2)}, u32[]{:S(2)}) collective-permute-start(bf16[160,512]{1,0:T(8,128)(2,1)S(1)} %get-tuple-element.43), channel_id=1, source_target_pairs={{0,3},{1,2},{2,1},{3,0},{4,7},{5,6},{6,5},{7,4},{8,11},{9,10},{10,... | collective-permute-start | bytes 491528 | tf_op jit(solution)/shard_map/ppermute | solution.py:331
  59.0 11.6 %collective-permute-start.14 = (bf16[256,512]{1,0:T(8,128)(2,1)S(1)}, bf16[256,512]{1,0:T(8,128)(2,1)S(1)}, u32[]{:S(2)}, u32[]{:S(2)}) collective-permute-start(bf16[256,512]{1,0:T(8,128)(2,1)S(1)} %shard_map.85), channel_id=1, source_target_pairs={{0,1},{1,0},{2,3},{3,2},{4,5},{5,4},{6,7},{7,6},{8,9},{9,8},{10,11... | collective-permute-start | bytes 786440 | tf_op jit(solution)/shard_map/ppermute | solution.py:331
  61.1 5.9 %collective-permute-start.13 = (bf16[96,512]{1,0:T(8,128)(2,1)S(1)}, bf16[96,512]{1,0:T(8,128)(2,1)S(1)}, u32[]{:S(2)}, u32[]{:S(2)}) collective-permute-start(bf16[96,512]{1,0:T(8,128)(2,1)S(1)} %shard_map.84), channel_id=1, source_target_pairs={{0,2},{1,3},{2,0},{3,1},{4,6},{5,7},{6,4},{7,5},{8,10},{9,11},{10,... | collective-permute-start | bytes 294920 | tf_op jit(solution)/shard_map/ppermute | solution.py:331
  62.8 42.0 %copy-start = (bf16[1024,1024]{1,0:T(8,128)(2,1)S(1)}, bf16[1024,1024]{1,0:T(8,128)(2,1)}, u32[]{:S(2)}) copy-start(bf16[1024,1024]{1,0:T(8,128)(2,1)} %interp.1) | copy-start | bytes 6291460

commit v6 on v5

--- a/solution.py
+++ b/solution.py
@@ -12,7 +12,7 @@
 OWN = 256
 SLOTS = 768
 LANES = 128
-UPPER = 160
+CUT = 96
 VMEM_LIMIT = 48 * 1024 * 1024
 PICK_LIMIT = 60 * 1024 * 1024
 
@@ -111,23 +111,29 @@
             hot.astype(jnp.float32).astype(jnp.bfloat16),
             orbitals[...],
             preferred_element_type=jnp.float32,
-        ).astype(jnp.bfloat16)
+        )
+        owners = step // capacity
+        packed = jnp.concatenate(
+            [
+                rows[:, c : c + LANES].reshape(owners, capacity, LANES)
+                for c in range(0, NORB, LANES)
+            ],
+            axis=1,
+        )
         first_owner = t // capacity
-        for c in range(NORB // LANES):
-            out[
-                first_owner : first_owner + step // capacity, c * capacity : (c + 1) * capacity, :
-            ] = rows[:, c * LANES : (c + 1) * LANES].reshape(step // capacity, capacity, LANES)
+        out[first_owner : first_owner + owners, : packed.shape[1], :] = packed.astype(jnp.bfloat16)
 
 
 def place_kernel(capacity, index, received, out, wanted):
     boxes = received.shape[0]
+    packed = received[:, : capacity * (NORB // LANES), :].astype(jnp.float32)
     rows = jnp.concatenate(
         [
-            received[:, c * capacity : (c + 1) * capacity, :].reshape(boxes * capacity, LANES)
+            packed[:, c * capacity : (c + 1) * capacity, :].reshape(boxes * capacity, LANES)
             for c in range(NORB // LANES)
         ],
         axis=1,
-    )
+    ).astype(jnp.bfloat16)
     hot = index[...] == lax.broadcasted_iota(jnp.int32, (index.shape[0], rows.shape[0]), 1)
     out[...] = jnp.dot(
         hot.astype(jnp.float32).astype(jnp.bfloat16), rows, preferred_element_type=jnp.float32
@@ -175,39 +181,43 @@
         copy.wait()
 
 
-def block_kernel(count, left, right, tile, *refs):
-    earlier, outs, weighted = refs[: -1 - count], refs[-1 - count : -1], refs[-1]
+def block_kernel(count, spans, at, *refs):
+    lefts, right, tile = refs[:count], refs[count], refs[count + 1]
+    earlier, outs, weighted = refs[count + 2 : -1 - len(spans)], refs[-1 - len(spans) : -1], refs[-1]
+    left = jnp.concatenate([ref[...] for ref in lefts]) if count > 1 else lefts[0][...]
+    rows = slice(at, at + left.shape[0])
     step = 512
     for t in range(0, right.shape[0], step):
-        pair = pair_block(left[...], right[t : t + step, :]).astype(jnp.float32)
+        pair = pair_block(left, right[t : t + step, :]).astype(jnp.float32)
         weighted[:, t : t + step] = (
-            pair * tile[:, t : t + step].astype(jnp.float32)
+            pair * tile[rows, t : t + step].astype(jnp.float32)
         ).astype(jnp.bfloat16)
     total = jnp.dot(weighted[...], right[...], preferred_element_type=jnp.float32)
-    at = 0
-    for out in outs:
-        rows = out.shape[0]
-        out[...] = total[at : at + rows, :].astype(out.dtype)
-        at += rows
+    for out, (low, high) in zip(outs, spans):
+        out[...] = total[low:high, :].astype(out.dtype)
     for ref in earlier:
-        rows = ref.shape[0]
-        outs[0][:rows, :] = total[:rows, :] + ref[...].astype(jnp.float32)
+        low = total.shape[0] - ref.shape[0]
+        outs[0][low:, :] = total[low:, :] + ref[...].astype(jnp.float32)
 
 
 def add_kernel(one, other, out):
     out[...] = (one[...] + other[...].astype(jnp.float32)).astype(out.dtype)
 
 
-def block_sum(left, right, tile, *parts, earlier=(), flops=0):
+def block_sum(lefts, right, tile, *parts, at=0, earlier=(), flops=0):
+    spans, low = [], 0
+    for rows, _ in parts:
+        spans.append((low, low + rows))
+        low += rows
     return local(
-        functools.partial(block_kernel, len(parts)),
+        functools.partial(block_kernel, len(lefts), spans, at),
         tuple(jax.ShapeDtypeStruct((rows, NORB), dtype) for rows, dtype in parts),
-        left,
+        *lefts,
         right,
         tile,
         *earlier,
         flops=flops,
-        scratch=[pltpu.VMEM((OWN, right.shape[0]), jnp.bfloat16)],
+        scratch=[pltpu.VMEM((low, right.shape[0]), jnp.bfloat16)],
     )
 
 
@@ -228,7 +238,7 @@
     )(*args)
 
 
-def select_kernel(per_owner, index, own, *refs):
+def select_kernel(per_owner, firsts, index, own, *refs):
     boxes = index.shape[0]
     spread = jnp.broadcast_to(index[...][:, None, :], (boxes, per_owner, LANES))
     diagonal = lax.broadcasted_iota(jnp.int32, spread.shape, 1) == lax.broadcasted_iota(
@@ -238,13 +248,11 @@
     picks = picks.reshape(boxes * per_owner, 1).astype(jnp.int32)
     out = refs[-1]
     totals = []
-    for rows in (slice(0, UPPER), slice(UPPER, OWN)):
-        total = own[rows, :]
-        for ref in refs[:-1]:
-            if ref.shape[0] == OWN:
-                total = total + ref[rows, :].astype(jnp.float32)
-            elif ref.shape[0] == rows.stop - rows.start:
-                total = total + ref[...].astype(jnp.float32)
+    for low, high in ((0, CUT), (CUT, OWN)):
+        total = own[low:high, :]
+        for ref, first in zip(refs[:-1], firsts):
+            if first <= low < first + ref.shape[0]:
+                total = total + ref[low - first : high - first, :].astype(jnp.float32)
         totals.append(total.astype(jnp.bfloat16))
     projected = jnp.concatenate(totals)
     hot = picks == lax.broadcasted_iota(jnp.int32, (boxes * per_owner, OWN), 1)
@@ -337,13 +345,13 @@
     def flip(rows, mask):
         return lax.ppermute(rows, "row", [(i, i ^ mask) for i in range(row_count)])
 
-    left = {0: owned_rows}
+    half = OWN // 2
+    left = {0: [owned_rows]}
     for mask in range(1, col_count):
         if mask & (mask - 1) == 0:
-            left[mask] = swap(owned_rows, mask)
+            left[mask] = [swap(owned_rows, mask)]
 
     whole = {0: owned_rows}
-    half = OWN // 2
     single = [1 << b for b in range(1, row_count.bit_length() - 1)]
     double = [mask for mask in range(2, row_count, 2) if mask not in single]
     for mask in single:
@@ -373,15 +381,17 @@
     held = local(
         hold_kernel,
         tuple(shape(owned_rows.shape, owned_rows.dtype) for _ in direct),
-        *[left[mask] for mask in direct],
+        *[left[mask][0] for mask in direct],
         flops=20 * 10**9,
     )
     *held, mirrored[0] = lax.optimization_barrier((*held, mirrored[0]))
-    left.update(zip(direct, held))
-    for mask in range(1, col_count):
+    left.update((mask, [rows]) for mask, rows in zip(direct, held))
+    for mask in range(3, col_count):
         if mask not in left:
             low = mask & -mask
-            left[mask] = swap(left[mask ^ low], low)
+            (rows,) = left[mask ^ low]
+            parts = [rows[:CUT], rows[CUT:]] if mask == 3 else [rows]
+            left[mask] = [swap(part, low) for part in parts]
 
     right = local(
         functools.partial(order_kernel, masks),
@@ -394,25 +404,30 @@
         return block_sum(left[mask], right, tiles[mask], *parts, **options)
 
     short, wide = jnp.bfloat16, jnp.float32
-    upper_two, lower_two = partial_sum(2, (UPPER, short), (OWN - UPPER, wide))
-    left[3], _ = lax.optimization_barrier((left[3], upper_two))
-    upper_three, lower_three = partial_sum(3, (UPPER, short), (OWN - UPPER, short))
-    first = swap(upper_two, 2)
-    handed = swap(lower_three, 1)
-    arrived = [swap(upper_three, 3)]
-    lower = local(add_kernel, shape(lower_two.shape, short), lower_two, handed)
-    arrived.append(swap(lower, 2))
-    left[1], _ = lax.optimization_barrier((left[1], upper_three))
+    first_two, last_two = partial_sum(2, (CUT, wide), (OWN - CUT, short))
+    last_two_there = swap(last_two, 2)
+    first, last = left[3]
+    first, _ = lax.optimization_barrier((first, last_two))
+    (first_three,) = block_sum([first], right, tiles[3], (CUT, short))
+    handed = swap(first_three, 1)
+    last, _ = lax.optimization_barrier((last, first_three))
+    (last_three,) = block_sum([last], right, tiles[3], (OWN - CUT, short), at=CUT)
+    arrived, firsts = [swap(last_three, 3)], [CUT]
+    first_both = local(add_kernel, shape(first_two.shape, short), first_two, handed)
+    arrived.append(swap(first_both, 2))
+    firsts.append(0)
+    left[1][0], _ = lax.optimization_barrier((left[1][0], last_three))
     for mask in [1, *range(4, col_count)]:
         arrived.append(swap(partial_sum(mask, (OWN, short))[0], mask))
-    (own_sum,) = partial_sum(0, (OWN, wide), earlier=[first], flops=10**10)
-    picked = pl.pallas_call(
-        functools.partial(select_kernel, per_owner),
-        out_shape=jax.ShapeDtypeStruct((LIST, NORB), jnp.bfloat16),
-        in_specs=[vmem()] * (2 + len(arrived)),
-        out_specs=vmem(),
-        compiler_params=params(),
-    )(wanted, own_sum, *arrived)
+        firsts.append(0)
+    (own_sum,) = partial_sum(0, (OWN, wide), earlier=[last_two_there], flops=10**10)
+    picked = local(
+        functools.partial(select_kernel, per_owner, firsts),
+        shape((LIST, NORB), jnp.bfloat16),
+        wanted,
+        own_sum,
+        *arrived,
+    )
     chosen = lax.all_to_all(
         picked.reshape(box_total, per_owner, NORB),
         ("row", "col"),

time: 107 us -> 107 us (level)
  waiting for transfers between devices: 40.2 us -> 36.7 us
  starting transfers between devices: 16.3 us -> 19 us
    ppermute x8 -> x9, starting transfers between devices: 3.57 us -> 6.35 us  [swap(): return lax.ppermute(rows, 'col', [(i, i ^ mask) for i in range(col_count)])]
    ppermute x8 -> x9, waiting for transfers between devices: 12.9 us -> 10.4 us  [swap(): return lax.ppermute(rows, 'col', [(i, i ^ mask) for i in range(col_count)])]
    pallas_call x11 -> x13, Pallas kernels: 8.13 us -> 9.63 us  [local(): pl.pallas_call(kernel, out_shape=out, in_specs=[spec(n, a) for n, a in en...]
  transfers between devices with their start and end apart: 16 -> 17, of which waited for: 10 -> 9; matrix products, arithmetic and copies ran while one was open for 2% -> 2% of each run, Pallas kernels for 8% -> 9%
where the time goes in v6:
time: 107 us
  waiting for transfers between devices  36.7 us (34%)
  blocking collectives  33 us (31%)
  starting transfers between devices  19 us (18%)
  Pallas kernels  15.6 us (15%)
  other arithmetic  1.73 us (2%)
    all_to_all x1, blocking collectives, shards(): lax.all_to_all(picked.reshape(box_total, per_owner, NORB), ('row', 'col')...  33 us
    all_to_all x1, waiting for transfers between devices, shards(): lax.all_to_all(outgoing, ('row', 'col'), split_axis=0, concat_axis=0, til...  20.2 us
    ppermute x9, waiting for transfers between devices, swap(): return lax.ppermute(rows, 'col', [(i, i ^ mask) for i in range(col_count)])  10.4 us
    pallas_call x13, Pallas kernels, local(): pl.pallas_call(kernel, out_shape=out, in_specs=[spec(n, a) for n, a in en...  9.63 us
    all_to_all x1, starting transfers between devices, shards(): lax.all_to_all(outgoing, ('row', 'col'), split_axis=0, concat_axis=0, til...  7.1 us
    ppermute x9, starting transfers between devices, swap(): return lax.ppermute(rows, 'col', [(i, i ^ mask) for i in range(col_count)])  6.35 us
    ppermute x7, waiting for transfers between devices, flip(): return lax.ppermute(rows, 'row', [(i, i ^ mask) for i in range(row_count)])  6.11 us
    ppermute x7, starting transfers between devices, flip(): return lax.ppermute(rows, 'row', [(i, i ^ mask) for i in range(row_count)])  5.59 us
  transfers between devices with their start and end apart: 17, of which 9 were waited for; matrix products, arithmetic and copies ran while one was open for 2% of the time, Pallas kernels for 9%

profile of v6, /device:TPU:1, one launch (start us, length us, event | category | flops | bytes accessed | tf_op | source)
XLA Modules:
  0.0 106.5 jit_solution(12723679307873727728)
XLA Ops:
  0.0 3.4 %shard_map.73 = bf16[32,104,128]{2,1,0:T(8,128)(2,1)} custom-call(s32[32]{0:T(128)} %counts_hbm.1, s32[8,128]{1,0:T(8,128)} %bitcast.13, s32[64,128]{1,0:T(8,128)} %bitcast.10, s32[8,128]{1,0:T(8,128)} %bitcast.14, bf16[1024,512]{1,0:T(8,128)(2,1)} %orbitals_hbm.1), custom_call_target="tpu_custom_call" | custom-call | flops 805306368 | bytes 2097152 | tf_op jit(solution)/shard_map/pallas_call | solution.py:289
  3.5 7.1 %all-to-all-start = ((bf16[32,104,128]{2,1,0:T(8,128)(2,1)}), bf16[32,104,128]{2,1,0:T(8,128)(2,1)S(1)}, u32[]{:S(2)}, u32[]{:S(2)}) async-start(bf16[32,104,128]{2,1,0:T(8,128)(2,1)} %shard_map.73), calls=%async_computation | async-start | bytes 1703936 | tf_op jit(solution)/shard_map/all_to_all | solution.py:313
  10.9 1.2 %select_reduce_fusion = s32[256]{0:T(256)S(1)} fusion(s32[8192]{0:T(1024)S(1)} %copy-done.1, s32[256]{0:T(256)S(1)} %iota_add_fusion), kind=kLoop, calls=%fused_computation | loop fusion | flops 6291200 | bytes 34816 | tf_op jit(solution)/shard_map/reduce_sum | solution.py:319
  12.6 20.2 %all-to-all-done.received = bf16[32,104,128]{2,1,0:T(8,128)(2,1)S(1)} async-done(((bf16[32,104,128]{2,1,0:T(8,128)(2,1)}), bf16[32,104,128]{2,1,0:T(8,128)(2,1)S(1)}, u32[]{:S(2)}, u32[]{:S(2)}) %all-to-all-start) | async-done | bytes 852000 | tf_op jit(solution)/shard_map/all_to_all | solution.py:313
  33.2 1.3 %collective-permute-start = (bf16[256,512]{1,0:T(8,128)(2,1)S(1)}, bf16[256,512]{1,0:T(8,128)(2,1)S(1)}, u32[]{:S(2)}, u32[]{:S(2)}) collective-permute-start(bf16[256,512]{1,0:T(8,128)(2,1)S(1)} %get-tuple-element.27.refs_0_), channel_id=1, source_target_pairs={{0,8},{4,12},{8,0},{12,4},{16,24},{20,28},{24,16},{28,20},{1,9},{5... | collective-permute-start | bytes 786440 | tf_op jit(solution)/shard_map/ppermute | solution.py:346
  35.6 5.5 %collective-permute-done.refs_0_ = bf16[256,512]{1,0:T(8,128)(2,1)S(1)} collective-permute-done((bf16[256,512]{1,0:T(8,128)(2,1)S(1)}, bf16[256,512]{1,0:T(8,128)(2,1)S(1)}, u32[]{:S(2)}, u32[]{:S(2)}) %collective-permute-start) | collective-permute-done | bytes 262176 | tf_op jit(solution)/shard_map/ppermute | solution.py:346
  41.1 1.3 %collective-permute-start.2 = (bf16[128,512]{1,0:T(8,128)(2,1)S(1)}, bf16[128,512]{1,0:T(8,128)(2,1)S(1)}, u32[]{:S(2)}, u32[]{:S(2)}) collective-permute-start(bf16[128,512]{1,0:T(8,128)(2,1)S(1)} %slice.16), channel_id=1, source_target_pairs={{0,16},{4,20},{8,24},{12,28},{16,0},{20,4},{24,8},{28,12},{1,17},{... | collective-permute-start | bytes 393224 | tf_op jit(solution)/shard_map/ppermute | solution.py:346
  42.9 2.8 %shard_map.78 = (bf16[256,2048]{1,0:T(8,128)(2,1)S(1)}, bf16[256,2048]{1,0:T(8,128)(2,1)S(1)}, bf16[256,2048]{1,0:T(8,128)(2,1)S(1)}, bf16[256,2048]{1,0:T(8,128)(2,1)S(1)}) custom-call(s32[4]{0:T(128)S(1)} %iota_xor_fusion.scalars, bf16[1024,2048]{1,0:T(8,128)(2,1)} %coulomb.1), custom_call_target="tpu_custom_call" | custom-call | tf_op jit(solution)/shard_map/pallas_call | solution.py:230
  45.7 1.3 %collective-permute-start.6 = (bf16[256,512]{1,0:T(8,128)(2,1)S(1)}, bf16[256,512]{1,0:T(8,128)(2,1)S(1)}, u32[]{:S(2)}, u32[]{:S(2)}) collective-permute-start(bf16[256,512]{1,0:T(8,128)(2,1)S(1)} %get-tuple-element.27.refs_0_), channel_id=1, source_target_pairs={{0,4},{4,0},{8,12},{12,8},{16,20},{20,16},{24,28},{28,24},{1,5},{5... | collective-permute-start | bytes 786440 | tf_op jit(solution)/shard_map/ppermute | solution.py:346
  47.6 1.0 collective-permute-start.8
  48.9 1.5 %collective-permute-start.10 = (bf16[160,512]{1,0:T(8,128)(2,1)S(1)}, bf16[160,512]{1,0:T(8,128)(2,1)S(1)}, u32[]{:S(2)}, u32[]{:S(2)}) collective-permute-start(bf16[160,512]{1,0:T(8,128)(2,1)S(1)} %slice.14), channel_id=1, source_target_pairs={{0,1},{1,0},{2,3},{3,2},{4,5},{5,4},{6,7},{7,6},{8,9},{9,8},{10,11... | collective-permute-start | bytes 491528 | tf_op jit(solution)/shard_map/ppermute | solution.py:339
  50.5 1.3 %shard_map.81 = (f32[96,512]{1,0:T(8,128)S(1)}, bf16[160,512]{1,0:T(8,128)(2,1)S(1)}) custom-call(bf16[256,512]{1,0:T(8,128)(2,1)S(1)} %get-tuple-element.37.refs_0_, bf16[2048,512]{1,0:T(8,128)(2,1)S(1)} %shard_map.80.refs_1_, bf16[256,2048]{1,0:T(8,128)(2,1)S(1)} %get-tuple-element.38.refs_2_), custom_call_target="tpu_custom_call" | custom-call | tf_op jit(solution)/shard_map/pallas_call | solution.py:230
  52.3 1.1 %shard_map.83 = bf16[96,512]{1,0:T(8,128)(2,1)S(1)} custom-call(bf16[96,512]{1,0:T(8,128)(2,1)S(1)} %collective-permute-done.11.refs_0_, bf16[2048,512]{1,0:T(8,128)(2,1)S(1)} %shard_map.80.refs_1_, bf16[256,2048]{1,0:T(8,128)(2,1)S(1)} %get-tuple-element.41.refs_2_), custom_call_target="tpu_custom_call" | custom-call | tf_op jit(solution)/shard_map/pallas_call | solution.py:230
  53.9 0.7 collective-permute-done.10.refs_0_
  54.6 1.2 %shard_map.84 = bf16[160,512]{1,0:T(8,128)(2,1)S(1)} custom-call(bf16[160,512]{1,0:T(8,128)(2,1)S(1)} %collective-permute-done.10.refs_0_, bf16[2048,512]{1,0:T(8,128)(2,1)S(1)} %shard_map.80.refs_1_, bf16[256,2048]{1,0:T(8,128)(2,1)S(1)} %get-tuple-element.41.refs_2_), custom_call_target="tpu_custom_call" | custom-call | tf_op jit(solution)/shard_map/pallas_call | solution.py:230
  55.8 2.0 %collective-permute-start.12 = (bf16[160,512]{1,0:T(8,128)(2,1)S(1)}, bf16[160,512]{1,0:T(8,128)(2,1)S(1)}, u32[]{:S(2)}, u32[]{:S(2)}) collective-permute-start(bf16[160,512]{1,0:T(8,128)(2,1)S(1)} %shard_map.84), channel_id=1, source_target_pairs={{0,3},{1,2},{2,1},{3,0},{4,7},{5,6},{6,5},{7,4},{8,11},{9,10},{10,... | collective-permute-start | bytes 491528 | tf_op jit(solution)/shard_map/ppermute | solution.py:339
  57.8 1.3 %shard_map.86 = bf16[256,512]{1,0:T(8,128)(2,1)S(1)} custom-call(bf16[256,512]{1,0:T(8,128)(2,1)S(1)} %get-tuple-element.45.refs_0_, bf16[2048,512]{1,0:T(8,128)(2,1)S(1)} %shard_map.80.refs_1_, bf16[256,2048]{1,0:T(8,128)(2,1)S(1)} %get-tuple-element.46.refs_2_), custom_call_target="tpu_custom_call" | custom-call | tf_op jit(solution)/shard_map/pallas_call | solution.py:230
  59.2 1.2 %collective-permute-done.13.other = bf16[96,512]{1,0:T(8,128)(2,1)S(1)} collective-permute-done((bf16[96,512]{1,0:T(8,128)(2,1)S(1)}, bf16[96,512]{1,0:T(8,128)(2,1)S(1)}, u32[]{:S(2)}, u32[]{:S(2)}) %collective-permute-start.13) | collective-permute-done | bytes 98336 | tf_op jit(solution)/shard_map/ppermute | solution.py:339
  60.4 0.9 collective-permute-start.14
  61.3 1.3 %shard_map.82.own = f32[256,512]{1,0:T(8,128)S(1)} custom-call(bf16[256,512]{1,0:T(8,128)(2,1)S(1)} %get-tuple-element.27.refs_0_, bf16[2048,512]{1,0:T(8,128)(2,1)S(1)} %shard_map.80.refs_1_, bf16[256,2048]{1,0:T(8,128)(2,1)S(1)} %get-tuple-element.36.refs_2_, bf16[160,512]{1,0:T(8,128)(2,1)S(1)} %collective-permute-done.9.refs_3_), custom_call_target="tpu_custom_call" | custom-call | flops 10000000000 | tf_op jit(solution)/shard_map/pallas_call | solution.py:230
  62.6 1.6 %collective-permute-done.12.refs_0_ = bf16[160,512]{1,0:T(8,128)(2,1)S(1)} collective-permute-done((bf16[160,512]{1,0:T(8,128)(2,1)S(1)}, bf16[160,512]{1,0:T(8,128)(2,1)S(1)}, u32[]{:S(2)}, u32[]{:S(2)}) %collective-permute-start.12) | collective-permute-done | bytes 163872 | tf_op jit(solution)/shard_map/ppermute | solution.py:339
  64.2 6.8 %collective-permute-done.14.refs_1_ = bf16[96,512]{1,0:T(8,128)(2,1)S(1)} collective-permute-done((bf16[96,512]{1,0:T(8,128)(2,1)S(1)}, bf16[96,512]{1,0:T(8,128)(2,1)S(1)}, u32[]{:S(2)}, u32[]{:S(2)}) %collective-permute-start.14) | collective-permute-done | bytes 98336 | tf_op jit(solution)/shard_map/ppermute | solution.py:339
  71.5 33.0 %all_to_all.10 = bf16[32,32,512]{2,1,0:T(8,128)(2,1)S(1)} all-to-all(bf16[32,32,512]{2,1,0:T(8,128)(2,1)S(1)} %bitcast.9), channel_id=1, replica_groups=mesh['row'=8,'col'=4] {'row','col'}, dimensions={0} | all-to-all | bytes 2097152 | tf_op jit(solution)/shard_map/all_to_all | solution.py:431
  104.5 2.1 %shard_map.88 = f32[1024,512]{1,0:T(8,128)} custom-call(bf16[1024,1024]{1,0:T(8,128)(2,1)S(1)} %copy-done, bf16[1024,512]{1,0:T(8,128)(2,1)S(1)} %bitcast.8), custom_call_target="tpu_custom_call" | custom-call | tf_op jit(solution)/shard_map/pallas_call | solution.py:439
  (47 shorter events, 5.4 us)
Async XLA Ops:
  0.0 10.6 %copy-start.2 = (s32[32]{0:T(128)S(1)}, s32[32]{0:T(128)}, u32[]{:S(2)}) copy-start(s32[32]{0:T(128)} %counts_hbm.1) | copy-start | bytes 388
  0.0 10.9 %copy-start.1 = (s32[8192]{0:T(1024)S(1)}, s32[8192]{0:T(1024)}, u32[]{:S(2)}) copy-start(s32[8192]{0:T(1024)} %param.11) | copy-start | bytes 98308
  3.5 29.3 %all-to-all-start = ((bf16[32,104,128]{2,1,0:T(8,128)(2,1)}), bf16[32,104,128]{2,1,0:T(8,128)(2,1)S(1)}, u32[]{:S(2)}, u32[]{:S(2)}) async-start(bf16[32,104,128]{2,1,0:T(8,128)(2,1)} %shard_map.73), calls=%async_computation | async-start | bytes 1703936 | tf_op jit(solution)/shard_map/all_to_all | solution.py:313
  33.2 7.9 %collective-permute-start = (bf16[256,512]{1,0:T(8,128)(2,1)S(1)}, bf16[256,512]{1,0:T(8,128)(2,1)S(1)}, u32[]{:S(2)}, u32[]{:S(2)}) collective-permute-start(bf16[256,512]{1,0:T(8,128)(2,1)S(1)} %get-tuple-element.27.refs_0_), channel_id=1, source_target_pairs={{0,8},{4,12},{8,0},{12,4},{16,24},{20,28},{24,16},{28,20},{1,9},{5... | collective-permute-start | bytes 786440 | tf_op jit(solution)/shard_map/ppermute | solution.py:346
  34.5 8.1 %collective-permute-start.1 = (bf16[256,512]{1,0:T(8,128)(2,1)S(1)}, bf16[256,512]{1,0:T(8,128)(2,1)S(1)}, u32[]{:S(2)}, u32[]{:S(2)}) collective-permute-start(bf16[256,512]{1,0:T(8,128)(2,1)S(1)} %get-tuple-element.27.refs_0_), channel_id=1, source_target_pairs={{0,16},{4,20},{8,24},{12,28},{16,0},{20,4},{24,8},{28,12},{1,17},{... | collective-permute-start | bytes 786440 | tf_op jit(solution)/shard_map/ppermute | solution.py:346
  34.7 13.9 %collective-permute-start.4 = (bf16[256,512]{1,0:T(8,128)(2,1)S(1)}, bf16[256,512]{1,0:T(8,128)(2,1)S(1)}, u32[]{:S(2)}, u32[]{:S(2)}) collective-permute-start(bf16[256,512]{1,0:T(8,128)(2,1)S(1)} %get-tuple-element.27.refs_0_), channel_id=1, source_target_pairs={{0,1},{1,0},{2,3},{3,2},{4,5},{5,4},{6,7},{7,6},{8,9},{9,8},{10,11... | collective-permute-start | bytes 786440 | tf_op jit(solution)/shard_map/ppermute | solution.py:339
  35.3 13.3 %collective-permute-start.5 = (bf16[256,512]{1,0:T(8,128)(2,1)S(1)}, bf16[256,512]{1,0:T(8,128)(2,1)S(1)}, u32[]{:S(2)}, u32[]{:S(2)}) collective-permute-start(bf16[256,512]{1,0:T(8,128)(2,1)S(1)} %get-tuple-element.27.refs_0_), channel_id=1, source_target_pairs={{0,2},{1,3},{2,0},{3,1},{4,6},{5,7},{6,4},{7,5},{8,10},{9,11},{10,... | collective-permute-start | bytes 786440 | tf_op jit(solution)/shard_map/ppermute | solution.py:339
  41.1 5.9 %collective-permute-start.2 = (bf16[128,512]{1,0:T(8,128)(2,1)S(1)}, bf16[128,512]{1,0:T(8,128)(2,1)S(1)}, u32[]{:S(2)}, u32[]{:S(2)}) collective-permute-start(bf16[128,512]{1,0:T(8,128)(2,1)S(1)} %slice.16), channel_id=1, source_target_pairs={{0,16},{4,20},{8,24},{12,28},{16,0},{20,4},{24,8},{28,12},{1,17},{... | collective-permute-start | bytes 393224 | tf_op jit(solution)/shard_map/ppermute | solution.py:346
  42.6 5.0 %collective-permute-start.3 = (bf16[128,512]{1,0:T(8,128)(2,1)S(1)}, bf16[128,512]{1,0:T(8,128)(2,1)S(1)}, u32[]{:S(2)}, u32[]{:S(2)}) collective-permute-start(bf16[128,512]{1,0:T(8,128)(2,1)S(1)} %slice.17), channel_id=1, source_target_pairs={{0,8},{4,12},{8,0},{12,4},{16,24},{20,28},{24,16},{28,20},{1,9},{5... | collective-permute-start | bytes 393224 | tf_op jit(solution)/shard_map/ppermute | solution.py:346
  45.7 3.0 %collective-permute-start.6 = (bf16[256,512]{1,0:T(8,128)(2,1)S(1)}, bf16[256,512]{1,0:T(8,128)(2,1)S(1)}, u32[]{:S(2)}, u32[]{:S(2)}) collective-permute-start(bf16[256,512]{1,0:T(8,128)(2,1)S(1)} %get-tuple-element.27.refs_0_), channel_id=1, source_target_pairs={{0,4},{4,0},{8,12},{12,8},{16,20},{20,16},{24,28},{28,24},{1,5},{5... | collective-permute-start | bytes 786440 | tf_op jit(solution)/shard_map/ppermute | solution.py:346
  47.1 3.3 %collective-permute-start.7 = (bf16[512,512]{1,0:T(8,128)(2,1)S(1)}, bf16[512,512]{1,0:T(8,128)(2,1)S(1)}, u32[]{:S(2)}, u32[]{:S(2)}) collective-permute-start(bf16[512,512]{1,0:T(8,128)(2,1)S(1)} %shard_map.75.refs_1_), channel_id=1, source_target_pairs={{0,4},{4,0},{8,12},{12,8},{16,20},{20,16},{24,28},{28,24},{1,5},{5... | collective-permute-start | bytes 1572872 | tf_op jit(solution)/shard_map/ppermute | solution.py:346
  47.6 2.7 %collective-permute-start.8 = (bf16[256,512]{1,0:T(8,128)(2,1)S(1)}, bf16[256,512]{1,0:T(8,128)(2,1)S(1)}, u32[]{:S(2)}, u32[]{:S(2)}) collective-permute-start(bf16[256,512]{1,0:T(8,128)(2,1)S(1)} %shard_map.77.refs_2_), channel_id=1, source_target_pairs={{0,4},{4,0},{8,12},{12,8},{16,20},{20,16},{24,28},{28,24},{1,5},{5... | collective-permute-start | bytes 786440 | tf_op jit(solution)/shard_map/ppermute | solution.py:346
  48.7 3.5 %collective-permute-start.11 = (bf16[96,512]{1,0:T(8,128)(2,1)S(1)}, bf16[96,512]{1,0:T(8,128)(2,1)S(1)}, u32[]{:S(2)}, u32[]{:S(2)}) collective-permute-start(bf16[96,512]{1,0:T(8,128)(2,1)S(1)} %slice.15), channel_id=1, source_target_pairs={{0,1},{1,0},{2,3},{3,2},{4,5},{5,4},{6,7},{7,6},{8,9},{9,8},{10,11... | collective-permute-start | bytes 294920 | tf_op jit(solution)/shard_map/ppermute | solution.py:339
  48.9 5.8 %collective-permute-start.10 = (bf16[160,512]{1,0:T(8,128)(2,1)S(1)}, bf16[160,512]{1,0:T(8,128)(2,1)S(1)}, u32[]{:S(2)}, u32[]{:S(2)}) collective-permute-start(bf16[160,512]{1,0:T(8,128)(2,1)S(1)} %slice.14), channel_id=1, source_target_pairs={{0,1},{1,0},{2,3},{3,2},{4,5},{5,4},{6,7},{7,6},{8,9},{9,8},{10,11... | collective-permute-start | bytes 491528 | tf_op jit(solution)/shard_map/ppermute | solution.py:339
  51.8 9.5 %collective-permute-start.9 = (bf16[160,512]{1,0:T(8,128)(2,1)S(1)}, bf16[160,512]{1,0:T(8,128)(2,1)S(1)}, u32[]{:S(2)}, u32[]{:S(2)}) collective-permute-start(bf16[160,512]{1,0:T(8,128)(2,1)S(1)} %get-tuple-element.39), channel_id=1, source_target_pairs={{0,2},{1,3},{2,0},{3,1},{4,6},{5,7},{6,4},{7,5},{8,10},{9,11},{10,... | collective-permute-start | bytes 491528 | tf_op jit(solution)/shard_map/ppermute | solution.py:339
  53.4 7.0 %collective-permute-start.13 = (bf16[96,512]{1,0:T(8,128)(2,1)S(1)}, bf16[96,512]{1,0:T(8,128)(2,1)S(1)}, u32[]{:S(2)}, u32[]{:S(2)}) collective-permute-start(bf16[96,512]{1,0:T(8,128)(2,1)S(1)} %shard_map.83), channel_id=1, source_target_pairs={{0,1},{1,0},{2,3},{3,2},{4,5},{5,4},{6,7},{7,6},{8,9},{9,8},{10,11... | collective-permute-start | bytes 294920 | tf_op jit(solution)/shard_map/ppermute | solution.py:339
  55.8 8.3 %collective-permute-start.12 = (bf16[160,512]{1,0:T(8,128)(2,1)S(1)}, bf16[160,512]{1,0:T(8,128)(2,1)S(1)}, u32[]{:S(2)}, u32[]{:S(2)}) collective-permute-start(bf16[160,512]{1,0:T(8,128)(2,1)S(1)} %shard_map.84), channel_id=1, source_target_pairs={{0,3},{1,2},{2,1},{3,0},{4,7},{5,6},{6,5},{7,4},{8,11},{9,10},{10,... | collective-permute-start | bytes 491528 | tf_op jit(solution)/shard_map/ppermute | solution.py:339
  59.1 11.9 %collective-permute-start.15 = (bf16[256,512]{1,0:T(8,128)(2,1)S(1)}, bf16[256,512]{1,0:T(8,128)(2,1)S(1)}, u32[]{:S(2)}, u32[]{:S(2)}) collective-permute-start(bf16[256,512]{1,0:T(8,128)(2,1)S(1)} %shard_map.86), channel_id=1, source_target_pairs={{0,1},{1,0},{2,3},{3,2},{4,5},{5,4},{6,7},{7,6},{8,9},{9,8},{10,11... | collective-permute-start | bytes 786440 | tf_op jit(solution)/shard_map/ppermute | solution.py:339
  60.4 10.6 %collective-permute-start.14 = (bf16[96,512]{1,0:T(8,128)(2,1)S(1)}, bf16[96,512]{1,0:T(8,128)(2,1)S(1)}, u32[]{:S(2)}, u32[]{:S(2)}) collective-permute-start(bf16[96,512]{1,0:T(8,128)(2,1)S(1)} %shard_map.85), channel_id=1, source_target_pairs={{0,2},{1,3},{2,0},{3,1},{4,6},{5,7},{6,4},{7,5},{8,10},{9,11},{10,... | collective-permute-start | bytes 294920 | tf_op jit(solution)/shard_map/ppermute | solution.py:339
  62.6 41.9 %copy-start = (bf16[1024,1024]{1,0:T(8,128)(2,1)S(1)}, bf16[1024,1024]{1,0:T(8,128)(2,1)}, u32[]{:S(2)}) copy-start(bf16[1024,1024]{1,0:T(8,128)(2,1)} %interp.1) | copy-start | bytes 6291460

commit v7 on v6

--- a/solution.py
+++ b/solution.py
@@ -34,8 +34,8 @@
 
 
 def pick_kernel(
-    box_total, capacity, counts_hbm, grid_hbm, owner_hbm, listed_hbm, orbitals_hbm, out,
-    counts, grid_rows, owner_map, listed, orbitals, sems,
+    box_total, capacity, counts_hbm, grid_hbm, owner_hbm, listed_hbm, orbitals_hbm, result,
+    counts, grid_rows, owner_map, listed, orbitals, out, sems, out_sems,
 ):
     copies = [
         pltpu.make_async_copy(source, target, sems.at[n])
@@ -104,6 +104,7 @@
     )
     box = orbitals.shape[0]
     step = targets // 4
+    sent = []
     copies[4].wait()
     for t in range(0, targets, step):
         hot = source[t : t + step] == lax.broadcasted_iota(jnp.int32, (step, box), 1)
@@ -122,6 +123,13 @@
         )
         first_owner = t // capacity
         out[first_owner : first_owner + owners, : packed.shape[1], :] = packed.astype(jnp.bfloat16)
+        part = slice(first_owner, first_owner + owners)
+        sent.append(
+            pltpu.make_async_copy(out.at[part], result.at[part], out_sems.at[t // step])
+        )
+        sent[-1].start()
+    for copy in sent:
+        copy.wait()
 
 
 def place_kernel(capacity, index, received, out, wanted):
@@ -290,14 +298,16 @@
         functools.partial(pick_kernel, box_total, capacity),
         out_shape=jax.ShapeDtypeStruct((box_total, packed, LANES), jnp.bfloat16),
         in_specs=[hbm()] * 5,
-        out_specs=vmem(),
+        out_specs=hbm(),
         scratch_shapes=[
             pltpu.SMEM((box_total,), jnp.int32),
             pltpu.VMEM((grid_rows.shape[1] // LANES, LANES), jnp.int32),
             pltpu.VMEM((point_total // LANES, LANES), jnp.int32),
             pltpu.VMEM((LIST // LANES, LANES), jnp.int32),
             pltpu.VMEM(orbitals.shape, jnp.bfloat16),
+            pltpu.VMEM((box_total, packed, LANES), jnp.bfloat16),
             pltpu.SemaphoreType.DMA((5,)),
+            pltpu.SemaphoreType.DMA((4,)),
         ],
         compiler_params=params(PICK_LIMIT),
         cost_estimate=pl.CostEstimate(
@@ -356,6 +366,16 @@
     double = [mask for mask in range(2, row_count, 2) if mask not in single]
     for mask in single:
         whole[mask] = flip(owned_rows, mask)
+    tiles = local(
+        fetch_kernel,
+        tuple(jax.ShapeDtypeStruct((OWN, row_count * OWN), jnp.bfloat16) for _ in range(col_count)),
+        jnp.bitwise_xor(my_col, jnp.arange(col_count)).astype(jnp.int32),
+        coulomb,
+        far=1,
+        scratch=[pltpu.SemaphoreType.DMA((col_count,))],
+    )
+
+    whole[single[0]], *tiles = lax.optimization_barrier((whole[single[0]], *tiles))
     passed_on = [owned_rows, join(*[whole[mask] for mask in single])]
     for mask in double:
         low, high = mask & -mask, 1 << (mask.bit_length() - 1)
@@ -366,16 +386,6 @@
         passed_on.append(join(*[whole[mask] for mask in double]))
     masks = [0] + single + double
     shape = jax.ShapeDtypeStruct
-    tiles = local(
-        fetch_kernel,
-        tuple(shape((OWN, row_count * OWN), jnp.bfloat16) for _ in range(col_count)),
-        jnp.bitwise_xor(my_col, jnp.arange(col_count)).astype(jnp.int32),
-        coulomb,
-        far=1,
-        scratch=[pltpu.SemaphoreType.DMA((col_count,))],
-    )
-
-    passed_on[-1], *tiles = lax.optimization_barrier((passed_on[-1], *tiles))
     mirrored = [flip(rows, 1) for rows in passed_on]
     direct = [mask for mask in left if mask]
     held = local(

time: 107 us -> 107 us (level)
  transfers between devices with their start and end apart: 17 -> 17, of which waited for: 9 -> 10; matrix products, arithmetic and copies ran while one was open for 2% -> 2% of each run, Pallas kernels for 9% -> 9%
where the time goes in v7:
time: 107 us; the launch traced here: 106 us
  waiting for transfers between devices  36.1 us (34%)
  blocking collectives  33 us (31%)
  starting transfers between devices  19.6 us (18%)
  Pallas kernels  15.4 us (14%)
  other arithmetic  1.73 us (2%)
    all_to_all x1, blocking collectives, shards(): lax.all_to_all(picked.reshape(box_total, per_owner, NORB), ('row', 'col')...  33 us
    all_to_all x1, waiting for transfers between devices, shards(): lax.all_to_all(outgoing, ('row', 'col'), split_axis=0, concat_axis=0, til...  20.2 us
    ppermute x9, waiting for transfers between devices, swap(): return lax.ppermute(rows, 'col', [(i, i ^ mask) for i in range(col_count)])  10.4 us
    pallas_call x13, Pallas kernels, local(): pl.pallas_call(kernel, out_shape=out, in_specs=[spec(n, a) for n, a in en...  9.65 us
    all_to_all x1, starting transfers between devices, shards(): lax.all_to_all(outgoing, ('row', 'col'), split_axis=0, concat_axis=0, til...  7.1 us
    ppermute x9, starting transfers between devices, swap(): return lax.ppermute(rows, 'col', [(i, i ^ mask) for i in range(col_count)])  6.37 us
    ppermute x7, starting transfers between devices, flip(): return lax.ppermute(rows, 'row', [(i, i ^ mask) for i in range(row_count)])  6.16 us
    ppermute x7, waiting for transfers between devices, flip(): return lax.ppermute(rows, 'row', [(i, i ^ mask) for i in range(row_count)])  5.53 us
  transfers between devices with their start and end apart: 17, of which 10 were waited for; matrix products, arithmetic and copies ran while one was open for 2% of the time, Pallas kernels for 9%

profile of v7, /device:TPU:1, one launch (start us, length us, event | category | flops | bytes accessed | tf_op | source)
XLA Modules:
  0.0 106.4 jit_solution(9370654405620330655)
XLA Ops:
  0.0 3.3 %shard_map.73 = bf16[32,104,128]{2,1,0:T(8,128)(2,1)} custom-call(s32[32]{0:T(128)} %counts_hbm.1, s32[8,128]{1,0:T(8,128)} %bitcast.13, s32[64,128]{1,0:T(8,128)} %bitcast.10, s32[8,128]{1,0:T(8,128)} %bitcast.14, bf16[1024,512]{1,0:T(8,128)(2,1)} %orbitals_hbm.1), custom_call_target="tpu_custom_call" | custom-call | flops 805306368 | bytes 2097152 | tf_op jit(solution)/shard_map/pallas_call | solution.py:297
  3.3 7.1 %all-to-all-start = ((bf16[32,104,128]{2,1,0:T(8,128)(2,1)}), bf16[32,104,128]{2,1,0:T(8,128)(2,1)S(1)}, u32[]{:S(2)}, u32[]{:S(2)}) async-start(bf16[32,104,128]{2,1,0:T(8,128)(2,1)} %shard_map.73), calls=%async_computation | async-start | bytes 1703936 | tf_op jit(solution)/shard_map/all_to_all | solution.py:323
  10.7 1.2 %select_reduce_fusion = s32[256]{0:T(256)S(1)} fusion(s32[8192]{0:T(1024)S(1)} %copy-done.1, s32[256]{0:T(256)S(1)} %iota_add_fusion), kind=kLoop, calls=%fused_computation | loop fusion | flops 6291200 | bytes 34816 | tf_op jit(solution)/shard_map/reduce_sum | solution.py:329
  12.4 20.2 %all-to-all-done.received = bf16[32,104,128]{2,1,0:T(8,128)(2,1)S(1)} async-done(((bf16[32,104,128]{2,1,0:T(8,128)(2,1)}), bf16[32,104,128]{2,1,0:T(8,128)(2,1)S(1)}, u32[]{:S(2)}, u32[]{:S(2)}) %all-to-all-start) | async-done | bytes 852000 | tf_op jit(solution)/shard_map/all_to_all | solution.py:323
  33.0 1.3 %collective-permute-start = (bf16[256,512]{1,0:T(8,128)(2,1)S(1)}, bf16[256,512]{1,0:T(8,128)(2,1)S(1)}, u32[]{:S(2)}, u32[]{:S(2)}) collective-permute-start(bf16[256,512]{1,0:T(8,128)(2,1)S(1)} %get-tuple-element.27.refs_0_), channel_id=1, source_target_pairs={{0,8},{4,12},{8,0},{12,4},{16,24},{20,28},{24,16},{28,20},{1,9},{5... | collective-permute-start | bytes 786440 | tf_op jit(solution)/shard_map/ppermute | solution.py:356
  35.4 2.8 %shard_map.75 = (bf16[256,2048]{1,0:T(8,128)(2,1)S(1)}, bf16[256,2048]{1,0:T(8,128)(2,1)S(1)}, bf16[256,2048]{1,0:T(8,128)(2,1)S(1)}, bf16[256,2048]{1,0:T(8,128)(2,1)S(1)}) custom-call(s32[4]{0:T(128)S(1)} %iota_xor_fusion.scalars, bf16[1024,2048]{1,0:T(8,128)(2,1)} %coulomb.1), custom_call_target="tpu_custom_call" | custom-call | tf_op jit(solution)/shard_map/pallas_call | solution.py:238
  38.2 2.7 %collective-permute-done.refs_0_ = bf16[256,512]{1,0:T(8,128)(2,1)S(1)} collective-permute-done((bf16[256,512]{1,0:T(8,128)(2,1)S(1)}, bf16[256,512]{1,0:T(8,128)(2,1)S(1)}, u32[]{:S(2)}, u32[]{:S(2)}) %collective-permute-start) | collective-permute-done | bytes 262176 | tf_op jit(solution)/shard_map/ppermute | solution.py:356
  40.9 1.3 %collective-permute-start.2 = (bf16[128,512]{1,0:T(8,128)(2,1)S(1)}, bf16[128,512]{1,0:T(8,128)(2,1)S(1)}, u32[]{:S(2)}, u32[]{:S(2)}) collective-permute-start(bf16[128,512]{1,0:T(8,128)(2,1)S(1)} %slice.12), channel_id=1, source_target_pairs={{0,16},{4,20},{8,24},{12,28},{16,0},{20,4},{24,8},{28,12},{1,17},{... | collective-permute-start | bytes 393224 | tf_op jit(solution)/shard_map/ppermute | solution.py:356
  42.7 1.3 %collective-permute-start.6 = (bf16[256,512]{1,0:T(8,128)(2,1)S(1)}, bf16[256,512]{1,0:T(8,128)(2,1)S(1)}, u32[]{:S(2)}, u32[]{:S(2)}) collective-permute-start(bf16[256,512]{1,0:T(8,128)(2,1)S(1)} %get-tuple-element.27.refs_0_), channel_id=1, source_target_pairs={{0,4},{4,0},{8,12},{12,8},{16,20},{20,16},{24,28},{28,24},{1,5},{5... | collective-permute-start | bytes 786440 | tf_op jit(solution)/shard_map/ppermute | solution.py:356
  44.0 2.1 %collective-permute-done.2.refs_0_ = bf16[128,512]{1,0:T(8,128)(2,1)S(1)} collective-permute-done((bf16[128,512]{1,0:T(8,128)(2,1)S(1)}, bf16[128,512]{1,0:T(8,128)(2,1)S(1)}, u32[]{:S(2)}, u32[]{:S(2)}) %collective-permute-start.2) | collective-permute-done | bytes 131104 | tf_op jit(solution)/shard_map/ppermute | solution.py:356
  47.4 1.0 collective-permute-start.8
  48.7 1.5 %collective-permute-start.10 = (bf16[160,512]{1,0:T(8,128)(2,1)S(1)}, bf16[160,512]{1,0:T(8,128)(2,1)S(1)}, u32[]{:S(2)}, u32[]{:S(2)}) collective-permute-start(bf16[160,512]{1,0:T(8,128)(2,1)S(1)} %slice.14), channel_id=1, source_target_pairs={{0,1},{1,0},{2,3},{3,2},{4,5},{5,4},{6,7},{7,6},{8,9},{9,8},{10,11... | collective-permute-start | bytes 491528 | tf_op jit(solution)/shard_map/ppermute | solution.py:349
  50.3 1.3 %shard_map.81 = (f32[96,512]{1,0:T(8,128)S(1)}, bf16[160,512]{1,0:T(8,128)(2,1)S(1)}) custom-call(bf16[256,512]{1,0:T(8,128)(2,1)S(1)} %get-tuple-element.37.refs_0_, bf16[2048,512]{1,0:T(8,128)(2,1)S(1)} %shard_map.80.refs_1_, bf16[256,2048]{1,0:T(8,128)(2,1)S(1)} %get-tuple-element.38.refs_2_), custom_call_target="tpu_custom_call" | custom-call | tf_op jit(solution)/shard_map/pallas_call | solution.py:238
  52.1 1.1 %shard_map.83 = bf16[96,512]{1,0:T(8,128)(2,1)S(1)} custom-call(bf16[96,512]{1,0:T(8,128)(2,1)S(1)} %collective-permute-done.11.refs_0_, bf16[2048,512]{1,0:T(8,128)(2,1)S(1)} %shard_map.80.refs_1_, bf16[256,2048]{1,0:T(8,128)(2,1)S(1)} %get-tuple-element.41.refs_2_), custom_call_target="tpu_custom_call" | custom-call | tf_op jit(solution)/shard_map/pallas_call | solution.py:238
  54.5 1.2 %shard_map.84 = bf16[160,512]{1,0:T(8,128)(2,1)S(1)} custom-call(bf16[160,512]{1,0:T(8,128)(2,1)S(1)} %collective-permute-done.10.refs_0_, bf16[2048,512]{1,0:T(8,128)(2,1)S(1)} %shard_map.80.refs_1_, bf16[256,2048]{1,0:T(8,128)(2,1)S(1)} %get-tuple-element.41.refs_2_), custom_call_target="tpu_custom_call" | custom-call | tf_op jit(solution)/shard_map/pallas_call | solution.py:238
  55.7 2.0 %collective-permute-start.12 = (bf16[160,512]{1,0:T(8,128)(2,1)S(1)}, bf16[160,512]{1,0:T(8,128)(2,1)S(1)}, u32[]{:S(2)}, u32[]{:S(2)}) collective-permute-start(bf16[160,512]{1,0:T(8,128)(2,1)S(1)} %shard_map.84), channel_id=1, source_target_pairs={{0,3},{1,2},{2,1},{3,0},{4,7},{5,6},{6,5},{7,4},{8,11},{9,10},{10,... | collective-permute-start | bytes 491528 | tf_op jit(solution)/shard_map/ppermute | solution.py:349
  57.7 1.3 %shard_map.86 = bf16[256,512]{1,0:T(8,128)(2,1)S(1)} custom-call(bf16[256,512]{1,0:T(8,128)(2,1)S(1)} %get-tuple-element.45.refs_0_, bf16[2048,512]{1,0:T(8,128)(2,1)S(1)} %shard_map.80.refs_1_, bf16[256,2048]{1,0:T(8,128)(2,1)S(1)} %get-tuple-element.46.refs_2_), custom_call_target="tpu_custom_call" | custom-call | tf_op jit(solution)/shard_map/pallas_call | solution.py:238
  59.0 1.2 %collective-permute-done.13.other = bf16[96,512]{1,0:T(8,128)(2,1)S(1)} collective-permute-done((bf16[96,512]{1,0:T(8,128)(2,1)S(1)}, bf16[96,512]{1,0:T(8,128)(2,1)S(1)}, u32[]{:S(2)}, u32[]{:S(2)}) %collective-permute-start.13) | collective-permute-done | bytes 98336 | tf_op jit(solution)/shard_map/ppermute | solution.py:349
  60.2 0.9 collective-permute-start.14
  61.1 1.3 %shard_map.82.own = f32[256,512]{1,0:T(8,128)S(1)} custom-call(bf16[256,512]{1,0:T(8,128)(2,1)S(1)} %get-tuple-element.27.refs_0_, bf16[2048,512]{1,0:T(8,128)(2,1)S(1)} %shard_map.80.refs_1_, bf16[256,2048]{1,0:T(8,128)(2,1)S(1)} %get-tuple-element.36.refs_2_, bf16[160,512]{1,0:T(8,128)(2,1)S(1)} %collective-permute-done.9.refs_3_), custom_call_target="tpu_custom_call" | custom-call | flops 10000000000 | tf_op jit(solution)/shard_map/pallas_call | solution.py:238
  62.4 1.6 %collective-permute-done.12.refs_0_ = bf16[160,512]{1,0:T(8,128)(2,1)S(1)} collective-permute-done((bf16[160,512]{1,0:T(8,128)(2,1)S(1)}, bf16[160,512]{1,0:T(8,128)(2,1)S(1)}, u32[]{:S(2)}, u32[]{:S(2)}) %collective-permute-start.12) | collective-permute-done | bytes 163872 | tf_op jit(solution)/shard_map/ppermute | solution.py:349
  64.0 6.8 %collective-permute-done.14.refs_1_ = bf16[96,512]{1,0:T(8,128)(2,1)S(1)} collective-permute-done((bf16[96,512]{1,0:T(8,128)(2,1)S(1)}, bf16[96,512]{1,0:T(8,128)(2,1)S(1)}, u32[]{:S(2)}, u32[]{:S(2)}) %collective-permute-start.14) | collective-permute-done | bytes 98336 | tf_op jit(solution)/shard_map/ppermute | solution.py:349
  71.3 33.0 %all_to_all.10 = bf16[32,32,512]{2,1,0:T(8,128)(2,1)S(1)} all-to-all(bf16[32,32,512]{2,1,0:T(8,128)(2,1)S(1)} %bitcast.9), channel_id=1, replica_groups=mesh['row'=8,'col'=4] {'row','col'}, dimensions={0} | all-to-all | bytes 2097152 | tf_op jit(solution)/shard_map/all_to_all | solution.py:441
  104.3 2.1 %shard_map.88 = f32[1024,512]{1,0:T(8,128)} custom-call(bf16[1024,1024]{1,0:T(8,128)(2,1)S(1)} %copy-done, bf16[1024,512]{1,0:T(8,128)(2,1)S(1)} %bitcast.8), custom_call_target="tpu_custom_call" | custom-call | tf_op jit(solution)/shard_map/pallas_call | solution.py:449
  (47 shorter events, 6.8 us)
Async XLA Ops:
  0.0 10.4 %copy-start.2 = (s32[32]{0:T(128)S(1)}, s32[32]{0:T(128)}, u32[]{:S(2)}) copy-start(s32[32]{0:T(128)} %counts_hbm.1) | copy-start | bytes 388
  0.0 10.7 %copy-start.1 = (s32[8192]{0:T(1024)S(1)}, s32[8192]{0:T(1024)}, u32[]{:S(2)}) copy-start(s32[8192]{0:T(1024)} %param.11) | copy-start | bytes 98308
  3.3 29.3 %all-to-all-start = ((bf16[32,104,128]{2,1,0:T(8,128)(2,1)}), bf16[32,104,128]{2,1,0:T(8,128)(2,1)S(1)}, u32[]{:S(2)}, u32[]{:S(2)}) async-start(bf16[32,104,128]{2,1,0:T(8,128)(2,1)} %shard_map.73), calls=%async_computation | async-start | bytes 1703936 | tf_op jit(solution)/shard_map/all_to_all | solution.py:323
  33.0 7.9 %collective-permute-start = (bf16[256,512]{1,0:T(8,128)(2,1)S(1)}, bf16[256,512]{1,0:T(8,128)(2,1)S(1)}, u32[]{:S(2)}, u32[]{:S(2)}) collective-permute-start(bf16[256,512]{1,0:T(8,128)(2,1)S(1)} %get-tuple-element.27.refs_0_), channel_id=1, source_target_pairs={{0,8},{4,12},{8,0},{12,4},{16,24},{20,28},{24,16},{28,20},{1,9},{5... | collective-permute-start | bytes 786440 | tf_op jit(solution)/shard_map/ppermute | solution.py:356
  34.3 8.1 %collective-permute-start.1 = (bf16[256,512]{1,0:T(8,128)(2,1)S(1)}, bf16[256,512]{1,0:T(8,128)(2,1)S(1)}, u32[]{:S(2)}, u32[]{:S(2)}) collective-permute-start(bf16[256,512]{1,0:T(8,128)(2,1)S(1)} %get-tuple-element.27.refs_0_), channel_id=1, source_target_pairs={{0,16},{4,20},{8,24},{12,28},{16,0},{20,4},{24,8},{28,12},{1,17},{... | collective-permute-start | bytes 786440 | tf_op jit(solution)/shard_map/ppermute | solution.py:356
  34.6 13.9 %collective-permute-start.4 = (bf16[256,512]{1,0:T(8,128)(2,1)S(1)}, bf16[256,512]{1,0:T(8,128)(2,1)S(1)}, u32[]{:S(2)}, u32[]{:S(2)}) collective-permute-start(bf16[256,512]{1,0:T(8,128)(2,1)S(1)} %get-tuple-element.27.refs_0_), channel_id=1, source_target_pairs={{0,1},{1,0},{2,3},{3,2},{4,5},{5,4},{6,7},{7,6},{8,9},{9,8},{10,11... | collective-permute-start | bytes 786440 | tf_op jit(solution)/shard_map/ppermute | solution.py:349
  35.2 13.3 %collective-permute-start.5 = (bf16[256,512]{1,0:T(8,128)(2,1)S(1)}, bf16[256,512]{1,0:T(8,128)(2,1)S(1)}, u32[]{:S(2)}, u32[]{:S(2)}) collective-permute-start(bf16[256,512]{1,0:T(8,128)(2,1)S(1)} %get-tuple-element.27.refs_0_), channel_id=1, source_target_pairs={{0,2},{1,3},{2,0},{3,1},{4,6},{5,7},{6,4},{7,5},{8,10},{9,11},{10,... | collective-permute-start | bytes 786440 | tf_op jit(solution)/shard_map/ppermute | solution.py:349
  40.9 5.3 %collective-permute-start.2 = (bf16[128,512]{1,0:T(8,128)(2,1)S(1)}, bf16[128,512]{1,0:T(8,128)(2,1)S(1)}, u32[]{:S(2)}, u32[]{:S(2)}) collective-permute-start(bf16[128,512]{1,0:T(8,128)(2,1)S(1)} %slice.12), channel_id=1, source_target_pairs={{0,16},{4,20},{8,24},{12,28},{16,0},{20,4},{24,8},{28,12},{1,17},{... | collective-permute-start | bytes 393224 | tf_op jit(solution)/shard_map/ppermute | solution.py:356
  42.4 5.0 %collective-permute-start.3 = (bf16[128,512]{1,0:T(8,128)(2,1)S(1)}, bf16[128,512]{1,0:T(8,128)(2,1)S(1)}, u32[]{:S(2)}, u32[]{:S(2)}) collective-permute-start(bf16[128,512]{1,0:T(8,128)(2,1)S(1)} %slice.16), channel_id=1, source_target_pairs={{0,8},{4,12},{8,0},{12,4},{16,24},{20,28},{24,16},{28,20},{1,9},{5... | collective-permute-start | bytes 393224 | tf_op jit(solution)/shard_map/ppermute | solution.py:356
  42.7 5.8 %collective-permute-start.6 = (bf16[256,512]{1,0:T(8,128)(2,1)S(1)}, bf16[256,512]{1,0:T(8,128)(2,1)S(1)}, u32[]{:S(2)}, u32[]{:S(2)}) collective-permute-start(bf16[256,512]{1,0:T(8,128)(2,1)S(1)} %get-tuple-element.27.refs_0_), channel_id=1, source_target_pairs={{0,4},{4,0},{8,12},{12,8},{16,20},{20,16},{24,28},{28,24},{1,5},{5... | collective-permute-start | bytes 786440 | tf_op jit(solution)/shard_map/ppermute | solution.py:356
  46.2 4.0 %collective-permute-start.7 = (bf16[512,512]{1,0:T(8,128)(2,1)S(1)}, bf16[512,512]{1,0:T(8,128)(2,1)S(1)}, u32[]{:S(2)}, u32[]{:S(2)}) collective-permute-start(bf16[512,512]{1,0:T(8,128)(2,1)S(1)} %shard_map.76.refs_1_), channel_id=1, source_target_pairs={{0,4},{4,0},{8,12},{12,8},{16,20},{20,16},{24,28},{28,24},{1,5},{5... | collective-permute-start | bytes 1572872 | tf_op jit(solution)/shard_map/ppermute | solution.py:356
  47.4 2.7 %collective-permute-start.8 = (bf16[256,512]{1,0:T(8,128)(2,1)S(1)}, bf16[256,512]{1,0:T(8,128)(2,1)S(1)}, u32[]{:S(2)}, u32[]{:S(2)}) collective-permute-start(bf16[256,512]{1,0:T(8,128)(2,1)S(1)} %shard_map.78.refs_2_), channel_id=1, source_target_pairs={{0,4},{4,0},{8,12},{12,8},{16,20},{20,16},{24,28},{28,24},{1,5},{5... | collective-permute-start | bytes 786440 | tf_op jit(solution)/shard_map/ppermute | solution.py:356
  48.5 3.5 %collective-permute-start.11 = (bf16[96,512]{1,0:T(8,128)(2,1)S(1)}, bf16[96,512]{1,0:T(8,128)(2,1)S(1)}, u32[]{:S(2)}, u32[]{:S(2)}) collective-permute-start(bf16[96,512]{1,0:T(8,128)(2,1)S(1)} %slice.15), channel_id=1, source_target_pairs={{0,1},{1,0},{2,3},{3,2},{4,5},{5,4},{6,7},{7,6},{8,9},{9,8},{10,11... | collective-permute-start | bytes 294920 | tf_op jit(solution)/shard_map/ppermute | solution.py:349
  48.7 5.8 %collective-permute-start.10 = (bf16[160,512]{1,0:T(8,128)(2,1)S(1)}, bf16[160,512]{1,0:T(8,128)(2,1)S(1)}, u32[]{:S(2)}, u32[]{:S(2)}) collective-permute-start(bf16[160,512]{1,0:T(8,128)(2,1)S(1)} %slice.14), channel_id=1, source_target_pairs={{0,1},{1,0},{2,3},{3,2},{4,5},{5,4},{6,7},{7,6},{8,9},{9,8},{10,11... | collective-permute-start | bytes 491528 | tf_op jit(solution)/shard_map/ppermute | solution.py:349
  51.6 9.5 %collective-permute-start.9 = (bf16[160,512]{1,0:T(8,128)(2,1)S(1)}, bf16[160,512]{1,0:T(8,128)(2,1)S(1)}, u32[]{:S(2)}, u32[]{:S(2)}) collective-permute-start(bf16[160,512]{1,0:T(8,128)(2,1)S(1)} %get-tuple-element.39), channel_id=1, source_target_pairs={{0,2},{1,3},{2,0},{3,1},{4,6},{5,7},{6,4},{7,5},{8,10},{9,11},{10,... | collective-permute-start | bytes 491528 | tf_op jit(solution)/shard_map/ppermute | solution.py:349
  53.2 7.0 %collective-permute-start.13 = (bf16[96,512]{1,0:T(8,128)(2,1)S(1)}, bf16[96,512]{1,0:T(8,128)(2,1)S(1)}, u32[]{:S(2)}, u32[]{:S(2)}) collective-permute-start(bf16[96,512]{1,0:T(8,128)(2,1)S(1)} %shard_map.83), channel_id=1, source_target_pairs={{0,1},{1,0},{2,3},{3,2},{4,5},{5,4},{6,7},{7,6},{8,9},{9,8},{10,11... | collective-permute-start | bytes 294920 | tf_op jit(solution)/shard_map/ppermute | solution.py:349
  55.7 8.3 %collective-permute-start.12 = (bf16[160,512]{1,0:T(8,128)(2,1)S(1)}, bf16[160,512]{1,0:T(8,128)(2,1)S(1)}, u32[]{:S(2)}, u32[]{:S(2)}) collective-permute-start(bf16[160,512]{1,0:T(8,128)(2,1)S(1)} %shard_map.84), channel_id=1, source_target_pairs={{0,3},{1,2},{2,1},{3,0},{4,7},{5,6},{6,5},{7,4},{8,11},{9,10},{10,... | collective-permute-start | bytes 491528 | tf_op jit(solution)/shard_map/ppermute | solution.py:349
  58.9 11.8 %collective-permute-start.15 = (bf16[256,512]{1,0:T(8,128)(2,1)S(1)}, bf16[256,512]{1,0:T(8,128)(2,1)S(1)}, u32[]{:S(2)}, u32[]{:S(2)}) collective-permute-start(bf16[256,512]{1,0:T(8,128)(2,1)S(1)} %shard_map.86), channel_id=1, source_target_pairs={{0,1},{1,0},{2,3},{3,2},{4,5},{5,4},{6,7},{7,6},{8,9},{9,8},{10,11... | collective-permute-start | bytes 786440 | tf_op jit(solution)/shard_map/ppermute | solution.py:349
  60.2 10.6 %collective-permute-start.14 = (bf16[96,512]{1,0:T(8,128)(2,1)S(1)}, bf16[96,512]{1,0:T(8,128)(2,1)S(1)}, u32[]{:S(2)}, u32[]{:S(2)}) collective-permute-start(bf16[96,512]{1,0:T(8,128)(2,1)S(1)} %shard_map.85), channel_id=1, source_target_pairs={{0,2},{1,3},{2,0},{3,1},{4,6},{5,7},{6,4},{7,5},{8,10},{9,11},{10,... | collective-permute-start | bytes 294920 | tf_op jit(solution)/shard_map/ppermute | solution.py:349
  62.4 41.9 %copy-start = (bf16[1024,1024]{1,0:T(8,128)(2,1)S(1)}, bf16[1024,1024]{1,0:T(8,128)(2,1)}, u32[]{:S(2)}) copy-start(bf16[1024,1024]{1,0:T(8,128)(2,1)} %interp.1) | copy-start | bytes 6291460

commit v8 on v7

--- a/solution.py
+++ b/solution.py
@@ -169,12 +169,19 @@
     ).astype(jnp.bfloat16)
 
 
+def turn(mask):
+    return mask & ~6 | (mask & 2) << 1 | (mask & 4) >> 1
+
+
 def order_kernel(masks, scalars, *refs):
     pieces, out = refs[:-1], refs[-1]
-    places = [mask ^ parity for parity in (0, 1) for mask in masks]
+    me = scalars[0]
+    odd = lax.rem(me, 2) == 1
+    places = [jnp.where(odd, turn(mask), mask) for mask in masks]
+    places += [jnp.where(odd, mask, turn(mask)) ^ 1 for mask in masks]
     for ref in pieces:
         for n in range(ref.shape[0] // OWN):
-            place = jnp.bitwise_xor(scalars[0], places.pop(0)) * OWN
+            place = jnp.bitwise_xor(me, places.pop(0)) * OWN
             out[pl.ds(pl.multiple_of(place, OWN), OWN), :] = ref[n * OWN : (n + 1) * OWN, :]
 
 
@@ -353,7 +360,9 @@
         return local(join_kernel, jax.ShapeDtypeStruct((total, NORB), rows[0].dtype), *rows)
 
     def flip(rows, mask):
-        return lax.ppermute(rows, "row", [(i, i ^ mask) for i in range(row_count)])
+        return lax.ppermute(
+            rows, "row", [(i, i ^ (turn(mask) if i & 1 else mask)) for i in range(row_count)]
+        )
 
     half = OWN // 2
     left = {0: [owned_rows]}

time: 107 us -> 107 us (level)
  starting transfers between devices: 19.6 us -> 23.3 us
  waiting for transfers between devices: 36.1 us -> 33 us
    ppermute x9, starting transfers between devices: 6.37 us -> 10.7 us  [swap(): return lax.ppermute(rows, 'col', [(i, i ^ mask) for i in range(col_count)])]
    ppermute x9, waiting for transfers between devices: 10.4 us -> 7.74 us  [swap(): return lax.ppermute(rows, 'col', [(i, i ^ mask) for i in range(col_count)])]
  transfers between devices with their start and end apart: 17 -> 17, of which waited for: 10 -> 7; matrix products, arithmetic and copies ran while one was open for 2% -> 2% of each run, Pallas kernels for 9% -> 9%
where the time goes in v8:
time: 107 us; the launch traced here: 106 us
  waiting for transfers between devices  33 us (31%)
  blocking collectives  32.5 us (30%)
  starting transfers between devices  23.3 us (22%)
  Pallas kernels  15.4 us (14%)
  other arithmetic  1.73 us (2%)
    all_to_all x1, blocking collectives, shards(): lax.all_to_all(picked.reshape(box_total, per_owner, NORB), ('row', 'col')...  32.5 us
    all_to_all x1, waiting for transfers between devices, shards(): lax.all_to_all(outgoing, ('row', 'col'), split_axis=0, concat_axis=0, til...  20.2 us
    ppermute x9, starting transfers between devices, swap(): return lax.ppermute(rows, 'col', [(i, i ^ mask) for i in range(col_count)])  10.7 us
    pallas_call x13, Pallas kernels, local(): pl.pallas_call(kernel, out_shape=out, in_specs=[spec(n, a) for n, a in en...  9.65 us
    ppermute x9, waiting for transfers between devices, swap(): return lax.ppermute(rows, 'col', [(i, i ^ mask) for i in range(col_count)])  7.74 us
    all_to_all x1, starting transfers between devices, shards(): lax.all_to_all(outgoing, ('row', 'col'), split_axis=0, concat_axis=0, til...  7.1 us
    ppermute x7, starting transfers between devices, flip(): lax.ppermute(rows, 'row', [(i, i ^ (turn(mask) if i & 1 else mask)) for i...  5.5 us
    ppermute x7, waiting for transfers between devices, flip(): lax.ppermute(rows, 'row', [(i, i ^ (turn(mask) if i & 1 else mask)) for i...  5.03 us
  transfers between devices with their start and end apart: 17, of which 7 were waited for; matrix products, arithmetic and copies ran while one was open for 2% of the time, Pallas kernels for 9%

profile of v8, /device:TPU:1, one launch (start us, length us, event | category | flops | bytes accessed | tf_op | source)
XLA Modules:
  0.0 106.4 jit_solution(11027750536166508534)
XLA Ops:
  0.0 3.3 %shard_map.73 = bf16[32,104,128]{2,1,0:T(8,128)(2,1)} custom-call(s32[32]{0:T(128)} %counts_hbm.1, s32[8,128]{1,0:T(8,128)} %bitcast.13, s32[64,128]{1,0:T(8,128)} %bitcast.10, s32[8,128]{1,0:T(8,128)} %bitcast.14, bf16[1024,512]{1,0:T(8,128)(2,1)} %orbitals_hbm.1), custom_call_target="tpu_custom_call" | custom-call | flops 805306368 | bytes 2097152 | tf_op jit(solution)/shard_map/pallas_call | solution.py:304
  3.3 7.1 %all-to-all-start = ((bf16[32,104,128]{2,1,0:T(8,128)(2,1)}), bf16[32,104,128]{2,1,0:T(8,128)(2,1)S(1)}, u32[]{:S(2)}, u32[]{:S(2)}) async-start(bf16[32,104,128]{2,1,0:T(8,128)(2,1)} %shard_map.73), calls=%async_computation | async-start | bytes 1703936 | tf_op jit(solution)/shard_map/all_to_all | solution.py:330
  10.7 1.2 %select_reduce_fusion = s32[256]{0:T(256)S(1)} fusion(s32[8192]{0:T(1024)S(1)} %copy-done.1, s32[256]{0:T(256)S(1)} %iota_add_fusion), kind=kLoop, calls=%fused_computation | loop fusion | flops 6291200 | bytes 34816 | tf_op jit(solution)/shard_map/reduce_sum | solution.py:336
  12.4 20.2 %all-to-all-done.received = bf16[32,104,128]{2,1,0:T(8,128)(2,1)S(1)} async-done(((bf16[32,104,128]{2,1,0:T(8,128)(2,1)}), bf16[32,104,128]{2,1,0:T(8,128)(2,1)S(1)}, u32[]{:S(2)}, u32[]{:S(2)}) %all-to-all-start) | async-done | bytes 852000 | tf_op jit(solution)/shard_map/all_to_all | solution.py:330
  33.0 1.3 %collective-permute-start = (bf16[256,512]{1,0:T(8,128)(2,1)S(1)}, bf16[256,512]{1,0:T(8,128)(2,1)S(1)}, u32[]{:S(2)}, u32[]{:S(2)}) collective-permute-start(bf16[256,512]{1,0:T(8,128)(2,1)S(1)} %get-tuple-element.27.refs_0_), channel_id=1, source_target_pairs={{0,8},{4,20},{8,0},{12,28},{16,24},{20,4},{24,16},{28,12},{1,9},{5... | collective-permute-start | bytes 786440 | tf_op jit(solution)/shard_map/ppermute | solution.py:363
  35.4 2.8 %shard_map.75 = (bf16[256,2048]{1,0:T(8,128)(2,1)S(1)}, bf16[256,2048]{1,0:T(8,128)(2,1)S(1)}, bf16[256,2048]{1,0:T(8,128)(2,1)S(1)}, bf16[256,2048]{1,0:T(8,128)(2,1)S(1)}) custom-call(s32[4]{0:T(128)S(1)} %iota_xor_fusion.scalars, bf16[1024,2048]{1,0:T(8,128)(2,1)} %coulomb.1), custom_call_target="tpu_custom_call" | custom-call | tf_op jit(solution)/shard_map/pallas_call | solution.py:245
  38.2 2.3 %collective-permute-done.refs_0_ = bf16[256,512]{1,0:T(8,128)(2,1)S(1)} collective-permute-done((bf16[256,512]{1,0:T(8,128)(2,1)S(1)}, bf16[256,512]{1,0:T(8,128)(2,1)S(1)}, u32[]{:S(2)}, u32[]{:S(2)}) %collective-permute-start) | collective-permute-done | bytes 262176 | tf_op jit(solution)/shard_map/ppermute | solution.py:363
  40.5 2.2 %collective-permute-start.2 = (bf16[128,512]{1,0:T(8,128)(2,1)S(1)}, bf16[128,512]{1,0:T(8,128)(2,1)S(1)}, u32[]{:S(2)}, u32[]{:S(2)}) collective-permute-start(bf16[128,512]{1,0:T(8,128)(2,1)S(1)} %slice.12), channel_id=1, source_target_pairs={{0,16},{4,12},{8,24},{12,4},{16,0},{20,28},{24,8},{28,20},{1,17},{... | collective-permute-start | bytes 393224 | tf_op jit(solution)/shard_map/ppermute | solution.py:363
  43.7 1.6 %collective-permute-done.2.refs_0_ = bf16[128,512]{1,0:T(8,128)(2,1)S(1)} collective-permute-done((bf16[128,512]{1,0:T(8,128)(2,1)S(1)}, bf16[128,512]{1,0:T(8,128)(2,1)S(1)}, u32[]{:S(2)}, u32[]{:S(2)}) %collective-permute-start.2) | collective-permute-done | bytes 131104 | tf_op jit(solution)/shard_map/ppermute | solution.py:363
  45.7 1.1 %collective-permute-done.3.refs_1_ = bf16[128,512]{1,0:T(8,128)(2,1)S(1)} collective-permute-done((bf16[128,512]{1,0:T(8,128)(2,1)S(1)}, bf16[128,512]{1,0:T(8,128)(2,1)S(1)}, u32[]{:S(2)}, u32[]{:S(2)}) %collective-permute-start.3) | collective-permute-done | bytes 131104 | tf_op jit(solution)/shard_map/ppermute | solution.py:363
  47.4 1.3 %collective-permute-start.11 = (bf16[96,512]{1,0:T(8,128)(2,1)S(1)}, bf16[96,512]{1,0:T(8,128)(2,1)S(1)}, u32[]{:S(2)}, u32[]{:S(2)}) collective-permute-start(bf16[96,512]{1,0:T(8,128)(2,1)S(1)} %slice.15), channel_id=1, source_target_pairs={{0,1},{1,0},{2,3},{3,2},{4,5},{5,4},{6,7},{7,6},{8,9},{9,8},{10,11... | collective-permute-start | bytes 294920 | tf_op jit(solution)/shard_map/ppermute | solution.py:356
  49.2 1.3 %shard_map.81 = (f32[96,512]{1,0:T(8,128)S(1)}, bf16[160,512]{1,0:T(8,128)(2,1)S(1)}) custom-call(bf16[256,512]{1,0:T(8,128)(2,1)S(1)} %get-tuple-element.37.refs_0_, bf16[2048,512]{1,0:T(8,128)(2,1)S(1)} %shard_map.80.refs_1_, bf16[256,2048]{1,0:T(8,128)(2,1)S(1)} %get-tuple-element.38.refs_2_), custom_call_target="tpu_custom_call" | custom-call | tf_op jit(solution)/shard_map/pallas_call | solution.py:245
  50.4 2.3 %collective-permute-start.9 = (bf16[160,512]{1,0:T(8,128)(2,1)S(1)}, bf16[160,512]{1,0:T(8,128)(2,1)S(1)}, u32[]{:S(2)}, u32[]{:S(2)}) collective-permute-start(bf16[160,512]{1,0:T(8,128)(2,1)S(1)} %get-tuple-element.39), channel_id=1, source_target_pairs={{0,2},{1,3},{2,0},{3,1},{4,6},{5,7},{6,4},{7,5},{8,10},{9,11},{10,... | collective-permute-start | bytes 491528 | tf_op jit(solution)/shard_map/ppermute | solution.py:356
  52.7 1.1 %shard_map.83 = bf16[96,512]{1,0:T(8,128)(2,1)S(1)} custom-call(bf16[96,512]{1,0:T(8,128)(2,1)S(1)} %collective-permute-done.11.refs_0_, bf16[2048,512]{1,0:T(8,128)(2,1)S(1)} %shard_map.80.refs_1_, bf16[256,2048]{1,0:T(8,128)(2,1)S(1)} %get-tuple-element.41.refs_2_), custom_call_target="tpu_custom_call" | custom-call | tf_op jit(solution)/shard_map/pallas_call | solution.py:245
  54.0 1.2 %shard_map.84 = bf16[160,512]{1,0:T(8,128)(2,1)S(1)} custom-call(bf16[160,512]{1,0:T(8,128)(2,1)S(1)} %collective-permute-done.10.refs_0_, bf16[2048,512]{1,0:T(8,128)(2,1)S(1)} %shard_map.80.refs_1_, bf16[256,2048]{1,0:T(8,128)(2,1)S(1)} %get-tuple-element.41.refs_2_), custom_call_target="tpu_custom_call" | custom-call | tf_op jit(solution)/shard_map/pallas_call | solution.py:245
  55.2 1.9 %collective-permute-start.12 = (bf16[160,512]{1,0:T(8,128)(2,1)S(1)}, bf16[160,512]{1,0:T(8,128)(2,1)S(1)}, u32[]{:S(2)}, u32[]{:S(2)}) collective-permute-start(bf16[160,512]{1,0:T(8,128)(2,1)S(1)} %shard_map.84), channel_id=1, source_target_pairs={{0,3},{1,2},{2,1},{3,0},{4,7},{5,6},{6,5},{7,4},{8,11},{9,10},{10,... | collective-permute-start | bytes 491528 | tf_op jit(solution)/shard_map/ppermute | solution.py:356
  57.2 1.3 %shard_map.86 = bf16[256,512]{1,0:T(8,128)(2,1)S(1)} custom-call(bf16[256,512]{1,0:T(8,128)(2,1)S(1)} %get-tuple-element.45.refs_0_, bf16[2048,512]{1,0:T(8,128)(2,1)S(1)} %shard_map.80.refs_1_, bf16[256,2048]{1,0:T(8,128)(2,1)S(1)} %get-tuple-element.46.refs_2_), custom_call_target="tpu_custom_call" | custom-call | tf_op jit(solution)/shard_map/pallas_call | solution.py:245
  58.4 1.0 collective-permute-start.15
  59.5 2.8 %collective-permute-start.14 = (bf16[96,512]{1,0:T(8,128)(2,1)S(1)}, bf16[96,512]{1,0:T(8,128)(2,1)S(1)}, u32[]{:S(2)}, u32[]{:S(2)}) collective-permute-start(bf16[96,512]{1,0:T(8,128)(2,1)S(1)} %shard_map.85), channel_id=1, source_target_pairs={{0,2},{1,3},{2,0},{3,1},{4,6},{5,7},{6,4},{7,5},{8,10},{9,11},{10,... | collective-permute-start | bytes 294920 | tf_op jit(solution)/shard_map/ppermute | solution.py:356
  62.3 1.3 %shard_map.82.own = f32[256,512]{1,0:T(8,128)S(1)} custom-call(bf16[256,512]{1,0:T(8,128)(2,1)S(1)} %get-tuple-element.27.refs_0_, bf16[2048,512]{1,0:T(8,128)(2,1)S(1)} %shard_map.80.refs_1_, bf16[256,2048]{1,0:T(8,128)(2,1)S(1)} %get-tuple-element.36.refs_2_, bf16[160,512]{1,0:T(8,128)(2,1)S(1)} %collective-permute-done.9.refs_3_), custom_call_target="tpu_custom_call" | custom-call | flops 10000000000 | tf_op jit(solution)/shard_map/pallas_call | solution.py:245
  63.6 1.3 %collective-permute-done.12.refs_0_ = bf16[160,512]{1,0:T(8,128)(2,1)S(1)} collective-permute-done((bf16[160,512]{1,0:T(8,128)(2,1)S(1)}, bf16[160,512]{1,0:T(8,128)(2,1)S(1)}, u32[]{:S(2)}, u32[]{:S(2)}) %collective-permute-start.12) | collective-permute-done | bytes 163872 | tf_op jit(solution)/shard_map/ppermute | solution.py:356
  64.8 6.1 %collective-permute-done.14.refs_1_ = bf16[96,512]{1,0:T(8,128)(2,1)S(1)} collective-permute-done((bf16[96,512]{1,0:T(8,128)(2,1)S(1)}, bf16[96,512]{1,0:T(8,128)(2,1)S(1)}, u32[]{:S(2)}, u32[]{:S(2)}) %collective-permute-start.14) | collective-permute-done | bytes 98336 | tf_op jit(solution)/shard_map/ppermute | solution.py:356
  71.8 32.5 %all_to_all.10 = bf16[32,32,512]{2,1,0:T(8,128)(2,1)S(1)} all-to-all(bf16[32,32,512]{2,1,0:T(8,128)(2,1)S(1)} %bitcast.9), channel_id=1, replica_groups=mesh['row'=8,'col'=4] {'row','col'}, dimensions={0} | all-to-all | bytes 2097152 | tf_op jit(solution)/shard_map/all_to_all | solution.py:450
  104.3 2.1 %shard_map.88 = f32[1024,512]{1,0:T(8,128)} custom-call(bf16[1024,1024]{1,0:T(8,128)(2,1)S(1)} %copy-done, bf16[1024,512]{1,0:T(8,128)(2,1)S(1)} %bitcast.8), custom_call_target="tpu_custom_call" | custom-call | tf_op jit(solution)/shard_map/pallas_call | solution.py:458
  (47 shorter events, 5.7 us)
Async XLA Ops:
  0.0 10.4 %copy-start.2 = (s32[32]{0:T(128)S(1)}, s32[32]{0:T(128)}, u32[]{:S(2)}) copy-start(s32[32]{0:T(128)} %counts_hbm.1) | copy-start | bytes 388
  0.0 10.7 %copy-start.1 = (s32[8192]{0:T(1024)S(1)}, s32[8192]{0:T(1024)}, u32[]{:S(2)}) copy-start(s32[8192]{0:T(1024)} %param.11) | copy-start | bytes 98308
  3.3 29.3 %all-to-all-start = ((bf16[32,104,128]{2,1,0:T(8,128)(2,1)}), bf16[32,104,128]{2,1,0:T(8,128)(2,1)S(1)}, u32[]{:S(2)}, u32[]{:S(2)}) async-start(bf16[32,104,128]{2,1,0:T(8,128)(2,1)} %shard_map.73), calls=%async_computation | async-start | bytes 1703936 | tf_op jit(solution)/shard_map/all_to_all | solution.py:330
  33.0 7.5 %collective-permute-start = (bf16[256,512]{1,0:T(8,128)(2,1)S(1)}, bf16[256,512]{1,0:T(8,128)(2,1)S(1)}, u32[]{:S(2)}, u32[]{:S(2)}) collective-permute-start(bf16[256,512]{1,0:T(8,128)(2,1)S(1)} %get-tuple-element.27.refs_0_), channel_id=1, source_target_pairs={{0,8},{4,20},{8,0},{12,28},{16,24},{20,4},{24,16},{28,12},{1,9},{5... | collective-permute-start | bytes 786440 | tf_op jit(solution)/shard_map/ppermute | solution.py:363
  34.3 8.4 %collective-permute-start.1 = (bf16[256,512]{1,0:T(8,128)(2,1)S(1)}, bf16[256,512]{1,0:T(8,128)(2,1)S(1)}, u32[]{:S(2)}, u32[]{:S(2)}) collective-permute-start(bf16[256,512]{1,0:T(8,128)(2,1)S(1)} %get-tuple-element.27.refs_0_), channel_id=1, source_target_pairs={{0,16},{4,12},{8,24},{12,4},{16,0},{20,28},{24,8},{28,20},{1,17},{... | collective-permute-start | bytes 786440 | tf_op jit(solution)/shard_map/ppermute | solution.py:363
  34.6 12.8 %collective-permute-start.4 = (bf16[256,512]{1,0:T(8,128)(2,1)S(1)}, bf16[256,512]{1,0:T(8,128)(2,1)S(1)}, u32[]{:S(2)}, u32[]{:S(2)}) collective-permute-start(bf16[256,512]{1,0:T(8,128)(2,1)S(1)} %get-tuple-element.27.refs_0_), channel_id=1, source_target_pairs={{0,1},{1,0},{2,3},{3,2},{4,5},{5,4},{6,7},{7,6},{8,9},{9,8},{10,11... | collective-permute-start | bytes 786440 | tf_op jit(solution)/shard_map/ppermute | solution.py:356
  35.2 12.2 %collective-permute-start.5 = (bf16[256,512]{1,0:T(8,128)(2,1)S(1)}, bf16[256,512]{1,0:T(8,128)(2,1)S(1)}, u32[]{:S(2)}, u32[]{:S(2)}) collective-permute-start(bf16[256,512]{1,0:T(8,128)(2,1)S(1)} %get-tuple-element.27.refs_0_), channel_id=1, source_target_pairs={{0,2},{1,3},{2,0},{3,1},{4,6},{5,7},{6,4},{7,5},{8,10},{9,11},{10,... | collective-permute-start | bytes 786440 | tf_op jit(solution)/shard_map/ppermute | solution.py:356
  40.5 4.8 %collective-permute-start.2 = (bf16[128,512]{1,0:T(8,128)(2,1)S(1)}, bf16[128,512]{1,0:T(8,128)(2,1)S(1)}, u32[]{:S(2)}, u32[]{:S(2)}) collective-permute-start(bf16[128,512]{1,0:T(8,128)(2,1)S(1)} %slice.12), channel_id=1, source_target_pairs={{0,16},{4,12},{8,24},{12,4},{16,0},{20,28},{24,8},{28,20},{1,17},{... | collective-permute-start | bytes 393224 | tf_op jit(solution)/shard_map/ppermute | solution.py:363
  42.7 4.2 %collective-permute-start.3 = (bf16[128,512]{1,0:T(8,128)(2,1)S(1)}, bf16[128,512]{1,0:T(8,128)(2,1)S(1)}, u32[]{:S(2)}, u32[]{:S(2)}) collective-permute-start(bf16[128,512]{1,0:T(8,128)(2,1)S(1)} %slice.16), channel_id=1, source_target_pairs={{0,8},{4,20},{8,0},{12,28},{16,24},{20,4},{24,16},{28,12},{1,9},{5... | collective-permute-start | bytes 393224 | tf_op jit(solution)/shard_map/ppermute | solution.py:363
  42.8 4.6 %collective-permute-start.6 = (bf16[256,512]{1,0:T(8,128)(2,1)S(1)}, bf16[256,512]{1,0:T(8,128)(2,1)S(1)}, u32[]{:S(2)}, u32[]{:S(2)}) collective-permute-start(bf16[256,512]{1,0:T(8,128)(2,1)S(1)} %get-tuple-element.27.refs_0_), channel_id=1, source_target_pairs={{0,4},{4,0},{8,12},{12,8},{16,20},{20,16},{24,28},{28,24},{1,5},{5... | collective-permute-start | bytes 786440 | tf_op jit(solution)/shard_map/ppermute | solution.py:363
  45.3 3.7 %collective-permute-start.7 = (bf16[512,512]{1,0:T(8,128)(2,1)S(1)}, bf16[512,512]{1,0:T(8,128)(2,1)S(1)}, u32[]{:S(2)}, u32[]{:S(2)}) collective-permute-start(bf16[512,512]{1,0:T(8,128)(2,1)S(1)} %shard_map.76.refs_1_), channel_id=1, source_target_pairs={{0,4},{4,0},{8,12},{12,8},{16,20},{20,16},{24,28},{28,24},{1,5},{5... | collective-permute-start | bytes 1572872 | tf_op jit(solution)/shard_map/ppermute | solution.py:363
  46.9 2.1 %collective-permute-start.8 = (bf16[256,512]{1,0:T(8,128)(2,1)S(1)}, bf16[256,512]{1,0:T(8,128)(2,1)S(1)}, u32[]{:S(2)}, u32[]{:S(2)}) collective-permute-start(bf16[256,512]{1,0:T(8,128)(2,1)S(1)} %shard_map.78.refs_2_), channel_id=1, source_target_pairs={{0,4},{4,0},{8,12},{12,8},{16,20},{20,16},{24,28},{28,24},{1,5},{5... | collective-permute-start | bytes 786440 | tf_op jit(solution)/shard_map/ppermute | solution.py:363
  47.4 5.4 %collective-permute-start.11 = (bf16[96,512]{1,0:T(8,128)(2,1)S(1)}, bf16[96,512]{1,0:T(8,128)(2,1)S(1)}, u32[]{:S(2)}, u32[]{:S(2)}) collective-permute-start(bf16[96,512]{1,0:T(8,128)(2,1)S(1)} %slice.15), channel_id=1, source_target_pairs={{0,1},{1,0},{2,3},{3,2},{4,5},{5,4},{6,7},{7,6},{8,9},{9,8},{10,11... | collective-permute-start | bytes 294920 | tf_op jit(solution)/shard_map/ppermute | solution.py:356
  48.7 5.3 %collective-permute-start.10 = (bf16[160,512]{1,0:T(8,128)(2,1)S(1)}, bf16[160,512]{1,0:T(8,128)(2,1)S(1)}, u32[]{:S(2)}, u32[]{:S(2)}) collective-permute-start(bf16[160,512]{1,0:T(8,128)(2,1)S(1)} %slice.14), channel_id=1, source_target_pairs={{0,1},{1,0},{2,3},{3,2},{4,5},{5,4},{6,7},{7,6},{8,9},{9,8},{10,11... | collective-permute-start | bytes 491528 | tf_op jit(solution)/shard_map/ppermute | solution.py:356
  50.4 11.8 %collective-permute-start.9 = (bf16[160,512]{1,0:T(8,128)(2,1)S(1)}, bf16[160,512]{1,0:T(8,128)(2,1)S(1)}, u32[]{:S(2)}, u32[]{:S(2)}) collective-permute-start(bf16[160,512]{1,0:T(8,128)(2,1)S(1)} %get-tuple-element.39), channel_id=1, source_target_pairs={{0,2},{1,3},{2,0},{3,1},{4,6},{5,7},{6,4},{7,5},{8,10},{9,11},{10,... | collective-permute-start | bytes 491528 | tf_op jit(solution)/shard_map/ppermute | solution.py:356
  53.8 5.6 %collective-permute-start.13 = (bf16[96,512]{1,0:T(8,128)(2,1)S(1)}, bf16[96,512]{1,0:T(8,128)(2,1)S(1)}, u32[]{:S(2)}, u32[]{:S(2)}) collective-permute-start(bf16[96,512]{1,0:T(8,128)(2,1)S(1)} %shard_map.83), channel_id=1, source_target_pairs={{0,1},{1,0},{2,3},{3,2},{4,5},{5,4},{6,7},{7,6},{8,9},{9,8},{10,11... | collective-permute-start | bytes 294920 | tf_op jit(solution)/shard_map/ppermute | solution.py:356
  55.2 9.6 %collective-permute-start.12 = (bf16[160,512]{1,0:T(8,128)(2,1)S(1)}, bf16[160,512]{1,0:T(8,128)(2,1)S(1)}, u32[]{:S(2)}, u32[]{:S(2)}) collective-permute-start(bf16[160,512]{1,0:T(8,128)(2,1)S(1)} %shard_map.84), channel_id=1, source_target_pairs={{0,3},{1,2},{2,1},{3,0},{4,7},{5,6},{6,5},{7,4},{8,11},{9,10},{10,... | collective-permute-start | bytes 491528 | tf_op jit(solution)/shard_map/ppermute | solution.py:356
  58.4 12.9 %collective-permute-start.15 = (bf16[256,512]{1,0:T(8,128)(2,1)S(1)}, bf16[256,512]{1,0:T(8,128)(2,1)S(1)}, u32[]{:S(2)}, u32[]{:S(2)}) collective-permute-start(bf16[256,512]{1,0:T(8,128)(2,1)S(1)} %shard_map.86), channel_id=1, source_target_pairs={{0,1},{1,0},{2,3},{3,2},{4,5},{5,4},{6,7},{7,6},{8,9},{9,8},{10,11... | collective-permute-start | bytes 786440 | tf_op jit(solution)/shard_map/ppermute | solution.py:356
  59.5 11.5 %collective-permute-start.14 = (bf16[96,512]{1,0:T(8,128)(2,1)S(1)}, bf16[96,512]{1,0:T(8,128)(2,1)S(1)}, u32[]{:S(2)}, u32[]{:S(2)}) collective-permute-start(bf16[96,512]{1,0:T(8,128)(2,1)S(1)} %shard_map.85), channel_id=1, source_target_pairs={{0,2},{1,3},{2,0},{3,1},{4,6},{5,7},{6,4},{7,5},{8,10},{9,11},{10,... | collective-permute-start | bytes 294920 | tf_op jit(solution)/shard_map/ppermute | solution.py:356
  63.6 40.8 %copy-start = (bf16[1024,1024]{1,0:T(8,128)(2,1)S(1)}, bf16[1024,1024]{1,0:T(8,128)(2,1)}, u32[]{:S(2)}) copy-start(bf16[1024,1024]{1,0:T(8,128)(2,1)} %interp.1) | copy-start | bytes 6291460

commit v9 on v7

--- a/solution.py
+++ b/solution.py
@@ -394,7 +394,6 @@
         *[left[mask][0] for mask in direct],
         flops=20 * 10**9,
     )
-    *held, mirrored[0] = lax.optimization_barrier((*held, mirrored[0]))
     left.update((mask, [rows]) for mask, rows in zip(direct, held))
     for mask in range(3, col_count):
         if mask not in left:

time: 107 us -> 107 us (level)
  no operation moved by 1% of the time
where the time goes in v9:
time: 107 us; the launch traced here: 106 us
  waiting for transfers between devices  36.1 us (34%)
  blocking collectives  33 us (31%)
  starting transfers between devices  19.7 us (18%)
  Pallas kernels  15.4 us (14%)
  other arithmetic  1.73 us (2%)
    all_to_all x1, blocking collectives, shards(): lax.all_to_all(picked.reshape(box_total, per_owner, NORB), ('row', 'col')...  33 us
    all_to_all x1, waiting for transfers between devices, shards(): lax.all_to_all(outgoing, ('row', 'col'), split_axis=0, concat_axis=0, til...  20.2 us
    ppermute x9, waiting for transfers between devices, swap(): return lax.ppermute(rows, 'col', [(i, i ^ mask) for i in range(col_count)])  10.3 us
    pallas_call x13, Pallas kernels, local(): pl.pallas_call(kernel, out_shape=out, in_specs=[spec(n, a) for n, a in en...  9.66 us
    all_to_all x1, starting transfers between devices, shards(): lax.all_to_all(outgoing, ('row', 'col'), split_axis=0, concat_axis=0, til...  7.1 us
    ppermute x9, starting transfers between devices, swap(): return lax.ppermute(rows, 'col', [(i, i ^ mask) for i in range(col_count)])  6.4 us
    ppermute x7, starting transfers between devices, flip(): return lax.ppermute(rows, 'row', [(i, i ^ mask) for i in range(row_count)])  6.16 us
    ppermute x7, waiting for transfers between devices, flip(): return lax.ppermute(rows, 'row', [(i, i ^ mask) for i in range(row_count)])  5.53 us
  transfers between devices with their start and end apart: 17, of which 10 were waited for; matrix products, arithmetic and copies ran while one was open for 2% of the time, Pallas kernels for 9%

profile of v9, /device:TPU:1, one launch (start us, length us, event | category | flops | bytes accessed | tf_op | source)
XLA Modules:
  0.0 106.3 jit_solution(16514304702776351458)
XLA Ops:
  0.0 3.3 %shard_map.73 = bf16[32,104,128]{2,1,0:T(8,128)(2,1)} custom-call(s32[32]{0:T(128)} %counts_hbm.1, s32[8,128]{1,0:T(8,128)} %bitcast.13, s32[64,128]{1,0:T(8,128)} %bitcast.10, s32[8,128]{1,0:T(8,128)} %bitcast.14, bf16[1024,512]{1,0:T(8,128)(2,1)} %orbitals_hbm.1), custom_call_target="tpu_custom_call" | custom-call | flops 805306368 | bytes 2097152 | tf_op jit(solution)/shard_map/pallas_call | solution.py:297
  3.3 7.1 %all-to-all-start = ((bf16[32,104,128]{2,1,0:T(8,128)(2,1)}), bf16[32,104,128]{2,1,0:T(8,128)(2,1)S(1)}, u32[]{:S(2)}, u32[]{:S(2)}) async-start(bf16[32,104,128]{2,1,0:T(8,128)(2,1)} %shard_map.73), calls=%async_computation | async-start | bytes 1703936 | tf_op jit(solution)/shard_map/all_to_all | solution.py:323
  10.7 1.2 %select_reduce_fusion = s32[256]{0:T(256)S(1)} fusion(s32[8192]{0:T(1024)S(1)} %copy-done.1, s32[256]{0:T(256)S(1)} %iota_add_fusion), kind=kLoop, calls=%fused_computation | loop fusion | flops 6291200 | bytes 34816 | tf_op jit(solution)/shard_map/reduce_sum | solution.py:329
  12.4 20.2 %all-to-all-done.received = bf16[32,104,128]{2,1,0:T(8,128)(2,1)S(1)} async-done(((bf16[32,104,128]{2,1,0:T(8,128)(2,1)}), bf16[32,104,128]{2,1,0:T(8,128)(2,1)S(1)}, u32[]{:S(2)}, u32[]{:S(2)}) %all-to-all-start) | async-done | bytes 852000 | tf_op jit(solution)/shard_map/all_to_all | solution.py:323
  33.0 1.3 %collective-permute-start = (bf16[256,512]{1,0:T(8,128)(2,1)S(1)}, bf16[256,512]{1,0:T(8,128)(2,1)S(1)}, u32[]{:S(2)}, u32[]{:S(2)}) collective-permute-start(bf16[256,512]{1,0:T(8,128)(2,1)S(1)} %get-tuple-element.24.refs_0_), channel_id=1, source_target_pairs={{0,8},{4,12},{8,0},{12,4},{16,24},{20,28},{24,16},{28,20},{1,9},{5... | collective-permute-start | bytes 786440 | tf_op jit(solution)/shard_map/ppermute | solution.py:356
  35.4 2.8 %shard_map.75 = (bf16[256,2048]{1,0:T(8,128)(2,1)S(1)}, bf16[256,2048]{1,0:T(8,128)(2,1)S(1)}, bf16[256,2048]{1,0:T(8,128)(2,1)S(1)}, bf16[256,2048]{1,0:T(8,128)(2,1)S(1)}) custom-call(s32[4]{0:T(128)S(1)} %iota_xor_fusion.scalars, bf16[1024,2048]{1,0:T(8,128)(2,1)} %coulomb.1), custom_call_target="tpu_custom_call" | custom-call | tf_op jit(solution)/shard_map/pallas_call | solution.py:238
  38.2 2.7 %collective-permute-done.refs_0_ = bf16[256,512]{1,0:T(8,128)(2,1)S(1)} collective-permute-done((bf16[256,512]{1,0:T(8,128)(2,1)S(1)}, bf16[256,512]{1,0:T(8,128)(2,1)S(1)}, u32[]{:S(2)}, u32[]{:S(2)}) %collective-permute-start) | collective-permute-done | bytes 262176 | tf_op jit(solution)/shard_map/ppermute | solution.py:356
  40.9 1.3 %collective-permute-start.2 = (bf16[128,512]{1,0:T(8,128)(2,1)S(1)}, bf16[128,512]{1,0:T(8,128)(2,1)S(1)}, u32[]{:S(2)}, u32[]{:S(2)}) collective-permute-start(bf16[128,512]{1,0:T(8,128)(2,1)S(1)} %slice.12), channel_id=1, source_target_pairs={{0,16},{4,20},{8,24},{12,28},{16,0},{20,4},{24,8},{28,12},{1,17},{... | collective-permute-start | bytes 393224 | tf_op jit(solution)/shard_map/ppermute | solution.py:356
  42.7 1.3 %collective-permute-start.4 = (bf16[256,512]{1,0:T(8,128)(2,1)S(1)}, bf16[256,512]{1,0:T(8,128)(2,1)S(1)}, u32[]{:S(2)}, u32[]{:S(2)}) collective-permute-start(bf16[256,512]{1,0:T(8,128)(2,1)S(1)} %get-tuple-element.24.refs_0_), channel_id=1, source_target_pairs={{0,4},{4,0},{8,12},{12,8},{16,20},{20,16},{24,28},{28,24},{1,5},{5... | collective-permute-start | bytes 786440 | tf_op jit(solution)/shard_map/ppermute | solution.py:356
  44.0 2.1 %collective-permute-done.2.refs_0_ = bf16[128,512]{1,0:T(8,128)(2,1)S(1)} collective-permute-done((bf16[128,512]{1,0:T(8,128)(2,1)S(1)}, bf16[128,512]{1,0:T(8,128)(2,1)S(1)}, u32[]{:S(2)}, u32[]{:S(2)}) %collective-permute-start.2) | collective-permute-done | bytes 131104 | tf_op jit(solution)/shard_map/ppermute | solution.py:356
  47.4 1.0 collective-permute-start.6
  48.6 1.5 %collective-permute-start.10 = (bf16[160,512]{1,0:T(8,128)(2,1)S(1)}, bf16[160,512]{1,0:T(8,128)(2,1)S(1)}, u32[]{:S(2)}, u32[]{:S(2)}) collective-permute-start(bf16[160,512]{1,0:T(8,128)(2,1)S(1)} %slice.14), channel_id=1, source_target_pairs={{0,1},{1,0},{2,3},{3,2},{4,5},{5,4},{6,7},{7,6},{8,9},{9,8},{10,11... | collective-permute-start | bytes 491528 | tf_op jit(solution)/shard_map/ppermute | solution.py:349
  50.3 1.3 %shard_map.81 = (f32[96,512]{1,0:T(8,128)S(1)}, bf16[160,512]{1,0:T(8,128)(2,1)S(1)}) custom-call(bf16[256,512]{1,0:T(8,128)(2,1)S(1)} %get-tuple-element.31.refs_0_, bf16[2048,512]{1,0:T(8,128)(2,1)S(1)} %shard_map.79.refs_1_, bf16[256,2048]{1,0:T(8,128)(2,1)S(1)} %get-tuple-element.32.refs_2_), custom_call_target="tpu_custom_call" | custom-call | tf_op jit(solution)/shard_map/pallas_call | solution.py:238
  52.1 1.1 %shard_map.83 = bf16[96,512]{1,0:T(8,128)(2,1)S(1)} custom-call(bf16[96,512]{1,0:T(8,128)(2,1)S(1)} %collective-permute-done.11.refs_0_, bf16[2048,512]{1,0:T(8,128)(2,1)S(1)} %shard_map.79.refs_1_, bf16[256,2048]{1,0:T(8,128)(2,1)S(1)} %get-tuple-element.35.refs_2_), custom_call_target="tpu_custom_call" | custom-call | tf_op jit(solution)/shard_map/pallas_call | solution.py:238
  54.4 1.2 %shard_map.84 = bf16[160,512]{1,0:T(8,128)(2,1)S(1)} custom-call(bf16[160,512]{1,0:T(8,128)(2,1)S(1)} %collective-permute-done.10.refs_0_, bf16[2048,512]{1,0:T(8,128)(2,1)S(1)} %shard_map.79.refs_1_, bf16[256,2048]{1,0:T(8,128)(2,1)S(1)} %get-tuple-element.35.refs_2_), custom_call_target="tpu_custom_call" | custom-call | tf_op jit(solution)/shard_map/pallas_call | solution.py:238
  55.6 2.0 %collective-permute-start.12 = (bf16[160,512]{1,0:T(8,128)(2,1)S(1)}, bf16[160,512]{1,0:T(8,128)(2,1)S(1)}, u32[]{:S(2)}, u32[]{:S(2)}) collective-permute-start(bf16[160,512]{1,0:T(8,128)(2,1)S(1)} %shard_map.84), channel_id=1, source_target_pairs={{0,3},{1,2},{2,1},{3,0},{4,7},{5,6},{6,5},{7,4},{8,11},{9,10},{10,... | collective-permute-start | bytes 491528 | tf_op jit(solution)/shard_map/ppermute | solution.py:349
  57.7 1.3 %shard_map.86 = bf16[256,512]{1,0:T(8,128)(2,1)S(1)} custom-call(bf16[256,512]{1,0:T(8,128)(2,1)S(1)} %get-tuple-element.39.refs_0_, bf16[2048,512]{1,0:T(8,128)(2,1)S(1)} %shard_map.79.refs_1_, bf16[256,2048]{1,0:T(8,128)(2,1)S(1)} %get-tuple-element.40.refs_2_), custom_call_target="tpu_custom_call" | custom-call | tf_op jit(solution)/shard_map/pallas_call | solution.py:238
  59.0 1.1 %collective-permute-done.13.other = bf16[96,512]{1,0:T(8,128)(2,1)S(1)} collective-permute-done((bf16[96,512]{1,0:T(8,128)(2,1)S(1)}, bf16[96,512]{1,0:T(8,128)(2,1)S(1)}, u32[]{:S(2)}, u32[]{:S(2)}) %collective-permute-start.13) | collective-permute-done | bytes 98336 | tf_op jit(solution)/shard_map/ppermute | solution.py:349
  60.2 0.9 collective-permute-start.14
  61.1 1.3 %shard_map.82.own = f32[256,512]{1,0:T(8,128)S(1)} custom-call(bf16[256,512]{1,0:T(8,128)(2,1)S(1)} %get-tuple-element.24.refs_0_, bf16[2048,512]{1,0:T(8,128)(2,1)S(1)} %shard_map.79.refs_1_, bf16[256,2048]{1,0:T(8,128)(2,1)S(1)} %get-tuple-element.30.refs_2_, bf16[160,512]{1,0:T(8,128)(2,1)S(1)} %collective-permute-done.9.refs_3_), custom_call_target="tpu_custom_call" | custom-call | flops 10000000000 | tf_op jit(solution)/shard_map/pallas_call | solution.py:238
  62.4 1.6 %collective-permute-done.12.refs_0_ = bf16[160,512]{1,0:T(8,128)(2,1)S(1)} collective-permute-done((bf16[160,512]{1,0:T(8,128)(2,1)S(1)}, bf16[160,512]{1,0:T(8,128)(2,1)S(1)}, u32[]{:S(2)}, u32[]{:S(2)}) %collective-permute-start.12) | collective-permute-done | bytes 163872 | tf_op jit(solution)/shard_map/ppermute | solution.py:349
  64.0 6.8 %collective-permute-done.14.refs_1_ = bf16[96,512]{1,0:T(8,128)(2,1)S(1)} collective-permute-done((bf16[96,512]{1,0:T(8,128)(2,1)S(1)}, bf16[96,512]{1,0:T(8,128)(2,1)S(1)}, u32[]{:S(2)}, u32[]{:S(2)}) %collective-permute-start.14) | collective-permute-done | bytes 98336 | tf_op jit(solution)/shard_map/ppermute | solution.py:349
  71.3 33.0 %all_to_all.10 = bf16[32,32,512]{2,1,0:T(8,128)(2,1)S(1)} all-to-all(bf16[32,32,512]{2,1,0:T(8,128)(2,1)S(1)} %bitcast.9), channel_id=1, replica_groups=mesh['row'=8,'col'=4] {'row','col'}, dimensions={0} | all-to-all | bytes 2097152 | tf_op jit(solution)/shard_map/all_to_all | solution.py:440
  104.3 2.1 %shard_map.88 = f32[1024,512]{1,0:T(8,128)} custom-call(bf16[1024,1024]{1,0:T(8,128)(2,1)S(1)} %copy-done, bf16[1024,512]{1,0:T(8,128)(2,1)S(1)} %bitcast.8), custom_call_target="tpu_custom_call" | custom-call | tf_op jit(solution)/shard_map/pallas_call | solution.py:448
  (47 shorter events, 6.8 us)
Async XLA Ops:
  0.0 10.4 %copy-start.2 = (s32[32]{0:T(128)S(1)}, s32[32]{0:T(128)}, u32[]{:S(2)}) copy-start(s32[32]{0:T(128)} %counts_hbm.1) | copy-start | bytes 388
  0.0 10.7 %copy-start.1 = (s32[8192]{0:T(1024)S(1)}, s32[8192]{0:T(1024)}, u32[]{:S(2)}) copy-start(s32[8192]{0:T(1024)} %param.11) | copy-start | bytes 98308
  3.3 29.3 %all-to-all-start = ((bf16[32,104,128]{2,1,0:T(8,128)(2,1)}), bf16[32,104,128]{2,1,0:T(8,128)(2,1)S(1)}, u32[]{:S(2)}, u32[]{:S(2)}) async-start(bf16[32,104,128]{2,1,0:T(8,128)(2,1)} %shard_map.73), calls=%async_computation | async-start | bytes 1703936 | tf_op jit(solution)/shard_map/all_to_all | solution.py:323
  33.0 7.9 %collective-permute-start = (bf16[256,512]{1,0:T(8,128)(2,1)S(1)}, bf16[256,512]{1,0:T(8,128)(2,1)S(1)}, u32[]{:S(2)}, u32[]{:S(2)}) collective-permute-start(bf16[256,512]{1,0:T(8,128)(2,1)S(1)} %get-tuple-element.24.refs_0_), channel_id=1, source_target_pairs={{0,8},{4,12},{8,0},{12,4},{16,24},{20,28},{24,16},{28,20},{1,9},{5... | collective-permute-start | bytes 786440 | tf_op jit(solution)/shard_map/ppermute | solution.py:356
  34.3 8.1 %collective-permute-start.1 = (bf16[256,512]{1,0:T(8,128)(2,1)S(1)}, bf16[256,512]{1,0:T(8,128)(2,1)S(1)}, u32[]{:S(2)}, u32[]{:S(2)}) collective-permute-start(bf16[256,512]{1,0:T(8,128)(2,1)S(1)} %get-tuple-element.24.refs_0_), channel_id=1, source_target_pairs={{0,16},{4,20},{8,24},{12,28},{16,0},{20,4},{24,8},{28,12},{1,17},{... | collective-permute-start | bytes 786440 | tf_op jit(solution)/shard_map/ppermute | solution.py:356
  34.6 13.9 %collective-permute-start.7 = (bf16[256,512]{1,0:T(8,128)(2,1)S(1)}, bf16[256,512]{1,0:T(8,128)(2,1)S(1)}, u32[]{:S(2)}, u32[]{:S(2)}) collective-permute-start(bf16[256,512]{1,0:T(8,128)(2,1)S(1)} %get-tuple-element.24.refs_0_), channel_id=1, source_target_pairs={{0,1},{1,0},{2,3},{3,2},{4,5},{5,4},{6,7},{7,6},{8,9},{9,8},{10,11... | collective-permute-start | bytes 786440 | tf_op jit(solution)/shard_map/ppermute | solution.py:349
  35.2 13.3 %collective-permute-start.8 = (bf16[256,512]{1,0:T(8,128)(2,1)S(1)}, bf16[256,512]{1,0:T(8,128)(2,1)S(1)}, u32[]{:S(2)}, u32[]{:S(2)}) collective-permute-start(bf16[256,512]{1,0:T(8,128)(2,1)S(1)} %get-tuple-element.24.refs_0_), channel_id=1, source_target_pairs={{0,2},{1,3},{2,0},{3,1},{4,6},{5,7},{6,4},{7,5},{8,10},{9,11},{10,... | collective-permute-start | bytes 786440 | tf_op jit(solution)/shard_map/ppermute | solution.py:349
  40.9 5.3 %collective-permute-start.2 = (bf16[128,512]{1,0:T(8,128)(2,1)S(1)}, bf16[128,512]{1,0:T(8,128)(2,1)S(1)}, u32[]{:S(2)}, u32[]{:S(2)}) collective-permute-start(bf16[128,512]{1,0:T(8,128)(2,1)S(1)} %slice.12), channel_id=1, source_target_pairs={{0,16},{4,20},{8,24},{12,28},{16,0},{20,4},{24,8},{28,12},{1,17},{... | collective-permute-start | bytes 393224 | tf_op jit(solution)/shard_map/ppermute | solution.py:356
  42.4 5.0 %collective-permute-start.3 = (bf16[128,512]{1,0:T(8,128)(2,1)S(1)}, bf16[128,512]{1,0:T(8,128)(2,1)S(1)}, u32[]{:S(2)}, u32[]{:S(2)}) collective-permute-start(bf16[128,512]{1,0:T(8,128)(2,1)S(1)} %slice.16), channel_id=1, source_target_pairs={{0,8},{4,12},{8,0},{12,4},{16,24},{20,28},{24,16},{28,20},{1,9},{5... | collective-permute-start | bytes 393224 | tf_op jit(solution)/shard_map/ppermute | solution.py:356
  42.7 7.4 %collective-permute-start.4 = (bf16[256,512]{1,0:T(8,128)(2,1)S(1)}, bf16[256,512]{1,0:T(8,128)(2,1)S(1)}, u32[]{:S(2)}, u32[]{:S(2)}) collective-permute-start(bf16[256,512]{1,0:T(8,128)(2,1)S(1)} %get-tuple-element.24.refs_0_), channel_id=1, source_target_pairs={{0,4},{4,0},{8,12},{12,8},{16,20},{20,16},{24,28},{28,24},{1,5},{5... | collective-permute-start | bytes 786440 | tf_op jit(solution)/shard_map/ppermute | solution.py:356
  46.2 4.0 %collective-permute-start.5 = (bf16[512,512]{1,0:T(8,128)(2,1)S(1)}, bf16[512,512]{1,0:T(8,128)(2,1)S(1)}, u32[]{:S(2)}, u32[]{:S(2)}) collective-permute-start(bf16[512,512]{1,0:T(8,128)(2,1)S(1)} %shard_map.76.refs_1_), channel_id=1, source_target_pairs={{0,4},{4,0},{8,12},{12,8},{16,20},{20,16},{24,28},{28,24},{1,5},{5... | collective-permute-start | bytes 1572872 | tf_op jit(solution)/shard_map/ppermute | solution.py:356
  47.4 2.7 %collective-permute-start.6 = (bf16[256,512]{1,0:T(8,128)(2,1)S(1)}, bf16[256,512]{1,0:T(8,128)(2,1)S(1)}, u32[]{:S(2)}, u32[]{:S(2)}) collective-permute-start(bf16[256,512]{1,0:T(8,128)(2,1)S(1)} %shard_map.78.refs_2_), channel_id=1, source_target_pairs={{0,4},{4,0},{8,12},{12,8},{16,20},{20,16},{24,28},{28,24},{1,5},{5... | collective-permute-start | bytes 786440 | tf_op jit(solution)/shard_map/ppermute | solution.py:356
  48.5 3.5 %collective-permute-start.11 = (bf16[96,512]{1,0:T(8,128)(2,1)S(1)}, bf16[96,512]{1,0:T(8,128)(2,1)S(1)}, u32[]{:S(2)}, u32[]{:S(2)}) collective-permute-start(bf16[96,512]{1,0:T(8,128)(2,1)S(1)} %slice.15), channel_id=1, source_target_pairs={{0,1},{1,0},{2,3},{3,2},{4,5},{5,4},{6,7},{7,6},{8,9},{9,8},{10,11... | collective-permute-start | bytes 294920 | tf_op jit(solution)/shard_map/ppermute | solution.py:349
  48.6 5.8 %collective-permute-start.10 = (bf16[160,512]{1,0:T(8,128)(2,1)S(1)}, bf16[160,512]{1,0:T(8,128)(2,1)S(1)}, u32[]{:S(2)}, u32[]{:S(2)}) collective-permute-start(bf16[160,512]{1,0:T(8,128)(2,1)S(1)} %slice.14), channel_id=1, source_target_pairs={{0,1},{1,0},{2,3},{3,2},{4,5},{5,4},{6,7},{7,6},{8,9},{9,8},{10,11... | collective-permute-start | bytes 491528 | tf_op jit(solution)/shard_map/ppermute | solution.py:349
  51.6 9.5 %collective-permute-start.9 = (bf16[160,512]{1,0:T(8,128)(2,1)S(1)}, bf16[160,512]{1,0:T(8,128)(2,1)S(1)}, u32[]{:S(2)}, u32[]{:S(2)}) collective-permute-start(bf16[160,512]{1,0:T(8,128)(2,1)S(1)} %get-tuple-element.33), channel_id=1, source_target_pairs={{0,2},{1,3},{2,0},{3,1},{4,6},{5,7},{6,4},{7,5},{8,10},{9,11},{10,... | collective-permute-start | bytes 491528 | tf_op jit(solution)/shard_map/ppermute | solution.py:349
  53.2 7.0 %collective-permute-start.13 = (bf16[96,512]{1,0:T(8,128)(2,1)S(1)}, bf16[96,512]{1,0:T(8,128)(2,1)S(1)}, u32[]{:S(2)}, u32[]{:S(2)}) collective-permute-start(bf16[96,512]{1,0:T(8,128)(2,1)S(1)} %shard_map.83), channel_id=1, source_target_pairs={{0,1},{1,0},{2,3},{3,2},{4,5},{5,4},{6,7},{7,6},{8,9},{9,8},{10,11... | collective-permute-start | bytes 294920 | tf_op jit(solution)/shard_map/ppermute | solution.py:349
  55.6 8.3 %collective-permute-start.12 = (bf16[160,512]{1,0:T(8,128)(2,1)S(1)}, bf16[160,512]{1,0:T(8,128)(2,1)S(1)}, u32[]{:S(2)}, u32[]{:S(2)}) collective-permute-start(bf16[160,512]{1,0:T(8,128)(2,1)S(1)} %shard_map.84), channel_id=1, source_target_pairs={{0,3},{1,2},{2,1},{3,0},{4,7},{5,6},{6,5},{7,4},{8,11},{9,10},{10,... | collective-permute-start | bytes 491528 | tf_op jit(solution)/shard_map/ppermute | solution.py:349
  58.9 11.8 %collective-permute-start.15 = (bf16[256,512]{1,0:T(8,128)(2,1)S(1)}, bf16[256,512]{1,0:T(8,128)(2,1)S(1)}, u32[]{:S(2)}, u32[]{:S(2)}) collective-permute-start(bf16[256,512]{1,0:T(8,128)(2,1)S(1)} %shard_map.86), channel_id=1, source_target_pairs={{0,1},{1,0},{2,3},{3,2},{4,5},{5,4},{6,7},{7,6},{8,9},{9,8},{10,11... | collective-permute-start | bytes 786440 | tf_op jit(solution)/shard_map/ppermute | solution.py:349
  60.2 10.6 %collective-permute-start.14 = (bf16[96,512]{1,0:T(8,128)(2,1)S(1)}, bf16[96,512]{1,0:T(8,128)(2,1)S(1)}, u32[]{:S(2)}, u32[]{:S(2)}) collective-permute-start(bf16[96,512]{1,0:T(8,128)(2,1)S(1)} %shard_map.85), channel_id=1, source_target_pairs={{0,2},{1,3},{2,0},{3,1},{4,6},{5,7},{6,4},{7,5},{8,10},{9,11},{10,... | collective-permute-start | bytes 294920 | tf_op jit(solution)/shard_map/ppermute | solution.py:349
  62.4 41.9 %copy-start = (bf16[1024,1024]{1,0:T(8,128)(2,1)S(1)}, bf16[1024,1024]{1,0:T(8,128)(2,1)}, u32[]{:S(2)}) copy-start(bf16[1024,1024]{1,0:T(8,128)(2,1)} %interp.1) | copy-start | bytes 6291460

commit v10 on v9

--- a/solution.py
+++ b/solution.py
@@ -419,7 +419,6 @@
     first, _ = lax.optimization_barrier((first, last_two))
     (first_three,) = block_sum([first], right, tiles[3], (CUT, short))
     handed = swap(first_three, 1)
-    last, _ = lax.optimization_barrier((last, first_three))
     (last_three,) = block_sum([last], right, tiles[3], (OWN - CUT, short), at=CUT)
     arrived, firsts = [swap(last_three, 3)], [CUT]
     first_both = local(add_kernel, shape(first_two.shape, short), first_two, handed)

time: 107 us -> 107 us (level)
  no operation moved by 1% of the time
where the time goes in v10:
time: 107 us; the launch traced here: 106 us
  waiting for transfers between devices  36.1 us (34%)
  blocking collectives  33 us (31%)
  starting transfers between devices  19.7 us (18%)
  Pallas kernels  15.4 us (14%)
  other arithmetic  1.73 us (2%)
    all_to_all x1, blocking collectives, shards(): lax.all_to_all(picked.reshape(box_total, per_owner, NORB), ('row', 'col')...  33 us
    all_to_all x1, waiting for transfers between devices, shards(): lax.all_to_all(outgoing, ('row', 'col'), split_axis=0, concat_axis=0, til...  20.2 us
    ppermute x9, waiting for transfers between devices, swap(): return lax.ppermute(rows, 'col', [(i, i ^ mask) for i in range(col_count)])  10.3 us
    pallas_call x13, Pallas kernels, local(): pl.pallas_call(kernel, out_shape=out, in_specs=[spec(n, a) for n, a in en...  9.66 us
    all_to_all x1, starting transfers between devices, shards(): lax.all_to_all(outgoing, ('row', 'col'), split_axis=0, concat_axis=0, til...  7.1 us
    ppermute x9, starting transfers between devices, swap(): return lax.ppermute(rows, 'col', [(i, i ^ mask) for i in range(col_count)])  6.4 us
    ppermute x7, starting transfers between devices, flip(): return lax.ppermute(rows, 'row', [(i, i ^ mask) for i in range(row_count)])  6.16 us
    ppermute x7, waiting for transfers between devices, flip(): return lax.ppermute(rows, 'row', [(i, i ^ mask) for i in range(row_count)])  5.53 us
  transfers between devices with their start and end apart: 17, of which 10 were waited for; matrix products, arithmetic and copies ran while one was open for 2% of the time, Pallas kernels for 9%

profile of v10, /device:TPU:1, one launch (start us, length us, event | category | flops | bytes accessed | tf_op | source)
XLA Modules:
  0.0 106.3 jit_solution(16514304702776351458)
XLA Ops:
  0.0 3.3 %shard_map.73 = bf16[32,104,128]{2,1,0:T(8,128)(2,1)} custom-call(s32[32]{0:T(128)} %counts_hbm.1, s32[8,128]{1,0:T(8,128)} %bitcast.13, s32[64,128]{1,0:T(8,128)} %bitcast.10, s32[8,128]{1,0:T(8,128)} %bitcast.14, bf16[1024,512]{1,0:T(8,128)(2,1)} %orbitals_hbm.1), custom_call_target="tpu_custom_call" | custom-call | flops 805306368 | bytes 2097152 | tf_op jit(solution)/shard_map/pallas_call | solution.py:297
  3.3 7.1 %all-to-all-start = ((bf16[32,104,128]{2,1,0:T(8,128)(2,1)}), bf16[32,104,128]{2,1,0:T(8,128)(2,1)S(1)}, u32[]{:S(2)}, u32[]{:S(2)}) async-start(bf16[32,104,128]{2,1,0:T(8,128)(2,1)} %shard_map.73), calls=%async_computation | async-start | bytes 1703936 | tf_op jit(solution)/shard_map/all_to_all | solution.py:323
  10.7 1.2 %select_reduce_fusion = s32[256]{0:T(256)S(1)} fusion(s32[8192]{0:T(1024)S(1)} %copy-done.1, s32[256]{0:T(256)S(1)} %iota_add_fusion), kind=kLoop, calls=%fused_computation | loop fusion | flops 6291200 | bytes 34816 | tf_op jit(solution)/shard_map/reduce_sum | solution.py:329
  12.4 20.2 %all-to-all-done.received = bf16[32,104,128]{2,1,0:T(8,128)(2,1)S(1)} async-done(((bf16[32,104,128]{2,1,0:T(8,128)(2,1)}), bf16[32,104,128]{2,1,0:T(8,128)(2,1)S(1)}, u32[]{:S(2)}, u32[]{:S(2)}) %all-to-all-start) | async-done | bytes 852000 | tf_op jit(solution)/shard_map/all_to_all | solution.py:323
  33.0 1.3 %collective-permute-start = (bf16[256,512]{1,0:T(8,128)(2,1)S(1)}, bf16[256,512]{1,0:T(8,128)(2,1)S(1)}, u32[]{:S(2)}, u32[]{:S(2)}) collective-permute-start(bf16[256,512]{1,0:T(8,128)(2,1)S(1)} %get-tuple-element.23.refs_0_), channel_id=1, source_target_pairs={{0,8},{4,12},{8,0},{12,4},{16,24},{20,28},{24,16},{28,20},{1,9},{5... | collective-permute-start | bytes 786440 | tf_op jit(solution)/shard_map/ppermute | solution.py:356
  35.4 2.8 %shard_map.75 = (bf16[256,2048]{1,0:T(8,128)(2,1)S(1)}, bf16[256,2048]{1,0:T(8,128)(2,1)S(1)}, bf16[256,2048]{1,0:T(8,128)(2,1)S(1)}, bf16[256,2048]{1,0:T(8,128)(2,1)S(1)}) custom-call(s32[4]{0:T(128)S(1)} %iota_xor_fusion.scalars, bf16[1024,2048]{1,0:T(8,128)(2,1)} %coulomb.1), custom_call_target="tpu_custom_call" | custom-call | tf_op jit(solution)/shard_map/pallas_call | solution.py:238
  38.2 2.7 %collective-permute-done.refs_0_ = bf16[256,512]{1,0:T(8,128)(2,1)S(1)} collective-permute-done((bf16[256,512]{1,0:T(8,128)(2,1)S(1)}, bf16[256,512]{1,0:T(8,128)(2,1)S(1)}, u32[]{:S(2)}, u32[]{:S(2)}) %collective-permute-start) | collective-permute-done | bytes 262176 | tf_op jit(solution)/shard_map/ppermute | solution.py:356
  40.9 1.3 %collective-permute-start.2 = (bf16[128,512]{1,0:T(8,128)(2,1)S(1)}, bf16[128,512]{1,0:T(8,128)(2,1)S(1)}, u32[]{:S(2)}, u32[]{:S(2)}) collective-permute-start(bf16[128,512]{1,0:T(8,128)(2,1)S(1)} %slice.12), channel_id=1, source_target_pairs={{0,16},{4,20},{8,24},{12,28},{16,0},{20,4},{24,8},{28,12},{1,17},{... | collective-permute-start | bytes 393224 | tf_op jit(solution)/shard_map/ppermute | solution.py:356
  42.7 1.3 %collective-permute-start.4 = (bf16[256,512]{1,0:T(8,128)(2,1)S(1)}, bf16[256,512]{1,0:T(8,128)(2,1)S(1)}, u32[]{:S(2)}, u32[]{:S(2)}) collective-permute-start(bf16[256,512]{1,0:T(8,128)(2,1)S(1)} %get-tuple-element.23.refs_0_), channel_id=1, source_target_pairs={{0,4},{4,0},{8,12},{12,8},{16,20},{20,16},{24,28},{28,24},{1,5},{5... | collective-permute-start | bytes 786440 | tf_op jit(solution)/shard_map/ppermute | solution.py:356
  44.0 2.1 %collective-permute-done.2.refs_0_ = bf16[128,512]{1,0:T(8,128)(2,1)S(1)} collective-permute-done((bf16[128,512]{1,0:T(8,128)(2,1)S(1)}, bf16[128,512]{1,0:T(8,128)(2,1)S(1)}, u32[]{:S(2)}, u32[]{:S(2)}) %collective-permute-start.2) | collective-permute-done | bytes 131104 | tf_op jit(solution)/shard_map/ppermute | solution.py:356
  47.4 1.0 collective-permute-start.6
  48.6 1.5 %collective-permute-start.10 = (bf16[160,512]{1,0:T(8,128)(2,1)S(1)}, bf16[160,512]{1,0:T(8,128)(2,1)S(1)}, u32[]{:S(2)}, u32[]{:S(2)}) collective-permute-start(bf16[160,512]{1,0:T(8,128)(2,1)S(1)} %slice.14), channel_id=1, source_target_pairs={{0,1},{1,0},{2,3},{3,2},{4,5},{5,4},{6,7},{7,6},{8,9},{9,8},{10,11... | collective-permute-start | bytes 491528 | tf_op jit(solution)/shard_map/ppermute | solution.py:349
  50.3 1.3 %shard_map.81 = (f32[96,512]{1,0:T(8,128)S(1)}, bf16[160,512]{1,0:T(8,128)(2,1)S(1)}) custom-call(bf16[256,512]{1,0:T(8,128)(2,1)S(1)} %get-tuple-element.30.refs_0_, bf16[2048,512]{1,0:T(8,128)(2,1)S(1)} %shard_map.79.refs_1_, bf16[256,2048]{1,0:T(8,128)(2,1)S(1)} %get-tuple-element.31.refs_2_), custom_call_target="tpu_custom_call" | custom-call | tf_op jit(solution)/shard_map/pallas_call | solution.py:238
  52.1 1.1 %shard_map.84 = bf16[96,512]{1,0:T(8,128)(2,1)S(1)} custom-call(bf16[96,512]{1,0:T(8,128)(2,1)S(1)} %collective-permute-done.12.refs_0_, bf16[2048,512]{1,0:T(8,128)(2,1)S(1)} %shard_map.79.refs_1_, bf16[256,2048]{1,0:T(8,128)(2,1)S(1)} %get-tuple-element.33.refs_2_), custom_call_target="tpu_custom_call" | custom-call | tf_op jit(solution)/shard_map/pallas_call | solution.py:238
  54.4 1.2 %shard_map.83 = bf16[160,512]{1,0:T(8,128)(2,1)S(1)} custom-call(bf16[160,512]{1,0:T(8,128)(2,1)S(1)} %collective-permute-done.10.refs_0_, bf16[2048,512]{1,0:T(8,128)(2,1)S(1)} %shard_map.79.refs_1_, bf16[256,2048]{1,0:T(8,128)(2,1)S(1)} %get-tuple-element.33.refs_2_), custom_call_target="tpu_custom_call" | custom-call | tf_op jit(solution)/shard_map/pallas_call | solution.py:238
  55.6 2.0 %collective-permute-start.11 = (bf16[160,512]{1,0:T(8,128)(2,1)S(1)}, bf16[160,512]{1,0:T(8,128)(2,1)S(1)}, u32[]{:S(2)}, u32[]{:S(2)}) collective-permute-start(bf16[160,512]{1,0:T(8,128)(2,1)S(1)} %shard_map.83), channel_id=1, source_target_pairs={{0,3},{1,2},{2,1},{3,0},{4,7},{5,6},{6,5},{7,4},{8,11},{9,10},{10,... | collective-permute-start | bytes 491528 | tf_op jit(solution)/shard_map/ppermute | solution.py:349
  57.7 1.3 %shard_map.86 = bf16[256,512]{1,0:T(8,128)(2,1)S(1)} custom-call(bf16[256,512]{1,0:T(8,128)(2,1)S(1)} %get-tuple-element.37.refs_0_, bf16[2048,512]{1,0:T(8,128)(2,1)S(1)} %shard_map.79.refs_1_, bf16[256,2048]{1,0:T(8,128)(2,1)S(1)} %get-tuple-element.38.refs_2_), custom_call_target="tpu_custom_call" | custom-call | tf_op jit(solution)/shard_map/pallas_call | solution.py:238
  59.0 1.1 %collective-permute-done.13.other = bf16[96,512]{1,0:T(8,128)(2,1)S(1)} collective-permute-done((bf16[96,512]{1,0:T(8,128)(2,1)S(1)}, bf16[96,512]{1,0:T(8,128)(2,1)S(1)}, u32[]{:S(2)}, u32[]{:S(2)}) %collective-permute-start.13) | collective-permute-done | bytes 98336 | tf_op jit(solution)/shard_map/ppermute | solution.py:349
  60.2 0.9 collective-permute-start.14
  61.1 1.3 %shard_map.82.own = f32[256,512]{1,0:T(8,128)S(1)} custom-call(bf16[256,512]{1,0:T(8,128)(2,1)S(1)} %get-tuple-element.23.refs_0_, bf16[2048,512]{1,0:T(8,128)(2,1)S(1)} %shard_map.79.refs_1_, bf16[256,2048]{1,0:T(8,128)(2,1)S(1)} %get-tuple-element.29.refs_2_, bf16[160,512]{1,0:T(8,128)(2,1)S(1)} %collective-permute-done.9.refs_3_), custom_call_target="tpu_custom_call" | custom-call | flops 10000000000 | tf_op jit(solution)/shard_map/pallas_call | solution.py:238
  62.4 1.6 %collective-permute-done.11.refs_0_ = bf16[160,512]{1,0:T(8,128)(2,1)S(1)} collective-permute-done((bf16[160,512]{1,0:T(8,128)(2,1)S(1)}, bf16[160,512]{1,0:T(8,128)(2,1)S(1)}, u32[]{:S(2)}, u32[]{:S(2)}) %collective-permute-start.11) | collective-permute-done | bytes 163872 | tf_op jit(solution)/shard_map/ppermute | solution.py:349
  64.0 6.8 %collective-permute-done.14.refs_1_ = bf16[96,512]{1,0:T(8,128)(2,1)S(1)} collective-permute-done((bf16[96,512]{1,0:T(8,128)(2,1)S(1)}, bf16[96,512]{1,0:T(8,128)(2,1)S(1)}, u32[]{:S(2)}, u32[]{:S(2)}) %collective-permute-start.14) | collective-permute-done | bytes 98336 | tf_op jit(solution)/shard_map/ppermute | solution.py:349
  71.3 33.0 %all_to_all.10 = bf16[32,32,512]{2,1,0:T(8,128)(2,1)S(1)} all-to-all(bf16[32,32,512]{2,1,0:T(8,128)(2,1)S(1)} %bitcast.9), channel_id=1, replica_groups=mesh['row'=8,'col'=4] {'row','col'}, dimensions={0} | all-to-all | bytes 2097152 | tf_op jit(solution)/shard_map/all_to_all | solution.py:439
  104.3 2.1 %shard_map.88 = f32[1024,512]{1,0:T(8,128)} custom-call(bf16[1024,1024]{1,0:T(8,128)(2,1)S(1)} %copy-done, bf16[1024,512]{1,0:T(8,128)(2,1)S(1)} %bitcast.8), custom_call_target="tpu_custom_call" | custom-call | tf_op jit(solution)/shard_map/pallas_call | solution.py:447
  (47 shorter events, 6.8 us)
Async XLA Ops:
  0.0 10.4 %copy-start.2 = (s32[32]{0:T(128)S(1)}, s32[32]{0:T(128)}, u32[]{:S(2)}) copy-start(s32[32]{0:T(128)} %counts_hbm.1) | copy-start | bytes 388
  0.0 10.7 %copy-start.1 = (s32[8192]{0:T(1024)S(1)}, s32[8192]{0:T(1024)}, u32[]{:S(2)}) copy-start(s32[8192]{0:T(1024)} %param.11) | copy-start | bytes 98308
  3.3 29.3 %all-to-all-start = ((bf16[32,104,128]{2,1,0:T(8,128)(2,1)}), bf16[32,104,128]{2,1,0:T(8,128)(2,1)S(1)}, u32[]{:S(2)}, u32[]{:S(2)}) async-start(bf16[32,104,128]{2,1,0:T(8,128)(2,1)} %shard_map.73), calls=%async_computation | async-start | bytes 1703936 | tf_op jit(solution)/shard_map/all_to_all | solution.py:323
  33.0 7.9 %collective-permute-start = (bf16[256,512]{1,0:T(8,128)(2,1)S(1)}, bf16[256,512]{1,0:T(8,128)(2,1)S(1)}, u32[]{:S(2)}, u32[]{:S(2)}) collective-permute-start(bf16[256,512]{1,0:T(8,128)(2,1)S(1)} %get-tuple-element.23.refs_0_), channel_id=1, source_target_pairs={{0,8},{4,12},{8,0},{12,4},{16,24},{20,28},{24,16},{28,20},{1,9},{5... | collective-permute-start | bytes 786440 | tf_op jit(solution)/shard_map/ppermute | solution.py:356
  34.3 8.1 %collective-permute-start.1 = (bf16[256,512]{1,0:T(8,128)(2,1)S(1)}, bf16[256,512]{1,0:T(8,128)(2,1)S(1)}, u32[]{:S(2)}, u32[]{:S(2)}) collective-permute-start(bf16[256,512]{1,0:T(8,128)(2,1)S(1)} %get-tuple-element.23.refs_0_), channel_id=1, source_target_pairs={{0,16},{4,20},{8,24},{12,28},{16,0},{20,4},{24,8},{28,12},{1,17},{... | collective-permute-start | bytes 786440 | tf_op jit(solution)/shard_map/ppermute | solution.py:356
  34.6 13.9 %collective-permute-start.7 = (bf16[256,512]{1,0:T(8,128)(2,1)S(1)}, bf16[256,512]{1,0:T(8,128)(2,1)S(1)}, u32[]{:S(2)}, u32[]{:S(2)}) collective-permute-start(bf16[256,512]{1,0:T(8,128)(2,1)S(1)} %get-tuple-element.23.refs_0_), channel_id=1, source_target_pairs={{0,1},{1,0},{2,3},{3,2},{4,5},{5,4},{6,7},{7,6},{8,9},{9,8},{10,11... | collective-permute-start | bytes 786440 | tf_op jit(solution)/shard_map/ppermute | solution.py:349
  35.2 13.3 %collective-permute-start.8 = (bf16[256,512]{1,0:T(8,128)(2,1)S(1)}, bf16[256,512]{1,0:T(8,128)(2,1)S(1)}, u32[]{:S(2)}, u32[]{:S(2)}) collective-permute-start(bf16[256,512]{1,0:T(8,128)(2,1)S(1)} %get-tuple-element.23.refs_0_), channel_id=1, source_target_pairs={{0,2},{1,3},{2,0},{3,1},{4,6},{5,7},{6,4},{7,5},{8,10},{9,11},{10,... | collective-permute-start | bytes 786440 | tf_op jit(solution)/shard_map/ppermute | solution.py:349
  40.9 5.3 %collective-permute-start.2 = (bf16[128,512]{1,0:T(8,128)(2,1)S(1)}, bf16[128,512]{1,0:T(8,128)(2,1)S(1)}, u32[]{:S(2)}, u32[]{:S(2)}) collective-permute-start(bf16[128,512]{1,0:T(8,128)(2,1)S(1)} %slice.12), channel_id=1, source_target_pairs={{0,16},{4,20},{8,24},{12,28},{16,0},{20,4},{24,8},{28,12},{1,17},{... | collective-permute-start | bytes 393224 | tf_op jit(solution)/shard_map/ppermute | solution.py:356
  42.4 5.0 %collective-permute-start.3 = (bf16[128,512]{1,0:T(8,128)(2,1)S(1)}, bf16[128,512]{1,0:T(8,128)(2,1)S(1)}, u32[]{:S(2)}, u32[]{:S(2)}) collective-permute-start(bf16[128,512]{1,0:T(8,128)(2,1)S(1)} %slice.16), channel_id=1, source_target_pairs={{0,8},{4,12},{8,0},{12,4},{16,24},{20,28},{24,16},{28,20},{1,9},{5... | collective-permute-start | bytes 393224 | tf_op jit(solution)/shard_map/ppermute | solution.py:356
  42.7 7.4 %collective-permute-start.4 = (bf16[256,512]{1,0:T(8,128)(2,1)S(1)}, bf16[256,512]{1,0:T(8,128)(2,1)S(1)}, u32[]{:S(2)}, u32[]{:S(2)}) collective-permute-start(bf16[256,512]{1,0:T(8,128)(2,1)S(1)} %get-tuple-element.23.refs_0_), channel_id=1, source_target_pairs={{0,4},{4,0},{8,12},{12,8},{16,20},{20,16},{24,28},{28,24},{1,5},{5... | collective-permute-start | bytes 786440 | tf_op jit(solution)/shard_map/ppermute | solution.py:356
  46.2 4.0 %collective-permute-start.5 = (bf16[512,512]{1,0:T(8,128)(2,1)S(1)}, bf16[512,512]{1,0:T(8,128)(2,1)S(1)}, u32[]{:S(2)}, u32[]{:S(2)}) collective-permute-start(bf16[512,512]{1,0:T(8,128)(2,1)S(1)} %shard_map.76.refs_1_), channel_id=1, source_target_pairs={{0,4},{4,0},{8,12},{12,8},{16,20},{20,16},{24,28},{28,24},{1,5},{5... | collective-permute-start | bytes 1572872 | tf_op jit(solution)/shard_map/ppermute | solution.py:356
  47.4 2.7 %collective-permute-start.6 = (bf16[256,512]{1,0:T(8,128)(2,1)S(1)}, bf16[256,512]{1,0:T(8,128)(2,1)S(1)}, u32[]{:S(2)}, u32[]{:S(2)}) collective-permute-start(bf16[256,512]{1,0:T(8,128)(2,1)S(1)} %shard_map.78.refs_2_), channel_id=1, source_target_pairs={{0,4},{4,0},{8,12},{12,8},{16,20},{20,16},{24,28},{28,24},{1,5},{5... | collective-permute-start | bytes 786440 | tf_op jit(solution)/shard_map/ppermute | solution.py:356
  48.5 3.5 %collective-permute-start.12 = (bf16[96,512]{1,0:T(8,128)(2,1)S(1)}, bf16[96,512]{1,0:T(8,128)(2,1)S(1)}, u32[]{:S(2)}, u32[]{:S(2)}) collective-permute-start(bf16[96,512]{1,0:T(8,128)(2,1)S(1)} %slice.15), channel_id=1, source_target_pairs={{0,1},{1,0},{2,3},{3,2},{4,5},{5,4},{6,7},{7,6},{8,9},{9,8},{10,11... | collective-permute-start | bytes 294920 | tf_op jit(solution)/shard_map/ppermute | solution.py:349
  48.6 5.8 %collective-permute-start.10 = (bf16[160,512]{1,0:T(8,128)(2,1)S(1)}, bf16[160,512]{1,0:T(8,128)(2,1)S(1)}, u32[]{:S(2)}, u32[]{:S(2)}) collective-permute-start(bf16[160,512]{1,0:T(8,128)(2,1)S(1)} %slice.14), channel_id=1, source_target_pairs={{0,1},{1,0},{2,3},{3,2},{4,5},{5,4},{6,7},{7,6},{8,9},{9,8},{10,11... | collective-permute-start | bytes 491528 | tf_op jit(solution)/shard_map/ppermute | solution.py:349
  51.6 9.5 %collective-permute-start.9 = (bf16[160,512]{1,0:T(8,128)(2,1)S(1)}, bf16[160,512]{1,0:T(8,128)(2,1)S(1)}, u32[]{:S(2)}, u32[]{:S(2)}) collective-permute-start(bf16[160,512]{1,0:T(8,128)(2,1)S(1)} %get-tuple-element.32), channel_id=1, source_target_pairs={{0,2},{1,3},{2,0},{3,1},{4,6},{5,7},{6,4},{7,5},{8,10},{9,11},{10,... | collective-permute-start | bytes 491528 | tf_op jit(solution)/shard_map/ppermute | solution.py:349
  53.2 7.0 %collective-permute-start.13 = (bf16[96,512]{1,0:T(8,128)(2,1)S(1)}, bf16[96,512]{1,0:T(8,128)(2,1)S(1)}, u32[]{:S(2)}, u32[]{:S(2)}) collective-permute-start(bf16[96,512]{1,0:T(8,128)(2,1)S(1)} %shard_map.84), channel_id=1, source_target_pairs={{0,1},{1,0},{2,3},{3,2},{4,5},{5,4},{6,7},{7,6},{8,9},{9,8},{10,11... | collective-permute-start | bytes 294920 | tf_op jit(solution)/shard_map/ppermute | solution.py:349
  55.6 8.3 %collective-permute-start.11 = (bf16[160,512]{1,0:T(8,128)(2,1)S(1)}, bf16[160,512]{1,0:T(8,128)(2,1)S(1)}, u32[]{:S(2)}, u32[]{:S(2)}) collective-permute-start(bf16[160,512]{1,0:T(8,128)(2,1)S(1)} %shard_map.83), channel_id=1, source_target_pairs={{0,3},{1,2},{2,1},{3,0},{4,7},{5,6},{6,5},{7,4},{8,11},{9,10},{10,... | collective-permute-start | bytes 491528 | tf_op jit(solution)/shard_map/ppermute | solution.py:349
  58.9 11.8 %collective-permute-start.15 = (bf16[256,512]{1,0:T(8,128)(2,1)S(1)}, bf16[256,512]{1,0:T(8,128)(2,1)S(1)}, u32[]{:S(2)}, u32[]{:S(2)}) collective-permute-start(bf16[256,512]{1,0:T(8,128)(2,1)S(1)} %shard_map.86), channel_id=1, source_target_pairs={{0,1},{1,0},{2,3},{3,2},{4,5},{5,4},{6,7},{7,6},{8,9},{9,8},{10,11... | collective-permute-start | bytes 786440 | tf_op jit(solution)/shard_map/ppermute | solution.py:349
  60.2 10.6 %collective-permute-start.14 = (bf16[96,512]{1,0:T(8,128)(2,1)S(1)}, bf16[96,512]{1,0:T(8,128)(2,1)S(1)}, u32[]{:S(2)}, u32[]{:S(2)}) collective-permute-start(bf16[96,512]{1,0:T(8,128)(2,1)S(1)} %shard_map.85), channel_id=1, source_target_pairs={{0,2},{1,3},{2,0},{3,1},{4,6},{5,7},{6,4},{7,5},{8,10},{9,11},{10,... | collective-permute-start | bytes 294920 | tf_op jit(solution)/shard_map/ppermute | solution.py:349
  62.4 41.9 %copy-start = (bf16[1024,1024]{1,0:T(8,128)(2,1)S(1)}, bf16[1024,1024]{1,0:T(8,128)(2,1)}, u32[]{:S(2)}) copy-start(bf16[1024,1024]{1,0:T(8,128)(2,1)} %interp.1) | copy-start | bytes 6291460
